TPU v7x, 32 devices: a whole 2x2x4 slice. The times are simulated.
32 devices in a mesh: lon: 8 (over z, y), lat: 4 (over x, core).
Axes of the slice: x: 2, y: 2, z: 4, core: 2. Of those that a mesh axis runs over, the one named last changes fastest.
Arguments:
- spectra: float32 [25, 36, 32768], P(None, None, ('lon', 'lat')), may hold values from 0 to 1
- wind_growth: float32 [32768], P(('lon', 'lat')), may hold values from 0.05 to 0.6
- wind_dir: float32 [32768], P(('lon', 'lat')), may hold values from -3.140625 to 3.140625
- point_cell: int32 [32768], P(('lon', 'lat')), may hold values from -1 to 32767, as said below
- land_mask: int32 [16, 2048], P('lon', 'lat'), may hold values from 0 to 1, as said below
- shoaling: float32 [16, 2048], P('lon', 'lat'), may hold values from 0.5 to 1
- slope_x: float32 [16, 2048], P('lon', 'lat'), may hold values from -0.5 to 0.5
- slope_y: float32 [16, 2048], P('lon', 'lat'), may hold values from -0.5 to 0.5
Outputs:
- wave_field: float32 [25, 36, 16, 2048], P(None, None, 'lon', 'lat')
Inputs may be any that keep to these rules, and one draw needn't show every extreme that they name: `point_cell`: every sea cell of land_mask is named by exactly one slot over all devices, land cells by none, other slots hold -1. The slots of one device name at most 32 cells of any one device's block of 2 x 512 cells, and in every draw some block gets exactly 32 from every device. `land_mask`: at least a quarter of the cells of each device's block are sea; some block is all sea.
All inputs are finite; a program needn't handle non-finite values.
Results may differ from a plain program's by a relative error of at most 0.0001.
Values sent between devices are 32-bit elements; how exact they have to be, the bound alone decides.
No kernel may reach another device: no remote copies, remote signals or barrier semaphores. Data moves between devices by JAX's collectives and lax.ppermute only.
A program may use at most 128 MiB of HBM per device.

v0:
```python
import math

import jax
import jax.numpy as jnp
from jax import lax
from jax.sharding import PartitionSpec as P

NSUB = 2


def with_halo(cells, sides, width):
    for axis, dim in sides:
        count = lax.axis_size(axis)
        head = lax.slice_in_dim(cells, 0, width, axis=dim)
        tail = lax.slice_in_dim(cells, cells.shape[dim] - width, cells.shape[dim], axis=dim)
        cells = jnp.concatenate(
            [
                lax.ppermute(tail, axis, [(i, (i + 1) % count) for i in range(count)]),
                cells,
                lax.ppermute(head, axis, [((i + 1) % count, i) for i in range(count)]),
            ],
            axis=dim,
        )
    return cells


def spectral_tables(nfreq, ndir):
    level = jnp.arange(nfreq, dtype=jnp.float32)
    ratio = 1.1 ** (level - (nfreq - 1))
    speed = 0.65 * 1.1 ** (-level)
    width = 0.1 * 1.1**level
    theta = (jnp.arange(ndir, dtype=jnp.float32) + 0.5) * (2.0 * math.pi / ndir)
    return (ratio, speed, width, theta)


def route_rows(values, target, slots):
    picker = (target[:, None] == jnp.arange(slots, dtype=jnp.int32)[None, :]).astype(jnp.float32)
    return (
        jnp.dot(
            values, picker, precision=lax.Precision.HIGHEST, preferred_element_type=jnp.float32
        ),
        picker,
    )


def on_device(spectra, wind_growth, wind_dir, point_cell, land_mask, shoaling, slope_x, slope_y):
    nfreq, ndir, slots = spectra.shape
    rows_x, rows_y = land_mask.shape
    lon_count = lax.axis_size("lon")
    lat_count = lax.axis_size("lat")
    devices = lon_count * lat_count
    capacity = slots // devices
    ratio, speed, width, theta = spectral_tables(nfreq, ndir)
    dtheta = 2.0 * math.pi / ndir
    energy = jnp.sum((width * dtheta)[:, None] * jnp.sum(spectra, axis=1), axis=0)
    load = energy / (energy + 10.0)
    lobe = jnp.maximum(jnp.cos(theta[:, None] - wind_dir[None, :]), 0.0) ** 2
    rate = (
        wind_growth[None, None, :] * lobe[None] * ratio[:, None, None]
        - 0.4 * ratio[:, None, None] * load[None, None, :]
    )
    sourced = spectra * jnp.exp(rate)
    valid = point_cell >= 0
    cell = jnp.maximum(point_cell, 0)
    total_y = rows_y * lat_count
    col_x = cell // total_y
    col_y = cell % total_y
    owner = col_x // rows_x * lat_count + col_y // rows_y
    local = col_x % rows_x * rows_y + col_y % rows_y
    owner = jnp.where(valid, owner, devices)
    onehot = (owner[:, None] == jnp.arange(devices, dtype=jnp.int32)[None, :]).astype(jnp.int32)
    before = jnp.cumsum(onehot, axis=0) - onehot
    place = jnp.sum(before * onehot, axis=1)
    target = jnp.where(valid, owner * capacity + place, slots)
    outgoing, picker = route_rows(sourced.reshape(nfreq * ndir, slots), target, slots)
    outgoing = outgoing.reshape(nfreq, ndir, slots)
    filled = jnp.sum(picker, axis=0)
    labels = jnp.dot(
        local.astype(jnp.float32)[None, :],
        picker,
        precision=lax.Precision.HIGHEST,
        preferred_element_type=jnp.float32,
    )[0] - (1.0 - filled)
    rows_in, ids_in = (
        lax.all_to_all(outgoing, ("lon", "lat"), split_axis=2, concat_axis=2, tiled=True),
        lax.all_to_all(
            labels.reshape(1, 1, slots), ("lon", "lat"), split_axis=2, concat_axis=2, tiled=True
        ),
    )
    ids_in = ids_in.reshape(slots)
    placed = ids_in.astype(jnp.int32)
    placed = jnp.where(placed >= 0, placed, slots)
    field, unused = route_rows(rows_in.reshape(nfreq * ndir, slots), placed, slots)
    field = field.reshape(nfreq, ndir, rows_x, rows_y)
    sea = land_mask.astype(jnp.float32)
    cos_t = jnp.cos(theta)
    sin_t = jnp.sin(theta)
    speed4 = speed[:, None, None, None]
    cos4 = cos_t[None, :, None, None]
    sin4 = sin_t[None, :, None, None]
    shoal_pad = with_halo(shoaling, (("lon", 0), ("lat", 1)), 1)
    cx_pad = speed4 * shoal_pad[None, None] * cos4
    cy_pad = speed4 * shoal_pad[None, None] * sin4
    turn = speed4 * (sin4 * slope_x[None, None] - cos4 * slope_y[None, None])
    lat_id = lax.axis_index("lat")
    low_keep = (lat_id > 0).astype(jnp.float32)
    high_keep = (lat_id < lat_count - 1).astype(jnp.float32)
    edge = jnp.concatenate([low_keep[None], jnp.ones((rows_y,), jnp.float32), high_keep[None]])
    for step in range(NSUB):
        padded = with_halo(field, (("lon", 2), ("lat", 3)), 1) * edge
        qx = cx_pad * padded
        qy = cy_pad * padded
        flux_x = jnp.maximum(qx[:, :, :-1, 1:-1], 0.0) + jnp.minimum(qx[:, :, 1:, 1:-1], 0.0)
        flux_y = jnp.maximum(qy[:, :, 1:-1, :-1], 0.0) + jnp.minimum(qy[:, :, 1:-1, 1:], 0.0)
        half = (
            field
            - (flux_x[:, :, 1:] - flux_x[:, :, :-1])
            - (flux_y[:, :, :, 1:] - flux_y[:, :, :, :-1])
        )
        qt = turn * half
        flux_t = jnp.maximum(qt, 0.0) + jnp.minimum(jnp.roll(qt, -1, axis=1), 0.0)
        field = (half - flux_t + jnp.roll(flux_t, 1, axis=1)) * sea
    return field


def solution(mesh):
    placed = (
        P(None, None, ("lon", "lat")),
        P(("lon", "lat")),
        P(("lon", "lat")),
        P(("lon", "lat")),
        P("lon", "lat"),
        P("lon", "lat"),
        P("lon", "lat"),
        P("lon", "lat"),
    )
    return jax.shard_map(
        on_device,
        mesh=mesh,
        in_specs=placed,
        out_specs=P(None, None, "lon", "lat"),
        check_vma=False,
    )
```

profile of v0, /device:TPU:0, one launch (start us, length us, event | category | flops | bytes accessed | tf_op | source)
XLA Modules:
  0.0 546.2 jit_solution(16184169512481730743)
XLA Ops:
  0.7 9.0 %reduce-window.6 = s32[32,8,128]{2,1,0:T(8,128)S(1)} reduce-window(s32[32,8,128]{2,1,0:T(8,128)S(1)} %fusion.34, s32[]{:T(128)} %constant.101.clone.1), window={size=1x1x128 pad=0_0x0_0x127_0}, to_apply=%region_2.3 | reduce-window | flops 4161536 | bytes 262148 | tf_op jit(solution)/shard_map/reduce-window
  14.0 7.3 %all-to-all-start.1 = ((f32[1,1,1024]{1,0,2:T(1,128)}), f32[1,1,1024]{1,0,2:T(1,128)S(1)}, u32[]{:S(2)}, u32[]{:S(2)}) async-start(f32[1,1,1024]{1,0,2:T(1,128)} %copy.59), calls=%async_computation.1 | async-start | bytes 1048576 | tf_op jit(solution)/shard_map/all_to_all | solution.py:86
  25.0 11.3 %fusion.8 = f32[25,36,1024]{2,1,0:T(8,128)} fusion(f32[25,36,1024]{2,1,0:T(8,128)} %param.8, s32[1024]{0:T(1024)S(1)} %add_select_fusion.6, f32[25,1024]{1,0:T(8,128)S(1)} %broadcast_multiply_fusion.1, f32[25]{0:T(128)S(1)} %add_power_fusion, f32[36,1024]{1,0:T(8,128)S(1)} %multiply_multiply_fusion.6), kind=kOutput, calls=%fused_computation.26 | convolution fusion | flops 11328434176 | bytes 7626852 | tf_op jit(solution)/shard_map/dot_general | solution.py:39
  36.3 14.6 %copy.58 = f32[25,36,1024]{1,0,2:T(8,128)} copy(f32[25,36,1024]{2,1,0:T(8,128)} %fusion.8) | data formatting | bytes 7372800 | tf_op jit(solution)/shard_map/dot_general | solution.py:39
  50.9 15.4 %reshape.196 = f32[32,1,28800]{2,1,0:T(1,128)} reshape(f32[1024,25,36]{2,1,0:T(8,128)} %bitcast.38) | data formatting | bytes 7372800
  66.3 6.2 %all-to-all-start = ((f32[32,1,28800]{2,1,0:T(1,128)}), f32[32,1,28800]{2,1,0:T(1,128)}, u32[]{:S(2)}, u32[]{:S(2)}) async-start(f32[32,1,28800]{2,1,0:T(1,128)} %reshape.196), calls=%async_computation | async-start | bytes 7372800 | tf_op jit(solution)/shard_map/all_to_all | solution.py:85
  72.5 18.5 %convert_reduce_fusion.1 = s32[1024]{0:T(1024)S(1)} fusion(f32[1,1,1024]{1,0,2:T(1,128)S(1)} %all-to-all-done.1), kind=kLoop, calls=%fused_computation.62 | loop fusion | flops 1024 | bytes 8192 | tf_op jit(solution)/shard_map/convert_element_type | solution.py:91
  91.0 64.2 %all-to-all-done = f32[32,1,28800]{2,1,0:T(1,128)} async-done(((f32[32,1,28800]{2,1,0:T(1,128)}), f32[32,1,28800]{2,1,0:T(1,128)}, u32[]{:S(2)}, u32[]{:S(2)}) %all-to-all-start) | async-done | bytes 3686432 | tf_op jit(solution)/shard_map/all_to_all | solution.py:85
  155.8 40.0 %reduce.2 = f32[32,28800]{1,0:T(8,128)} reduce(f32[32,1,28800]{2,1,0:T(1,128)} %all-to-all-done, f32[]{:T(128)} %broadcast.282), dimensions={1}, to_apply=%all_to_all.6.reduce_sub_computation | reduce | bytes 7372804 | tf_op jit(solution)/shard_map/all_to_all | solution.py:85
  195.8 10.1 %reshape.197 = f32[1024,25,36]{2,1,0:T(8,128)} reshape(f32[32,28800]{1,0:T(8,128)} %reduce.2) | data formatting | bytes 7372800
  206.0 11.6 %bitcast_bitcast_fusion.1 = f32[25,36,1024,1]{1,0,2,3:T(8,128)} fusion(f32[1024,25,36]{2,1,0:T(8,128)} %reshape.197), kind=kLoop, calls=%fused_computation.124 | loop fusion | bytes 7372800 | tf_op jit(solution)/shard_map/all_to_all | solution.py:85
  217.5 52.4 %fusion = f32[25,36,2,512]{3,1,2,0:T(8,128)S(1)} fusion(f32[25,36,1024,1]{1,0,2,3:T(8,128)} %bitcast_bitcast_fusion.1, s32[2,512]{1,0:T(2,128)S(1)} %multiply_add_fusion, s32[1024]{0:T(1024)S(1)} %compare_select_fusion), kind=kOutput, calls=%fused_computation.4 | convolution fusion | flops 11325669376 | bytes 7380992 | tf_op jit(solution)/shard_map/dot_general | solution.py:39
  284.8 70.0 %collective-permute-done = f32[1,512]{1,0:T(1,128)S(1)} collective-permute-done((f32[1,512]{1,0:T(1,128)S(1)}, f32[1,512]{1,0:T(1,128)S(1)}, u32[]{:S(2)}, u32[]{:S(2)}) %collective-permute-start) | collective-permute-done | bytes 2080 | tf_op jit(solution)/shard_map/ppermute | solution.py:18
  371.3 3.9 collective-permute-done.6
  379.5 11.7 %multiply_multiply_fusion.3 = (f32[25,36,4,514]{3,1,2,0:T(8,128)S(1)}, f32[25,36,4,514]{3,1,2,0:T(8,128)}) fusion(f32[36]{0:T(128)S(1)} %get-tuple-element.28, f32[25,4,514]{2,1,0:T(4,128)S(1)} %broadcast_multiply_fusion, f32[514]{0:T(1024)S(1)} %pad_maximum_fusion.7, f32[25,36,4,1]{3,1,2,0:T(8,128)} %copy.68, f32[25,36,1,512]{3,1,2,0:T(8,128)S(1)} %copy.64, ...), kind=kLoop, calls=%fused_computation.3 | loop fusion | flops 16653600 | bytes 22412744 | tf_op jit(solution)/shard_map/mul | solution.py:111
  391.2 5.8 %fusion.3 = f32[25,36,3,512]{3,1,2,0:T(8,128)} fusion(f32[25,36,4,514]{3,1,2,0:T(8,128)S(1)} %get-tuple-element.11), kind=kLoop, calls=%fused_computation.12 | loop fusion | flops 4147200 | bytes 16588800 | tf_op jit(solution)/shard_map/add | solution.py:113
  397.0 5.5 %fusion.5 = f32[25,36,2,513]{3,1,2,0:T(8,128)S(1)} fusion(f32[25,36,4,514]{3,1,2,0:T(8,128)} %get-tuple-element.12), kind=kLoop, calls=%fused_computation.20 | loop fusion | flops 2770200 | bytes 11080800 | tf_op jit(solution)/shard_map/add | solution.py:114
  412.9 4.9 collective-permute-start.9
  419.7 74.2 %collective-permute-done.9 = f32[25,36,1,512]{3,2,1,0:T(1,128)S(1)} collective-permute-done((f32[25,36,1,512]{3,2,1,0:T(1,128)S(1)}, f32[25,36,1,512]{3,2,1,0:T(1,128)S(1)}, u32[]{:S(2)}, u32[]{:S(2)}) %collective-permute-start.9) | collective-permute-done | bytes 1843232 | tf_op jit(solution)/shard_map/ppermute | solution.py:20
  508.1 11.5 %multiply_multiply_fusion.2 = (f32[25,36,4,514]{3,1,2,0:T(8,128)S(1)}, f32[25,36,4,514]{3,1,2,0:T(8,128)}) fusion(f32[36]{0:T(128)S(1)} %get-tuple-element.28, f32[25,4,514]{2,1,0:T(4,128)S(1)} %copy-done.9, f32[514]{0:T(1024)S(1)} %pad_maximum_fusion.7, f32[25,36,4,1]{3,1,2,0:T(8,128)} %copy.76, f32[25,36,1,512]{3,1,2,0:T(8,128)S(1)} %copy.72, ...), kind=kLoop, calls=%fused_computation.2 | loop fusion | flops 16653600 | bytes 22412744 | tf_op jit(solution)/shard_map/mul | solution.py:111
  519.6 5.8 %fusion.2 = f32[25,36,3,512]{3,1,2,0:T(8,128)} fusion(f32[25,36,4,514]{3,1,2,0:T(8,128)S(1)} %get-tuple-element.9), kind=kLoop, calls=%fused_computation.9 | loop fusion | flops 4147200 | bytes 16588800 | tf_op jit(solution)/shard_map/add | solution.py:113
  525.4 5.5 %fusion.4 = f32[25,36,2,513]{3,1,2,0:T(8,128)S(1)} fusion(f32[25,36,4,514]{3,1,2,0:T(8,128)} %get-tuple-element.10), kind=kLoop, calls=%fused_computation.17 | loop fusion | flops 2770200 | bytes 11080800 | tf_op jit(solution)/shard_map/add | solution.py:114
  532.3 3.9 multiply_multiply_fusion.4
  541.0 4.7 copy.77
  (134 shorter events, 77.1 us)
Async XLA Ops:
  9.7 14.6 %copy-start.13 = (f32[1024]{0:T(1024)S(1)}, f32[1024]{0:T(1024)}, u32[]{:S(2)}) copy-start(f32[1024]{0:T(1024)} %param.10) | copy-start | bytes 12292
  9.7 14.6 %copy-start.14 = (f32[1024]{0:T(1024)S(1)}, f32[1024]{0:T(1024)}, u32[]{:S(2)}) copy-start(f32[1024]{0:T(1024)} %param.9) | copy-start | bytes 12292
  14.0 52.4 %all-to-all-start.1 = ((f32[1,1,1024]{1,0,2:T(1,128)}), f32[1,1,1024]{1,0,2:T(1,128)S(1)}, u32[]{:S(2)}, u32[]{:S(2)}) async-start(f32[1,1,1024]{1,0,2:T(1,128)} %copy.59), calls=%async_computation.1 | async-start | bytes 1048576 | tf_op jit(solution)/shard_map/all_to_all | solution.py:86
  66.3 88.9 %all-to-all-start = ((f32[32,1,28800]{2,1,0:T(1,128)}), f32[32,1,28800]{2,1,0:T(1,128)}, u32[]{:S(2)}, u32[]{:S(2)}) async-start(f32[32,1,28800]{2,1,0:T(1,128)} %reshape.196), calls=%async_computation | async-start | bytes 7372800 | tf_op jit(solution)/shard_map/all_to_all | solution.py:85
  270.4 8.6 %copy-start.12 = (f32[2,512]{1,0:T(2,128)S(1)}, f32[2,512]{1,0:T(2,128)}, u32[]{:S(2)}) copy-start(f32[2,512]{1,0:T(2,128)} %param.13) | copy-start | bytes 12292
  270.4 13.6 %copy-start.15 = (f32[2,512]{1,0:T(2,128)S(1)}, f32[2,512]{1,0:T(2,128)}, u32[]{:S(2)}) copy-start(f32[2,512]{1,0:T(2,128)} %param.15) | copy-start | bytes 12292
  270.4 13.6 %copy-start.16 = (f32[2,512]{1,0:T(2,128)S(1)}, f32[2,512]{1,0:T(2,128)}, u32[]{:S(2)}) copy-start(f32[2,512]{1,0:T(2,128)} %param.14) | copy-start | bytes 12292
  270.4 14.4 %copy-start.17 = (s32[2,512]{1,0:T(2,128)S(1)}, s32[2,512]{1,0:T(2,128)}, u32[]{:S(2)}) copy-start(s32[2,512]{1,0:T(2,128)} %param.12) | copy-start | bytes 12292
  273.7 84.7 %collective-permute-start.5 = (f32[25,36,1,512]{3,2,1,0:T(1,128)S(1)}, f32[25,36,1,512]{3,2,1,0:T(1,128)}, u32[]{:S(2)}, u32[]{:S(2)}) collective-permute-start(f32[25,36,1,512]{3,2,1,0:T(1,128)S(1)} %copy.62), channel_id=1, source_target_pairs={{4,0},{8,4},{12,8},{16,12},{20,16},{24,20},{28,24},{0,28},{5,1},{9... | collective-permute-start | bytes 5529608 | tf_op jit(solution)/shard_map/ppermute | solution.py:20
  279.0 81.1 %collective-permute-start.4 = (f32[25,36,1,512]{3,2,1,0:T(1,128)}, f32[25,36,1,512]{3,2,1,0:T(1,128)}, u32[]{:S(2)}, u32[]{:S(2)}) collective-permute-start(f32[25,36,1,512]{3,2,1,0:T(1,128)} %copy.61), channel_id=1, source_target_pairs={{0,4},{4,8},{8,12},{12,16},{16,20},{20,24},{24,28},{28,0},{1,5},{5... | collective-permute-start | bytes 5529608 | tf_op jit(solution)/shard_map/ppermute | solution.py:18
  279.0 75.8 %collective-permute-start = (f32[1,512]{1,0:T(1,128)S(1)}, f32[1,512]{1,0:T(1,128)S(1)}, u32[]{:S(2)}, u32[]{:S(2)}) collective-permute-start(f32[1,512]{1,0:T(1,128)S(1)} %get-tuple-element.25), channel_id=1, source_target_pairs={{0,4},{4,8},{8,12},{12,16},{16,20},{20,24},{24,28},{28,0},{1,5},{5... | collective-permute-start | bytes 6152 | tf_op jit(solution)/shard_map/ppermute | solution.py:18
  281.1 74.0 %collective-permute-start.1 = (f32[1,512]{1,0:T(1,128)S(1)}, f32[1,512]{1,0:T(1,128)S(1)}, u32[]{:S(2)}, u32[]{:S(2)}) collective-permute-start(f32[1,512]{1,0:T(1,128)S(1)} %get-tuple-element.26), channel_id=1, source_target_pairs={{4,0},{8,4},{12,8},{16,12},{20,16},{24,20},{28,24},{0,28},{5,1},{9... | collective-permute-start | bytes 6152 | tf_op jit(solution)/shard_map/ppermute | solution.py:20
  283.9 78.0 %copy-start.1 = (f32[25,36,2,512]{3,1,2,0:T(8,128)S(1)}, f32[25,36,2,512]{3,1,2,0:T(8,128)}, u32[]{:S(2)}) copy-start(f32[25,36,2,512]{3,1,2,0:T(8,128)} %copy-done) | copy-start | bytes 11059204
  355.3 3.0 collective-permute-start.2
  355.3 3.1 collective-permute-start.3
  369.5 7.9 %collective-permute-start.7 = (f32[25,36,4,1]{1,2,3,0:T(4,128)S(1)}, f32[25,36,4,1]{1,2,3,0:T(4,128)S(1)}, u32[]{:S(2)}, u32[]{:S(2)}) collective-permute-start(f32[25,36,4,1]{1,2,3,0:T(4,128)S(1)} %copy.66), channel_id=1, source_target_pairs={{1,0},{2,1},{3,2},{0,3},{5,4},{6,5},{7,6},{4,7},{9,8},{10,9},{11,1... | collective-permute-start | bytes 43208 | tf_op jit(solution)/shard_map/ppermute | solution.py:20
  371.2 4.0 collective-permute-start.6
  371.3 19.8 %copy-start.8 = (f32[25,4,514]{2,1,0:T(4,128)}, f32[25,4,514]{2,1,0:T(4,128)S(1)}, u32[]{:S(2)}) copy-start(f32[25,4,514]{2,1,0:T(4,128)S(1)} %broadcast_multiply_fusion) | copy-start | bytes 616804
  410.4 83.9 %copy-start.3 = (f32[25,36,2,512]{3,1,2,0:T(8,128)}, f32[25,36,2,512]{3,1,2,0:T(8,128)S(1)}, u32[]{:S(2)}) copy-start(f32[25,36,2,512]{3,1,2,0:T(8,128)S(1)} %fusion.17) | copy-start | bytes 11059204
  412.9 81.1 %collective-permute-start.9 = (f32[25,36,1,512]{3,2,1,0:T(1,128)S(1)}, f32[25,36,1,512]{3,2,1,0:T(1,128)S(1)}, u32[]{:S(2)}, u32[]{:S(2)}) collective-permute-start(f32[25,36,1,512]{3,2,1,0:T(1,128)S(1)} %copy.70), channel_id=1, source_target_pairs={{4,0},{8,4},{12,8},{16,12},{20,16},{24,20},{28,24},{0,28},{5,1},{9... | collective-permute-start | bytes 5529608 | tf_op jit(solution)/shard_map/ppermute | solution.py:20
  419.6 74.5 %collective-permute-start.8 = (f32[25,36,1,512]{3,2,1,0:T(1,128)S(1)}, f32[25,36,1,512]{3,2,1,0:T(1,128)S(1)}, u32[]{:S(2)}, u32[]{:S(2)}) collective-permute-start(f32[25,36,1,512]{3,2,1,0:T(1,128)S(1)} %copy.69), channel_id=1, source_target_pairs={{0,4},{4,8},{8,12},{12,16},{16,20},{20,24},{24,28},{28,0},{1,5},{5... | collective-permute-start | bytes 5529608 | tf_op jit(solution)/shard_map/ppermute | solution.py:18
  497.2 10.9 %copy-start.9 = (f32[25,4,514]{2,1,0:T(4,128)S(1)}, f32[25,4,514]{2,1,0:T(4,128)}, u32[]{:S(2)}) copy-start(f32[25,4,514]{2,1,0:T(4,128)} %copy-done.8) | copy-start | bytes 616804
  499.6 4.2 collective-permute-start.10
  502.0 3.9 collective-permute-start.11
  (12 other events, 61.4 us)
where the time goes:
time: 557 us; the launch traced here: 546 us
  waiting for transfers between devices  214 us (38%)
  other arithmetic  138 us (25%)
  local copies, waits for them, and re-layouts  96.9 us (17%)
  matrix products  65.2 us (12%)
  starting transfers between devices  30.7 us (6%)
    ppermute x6, waiting for transfers between devices, with_halo(): lax.ppermute(tail, axis, [(i, (i + 1) % count) for i in range(count)])  75.2 us
    ppermute x6, waiting for transfers between devices, with_halo(): lax.ppermute(head, axis, [((i + 1) % count, i) for i in range(count)])  74.6 us
    all_to_all x1, waiting for transfers between devices, on_device(): lax.all_to_all(outgoing, ('lon', 'lat'), split_axis=2, concat_axis=2, til...  64.2 us
    dot_general x2, matrix products, route_rows(): jnp.dot(values, picker, precision=lax.Precision.HIGHEST, preferred_elemen...  63.7 us
    all_to_all x1, other arithmetic, on_device(): lax.all_to_all(outgoing, ('lon', 'lat'), split_axis=2, concat_axis=2, til...  40 us
    unnamed x46, local copies, waits for them, and re-layouts  30.8 us
    mul x2, other arithmetic, on_device(): qx = cx_pad * padded  23.2 us
    convert_element_type x1, other arithmetic, on_device(): placed = ids_in.astype(jnp.int32)  18.5 us
  transfers between devices with their start and end apart: 14, of which 6 were waited for; matrix products, arithmetic and copies ran while one was open for 14% of the time, Pallas kernels for 0%

commit v1 on v0

v1 whole, which is shorter than its diff:
```python
import functools
import math

import jax
import jax.numpy as jnp
import numpy as np
from jax import lax
from jax.experimental import pallas as pl
from jax.experimental.pallas import tpu as pltpu
from jax.sharding import PartitionSpec as P

F32 = jnp.float32
BF16 = jnp.bfloat16
NSUB = 2
LANES = 128
SUB = 8
CHUNKS = (9, 8, 8)
NBLOCK = 256
VMEM_LIMIT = 32 * 2**20


def ceil_to(value, step):
    return -(-value // step) * step


def divide(value, count):
    if count & (count - 1) == 0:
        return value >> (count.bit_length() - 1), value & (count - 1)
    quotient = value // count
    return quotient, value - quotient * count


class Plan:
    def __init__(self, count, ndir, cap, labels):
        self.cap = cap
        self.parts = LANES // cap
        self.rows = count * ndir + (1 if labels else 0)
        self.per = -(-self.rows // self.parts)
        self.padded = ceil_to(self.per, SUB)
        self.total = self.parts * self.padded
        self.label_row = (
            count * ndir // self.per * self.padded + count * ndir % self.per if labels else None
        )

    def pieces(self, start, length):
        found = []
        at = start
        while at < start + length:
            part, inside = divmod(at, self.per)
            take = min(self.per - inside, start + length - at)
            found.append((at - start, part * self.padded + inside, take))
            at += take
        return found


def swap_blocks(blocks, cap):
    parts = len(blocks)
    lane = lax.broadcasted_iota(jnp.int32, blocks[0].shape, 1)
    rolled = [pltpu.roll(b, cap * q, 1) if q else b for q, b in enumerate(blocks)]
    result = []
    for i in range(parts):
        mixed = rolled[-i % parts]
        for j in range(1, parts):
            mixed = jnp.where(lane >= j * cap, rolled[(j - i) % parts], mixed)
        result.append(pltpu.roll(mixed, LANES - cap * i, 1) if i else mixed)
    return result


def split_rows(x_ref, pair_ref):
    total = x_ref.shape[0]
    whole = x_ref[...]
    high = whole.astype(BF16)
    pair_ref[0:total, :] = high
    pair_ref[total : 2 * total, :] = (whole - high.astype(F32)).astype(BF16)


def route(pair_ref, picks, first):
    slots = pair_ref.shape[1]
    total = pair_ref.shape[0] // 2
    wanted = lax.broadcasted_iota(jnp.int32, (NBLOCK, slots), 0) + first
    onehot = jnp.where(wanted == picks, 1.0, 0.0).astype(BF16)
    both = lax.dot_general(
        pair_ref[...], onehot, (((1,), (1,)), ((), ())), preferred_element_type=F32
    )
    return both[:total] + both[total:]


def send_rows(plan, pair_ref, target, out_ref):
    slots = pair_ref.shape[1]
    groups = NBLOCK // LANES
    for block in range(slots // NBLOCK):
        moved = route(pair_ref, target, block * NBLOCK)
        for g in range(groups):
            blocks = [
                moved[q * plan.padded : (q + 1) * plan.padded, g * LANES : (g + 1) * LANES]
                for q in range(plan.parts)
            ]
            for i, message in enumerate(swap_blocks(blocks, plan.cap)):
                out_ref[(block * groups + g) * plan.parts + i] = message


def source_rows(plan, spectra_ref, first, count, nfreq, gain, x_ref):
    ndir = spectra_ref.shape[1]
    for f in range(count):
        ratio = float(np.float32(1.1) ** np.float32(first + f - (nfreq - 1)))
        rows = spectra_ref[f] * jnp.exp(gain * ratio)
        for offset, row, length in plan.pieces(f * ndir, ndir):
            x_ref[row : row + length, :] = rows[offset : offset + length]


def first_source_kernel(
    plan, count, shape, spectra_ref, growth_ref, dir_ref, cell_ref,
    out_ref, gain_ref, target_ref, x_ref, pair_ref,
):
    rows_x, rows_y, lat_count, devices = shape
    nfreq, ndir, slots = spectra_ref.shape
    dtheta = 2.0 * math.pi / ndir
    total = None
    for f in range(nfreq):
        width = float(np.float32(0.1) * np.float32(1.1) ** np.float32(f)) * dtheta
        term = spectra_ref[f] * width
        total = term if total is None else total + term
    energy = jnp.sum(total, axis=0, keepdims=True)
    load = energy / (energy + 10.0)
    theta = (lax.broadcasted_iota(jnp.int32, (ndir, slots), 0).astype(F32) + 0.5) * dtheta
    lobe = jnp.maximum(jnp.cos(theta - dir_ref[...]), 0.0)
    gain = growth_ref[...] * (lobe * lobe) - 0.4 * load
    gain_ref[...] = gain

    point = cell_ref[...]
    valid = point >= 0
    col_x, col_y = divide(jnp.maximum(point, 0), rows_y * lat_count)
    own_x, in_x = divide(col_x, rows_x)
    own_y, in_y = divide(col_y, rows_y)
    owner = jnp.where(valid, own_x * lat_count + own_y, devices)
    band, lane = divide(in_y, LANES)
    label = jnp.where(valid, (band * rows_x + in_x) * LANES + lane + 1, 0).astype(F32)
    ids = lax.broadcasted_iota(jnp.int32, (devices, slots), 0)
    hits = jnp.where(ids == owner, 1.0, 0.0)
    lower = lax.broadcasted_iota(jnp.int32, (LANES, LANES), 0) < lax.broadcasted_iota(
        jnp.int32, (LANES, LANES), 1
    )
    ahead = jnp.where(lower, 1.0, 0.0).astype(BF16)
    carry = jnp.zeros((devices, 1), F32)
    places = []
    for b in range(slots // LANES):
        part = hits[:, b * LANES : (b + 1) * LANES]
        before = jnp.dot(part.astype(BF16), ahead, preferred_element_type=F32) + carry
        places.append(jnp.sum(before * part, axis=0, keepdims=True))
        carry = carry + jnp.sum(part, axis=1, keepdims=True)
    place = jnp.concatenate(places, axis=1).astype(jnp.int32)
    target = jnp.where(valid, owner * plan.cap + place, slots)
    target_ref[...] = target

    source_rows(plan, spectra_ref, 0, count, nfreq, gain, x_ref)
    x_ref[plan.label_row : plan.label_row + 1, :] = label
    split_rows(x_ref, pair_ref)
    send_rows(plan, pair_ref, target, out_ref)


def later_source_kernel(
    plan, first, count, nfreq, spectra_ref, gain_ref, target_ref, out_ref, x_ref, pair_ref
):
    source_rows(plan, spectra_ref, first, count, nfreq, gain_ref[...], x_ref)
    split_rows(x_ref, pair_ref)
    send_rows(plan, pair_ref, target_ref[...], out_ref)


def as_tile(grid_ref):
    grid = grid_ref[...].astype(F32)
    bands = grid.shape[1] // LANES
    return jnp.concatenate([grid[:, b * LANES : (b + 1) * LANES] for b in range(bands)], axis=0)


def tile_ids():
    return (
        lax.broadcasted_iota(jnp.int32, (SUB, LANES), 0),
        lax.broadcasted_iota(jnp.int32, (SUB, LANES), 1),
    )


def edge_messages(read, weight, f, ndir, right_ref, left_ref, up_ref, down_ref):
    row, lane = tile_ids()
    odd = (row & 1) == 1
    quarter = ndir // 4
    up = jnp.zeros((SUB, LANES), F32)
    down = jnp.zeros((SUB, LANES), F32)
    moved = [read(d) * weight for d in range(ndir)]
    for e in range(quarter):
        a, b = moved[3 * quarter + e], moved[e]
        right_ref[f, e] = jnp.where(odd, b, pltpu.roll(a, SUB - 1, 0))
        a, b = moved[quarter + e], moved[2 * quarter + e]
        left_ref[f, e] = jnp.where(odd, pltpu.roll(b, 1, 0), a)
    for k in range(2 * quarter):
        up = jnp.where(lane == k, pltpu.roll(moved[k], k + 1, 1), up)
        low = moved[2 * quarter + k]
        down = jnp.where(lane == k, pltpu.roll(low, k, 1) if k else low, down)
    up_ref[f] = up
    down_ref[f] = down


def place_kernel(plan, first, count, ndir, with_labels, *refs):
    if with_labels:
        in_ref, speed_ref, shoal_ref, *refs = refs
        own_ref, right_ref, left_ref, up_ref, down_ref, label_ref, x_ref, pair_ref = refs
    else:
        in_ref, speed_ref, shoal_ref, label_ref, *refs = refs
        own_ref, right_ref, left_ref, up_ref, down_ref, x_ref, pair_ref = refs
    slots = x_ref.shape[1]
    for g in range(slots // LANES):
        blocks = [in_ref[g * plan.parts + i] for i in range(plan.parts)]
        for q, part in enumerate(swap_blocks(blocks, plan.cap)):
            x_ref[q * plan.padded : (q + 1) * plan.padded, g * LANES : (g + 1) * LANES] = part
    if with_labels:
        label_ref[...] = x_ref[plan.label_row : plan.label_row + 1, :].astype(jnp.int32) - 1
    label = label_ref[...]
    split_rows(x_ref, pair_ref)
    for block in range(slots // NBLOCK):
        placed = route(pair_ref, label, block * NBLOCK)
        for t in range(NBLOCK // LANES):
            row = block * (NBLOCK // LANES) + t
            for q in range(plan.parts):
                length = min(plan.per, count * ndir - q * plan.per)
                if length > 0:
                    own_ref[pl.ds(q * plan.per * SUB + row, length, stride=SUB), :] = placed[
                        q * plan.padded : q * plan.padded + length, t * LANES : (t + 1) * LANES
                    ]
    shoal = as_tile(shoal_ref)

    @pl.loop(0, count)
    def pack(f):
        def read(d):
            return own_ref[pl.ds(pl.multiple_of((f * ndir + d) * SUB, SUB), SUB), :]

        edge_messages(
            read, shoal * speed_ref[first + f], f, ndir, right_ref, left_ref, up_ref, down_ref
        )


def step_kernel(first, last, *refs):
    (own_ref, right_in, left_in, up_in, down_in, speed_ref,
     shoal_ref, slope_x_ref, slope_y_ref, mask_ref, *refs) = refs
    if last:
        *refs, new_ref, turn_ref, done_sem = refs
        out_ref = refs[-1]
    else:
        new_ref, right_ref, left_ref, up_ref, down_ref, turn_ref = refs
    count, ndir = own_ref.shape[:2]
    quarter = ndir // 4
    row, lane = tile_ids()
    odd = (row & 1) == 1
    shoal = as_tile(shoal_ref)
    slope_x = as_tile(slope_x_ref)
    slope_y = as_tile(slope_y_ref)
    sea = as_tile(mask_ref)
    angle = [(d + 0.5) * (2.0 * math.pi / ndir) for d in range(ndir)]
    cos = [math.cos(a) for a in angle]
    sin = [math.sin(a) for a in angle]
    for d in range(ndir):
        turn_ref[d] = sin[d] * slope_x - cos[d] * slope_y

    @pl.loop(0, count)
    def advance(f):
        speed = speed_ref[first + f]
        weight = shoal * speed
        up_all = up_in[f]
        down_all = down_in[f]

        def halved(d):
            field = own_ref[f, d]
            moved = weight * field
            if d >= 3 * quarter or d < quarter:
                edge = right_in[f, d % quarter]
                if d < quarter:
                    edge = pltpu.roll(edge, SUB - 1, 0)
                from_x = jnp.where(odd, pltpu.roll(moved, 1, 0), edge)
            else:
                edge = left_in[f, d % quarter]
                if d < 2 * quarter:
                    edge = pltpu.roll(edge, 1, 0)
                from_x = jnp.where(odd, edge, pltpu.roll(moved, SUB - 1, 0))
            if d < 2 * quarter:
                near = pltpu.roll(moved, 1, 1)
                edge = pltpu.roll(up_all, LANES - d, 1) if d else up_all
                far = pltpu.roll(jnp.where(row >= SUB - 2, edge, near), 2, 0)
                from_y = jnp.where(lane == 0, far, near)
            else:
                near = pltpu.roll(moved, LANES - 1, 1)
                edge = pltpu.roll(down_all, LANES - 1 - (d - 2 * quarter), 1)
                far = pltpu.roll(jnp.where(row < 2, edge, near), SUB - 2, 0)
                from_y = jnp.where(lane == LANES - 1, far, near)
            along, across = abs(cos[d]), abs(sin[d])
            half = field - (along + across) * moved + along * from_x + across * from_y
            return half, turn_ref[d] * (half * speed)

        half_top, qt_top = halved(ndir - 1)
        half, qt = halved(0)
        below = jnp.maximum(qt_top, 0.0) + jnp.minimum(qt, 0.0)
        flux_top = below
        for d in range(ndir):
            if d < ndir - 2:
                half_next, qt_next = halved(d + 1)
            else:
                half_next, qt_next = half_top, qt_top
            if d < ndir - 1:
                above = jnp.maximum(qt, 0.0) + jnp.minimum(qt_next, 0.0)
            else:
                above = flux_top
            new_ref[f, d] = (half - above + below) * sea
            half, qt, below = half_next, qt_next, above
        if not last:
            edge_messages(
                lambda d: new_ref[f, d], weight, f, ndir, right_ref, left_ref, up_ref, down_ref
            )

    if last:
        copy = pltpu.make_async_copy(new_ref, out_ref.at[pl.ds(first, count)], done_sem)
        copy.start()
        copy.wait()


def params():
    return pltpu.CompilerParams(vmem_limit_bytes=VMEM_LIMIT)


def vmem(count):
    return [pl.BlockSpec(memory_space=pltpu.VMEM)] * count


SMEM_SPEC = pl.BlockSpec(memory_space=pltpu.SMEM)
ANY_SPEC = pl.BlockSpec(memory_space=pl.ANY)


def edge_shapes(count, ndir):
    tile = jax.ShapeDtypeStruct((count, ndir // 4, SUB, LANES), F32)
    line = jax.ShapeDtypeStruct((count, SUB, LANES), F32)
    return [tile, tile, line, line]


def send_edges(edges):
    right, left, up, down = edges
    lon = lax.axis_size("lon")
    lat = lax.axis_size("lat")
    return (
        lax.ppermute(right, "lon", [(i, (i + 1) % lon) for i in range(lon)]),
        lax.ppermute(left, "lon", [((i + 1) % lon, i) for i in range(lon)]),
        lax.ppermute(up, "lat", [(i, i + 1) for i in range(lat - 1)]),
        lax.ppermute(down, "lat", [(i + 1, i) for i in range(lat - 1)]),
    )


def on_device(spectra, wind_growth, wind_dir, point_cell, land_mask, shoaling, slope_x, slope_y):
    nfreq, ndir, slots = spectra.shape
    rows_x, rows_y = land_mask.shape
    lat_count = lax.axis_size("lat")
    devices = lax.axis_size("lon") * lat_count
    cap = slots // devices
    speed = jnp.asarray((0.65 * 1.1 ** -np.arange(nfreq)).astype(np.float32))
    starts = [sum(CHUNKS[:i]) for i in range(len(CHUNKS))]
    plans = [Plan(count, ndir, cap, i == 0) for i, count in enumerate(CHUNKS)]

    messages = []
    for i, (first, count, plan) in enumerate(zip(starts, CHUNKS, plans)):
        shape = jax.ShapeDtypeStruct((devices, plan.padded, LANES), F32)
        scratch = [
            pltpu.VMEM((plan.total, slots), F32),
            pltpu.VMEM((2 * plan.total, slots), BF16),
        ]
        if i == 0:
            message, gain, target = pl.pallas_call(
                functools.partial(
                    first_source_kernel, plan, count, (rows_x, rows_y, lat_count, devices)
                ),
                out_shape=[
                    shape,
                    jax.ShapeDtypeStruct((ndir, slots), F32),
                    jax.ShapeDtypeStruct((1, slots), jnp.int32),
                ],
                in_specs=vmem(4),
                out_specs=vmem(3),
                scratch_shapes=scratch,
                compiler_params=params(),
                name="source_first",
            )(
                spectra,
                wind_growth.reshape(1, slots),
                wind_dir.reshape(1, slots),
                point_cell.reshape(1, slots),
            )
        else:
            message = pl.pallas_call(
                functools.partial(later_source_kernel, plan, first, count, nfreq),
                out_shape=shape,
                in_specs=[pl.BlockSpec((pl.Element(count), pl.Element(ndir), pl.Element(slots)), lambda i, s=first: (s, 0, 0))]
                + [pl.BlockSpec((ndir, slots), lambda i: (0, 0)), pl.BlockSpec((1, slots), lambda i: (0, 0))],
                out_specs=pl.BlockSpec(shape.shape, lambda i: (0, 0, 0)),
                grid=(1,),
                scratch_shapes=scratch,
                compiler_params=params(),
                name="source_later",
            )(spectra, gain, target)
        messages.append(message)

    out = None
    label = None
    for i, (first, count, plan) in enumerate(zip(starts, CHUNKS, plans)):
        arrived = lax.all_to_all(
            messages[i], ("lon", "lat"), split_axis=0, concat_axis=0, tiled=True
        )
        edges = edge_shapes(count, ndir)
        own_shape = jax.ShapeDtypeStruct((count * ndir * SUB, LANES), F32)
        label_shape = jax.ShapeDtypeStruct((1, slots), jnp.int32)
        placed = pl.pallas_call(
            functools.partial(place_kernel, plan, first, count, ndir, i == 0),
            out_shape=[own_shape] + edges + ([label_shape] if i == 0 else []),
            in_specs=vmem(1) + [SMEM_SPEC] + vmem(1 if i == 0 else 2),
            out_specs=vmem(6 if i == 0 else 5),
            scratch_shapes=[
                pltpu.VMEM((plan.total, slots), F32),
                pltpu.VMEM((2 * plan.total, slots), BF16),
            ],
            compiler_params=params(),
            name="place",
        )(arrived, speed, shoaling, *([] if i == 0 else [label]))
        if i == 0:
            *placed, label = placed
        field, *sent = placed
        field = field.reshape(count, ndir, SUB, LANES)
        for step in range(NSUB):
            last = step == NSUB - 1
            received = send_edges(sent)
            whole = jax.ShapeDtypeStruct((nfreq, ndir, SUB, LANES), F32)
            same = jax.ShapeDtypeStruct(field.shape, F32)
            tables = [pltpu.VMEM((ndir, SUB, LANES), F32)]
            chained = last and out is not None
            result = pl.pallas_call(
                functools.partial(step_kernel, first, last),
                out_shape=whole if last else [same] + edges,
                in_specs=vmem(5) + [SMEM_SPEC] + vmem(4) + ([ANY_SPEC] if chained else []),
                out_specs=ANY_SPEC if last else vmem(5),
                scratch_shapes=(
                    [pltpu.VMEM(field.shape, F32)] + tables + [pltpu.SemaphoreType.DMA(())]
                    if last
                    else tables
                ),
                input_output_aliases={10: 0} if chained else {},
                compiler_params=params(),
                name="last_step" if last else "step",
            )(
                field, *received, speed, shoaling, slope_x, slope_y, land_mask,
                *([out] if chained else []),
            )
            if last:
                out = result
            else:
                field, *sent = result
    bands = rows_y // LANES
    out = out.reshape(nfreq, ndir, bands, rows_x, LANES)
    return out.transpose(0, 1, 3, 2, 4).reshape(nfreq, ndir, rows_x, rows_y)


def solution(mesh):
    placed = (
        P(None, None, ("lon", "lat")),
        P(("lon", "lat")),
        P(("lon", "lat")),
        P(("lon", "lat")),
        P("lon", "lat"),
        P("lon", "lat"),
        P("lon", "lat"),
        P("lon", "lat"),
    )
    return jax.shard_map(
        on_device,
        mesh=mesh,
        in_specs=placed,
        out_specs=P(None, None, "lon", "lat"),
        check_vma=False,
    )
```

time: 557 us -> 204 us (0.37)
  the two profiles are of different devices: /device:TPU:0 before, /device:TPU:29 now
where the time goes in v1:
time: 204 us; the launch traced here: 203 us
  starting transfers between devices  61.2 us (30%)
  waiting for transfers between devices  59.9 us (29%)
  Pallas kernels  34.5 us (17%)
  blocking collectives  33.3 us (16%)
  local copies, waits for them, and re-layouts  14 us (7%)
    all_to_all x2, waiting for transfers between devices, on_device(): lax.all_to_all(messages[i], ('lon', 'lat'), split_axis=0, concat_axis=0,...  39.4 us
    all_to_all x1, blocking collectives, on_device(): lax.all_to_all(messages[i], ('lon', 'lat'), split_axis=0, concat_axis=0,...  33.3 us
    ppermute x6, starting transfers between devices, send_edges(): lax.ppermute(up, 'lat', [(i, i + 1) for i in range(lat - 1)])  21.5 us
    pallas_call x6, Pallas kernels, on_device(): pl.pallas_call(functools.partial(step_kernel, first, last), out_shape=who...  16.7 us
    ppermute x6, waiting for transfers between devices, send_edges(): lax.ppermute(right, 'lon', [(i, (i + 1) % lon) for i in range(lon)])  15.4 us
    unnamed x44, local copies, waits for them, and re-layouts  14 us
    ppermute x6, starting transfers between devices, send_edges(): lax.ppermute(right, 'lon', [(i, (i + 1) % lon) for i in range(lon)])  12.5 us
    all_to_all x2, starting transfers between devices, on_device(): lax.all_to_all(messages[i], ('lon', 'lat'), split_axis=0, concat_axis=0,...  12.3 us
  transfers between devices with their start and end apart: 26, of which 5 were waited for; matrix products, arithmetic and copies ran while one was open for 0% of the time, Pallas kernels for 13%

profile of v1, /device:TPU:29, one launch (start us, length us, event | category | flops | bytes accessed | tf_op | source)
XLA Modules:
  0.0 203.3 jit_solution(13941116885392160613)
XLA Ops:
  4.2 3.2 %source_first.1 = (f32[32,88,128]{2,1,0:T(8,128)S(1)}, f32[36,1024]{1,0:T(8,128)S(1)}, s32[1,1024]{1,0:T(1,128)S(1)}) custom-call(f32[25,36,1024]{2,1,0:T(8,128)S(1)} %copy-done, f32[1,1024]{1,0:T(1,128)S(1)} %bitcast.14, f32[1,1024]{1,0:T(1,128)S(1)} %bitcast.15, s32[1,1024]{1,0:T(1,128)S(1)} %bitcast.16), custom_call_target="tpu_custom_call" | custom-call | tf_op jit(solution)/shard_map/source_first/pallas_call | solution.py:370
  10.3 33.3 %all_to_all.15.refs_0_ = f32[32,72,128]{2,1,0:T(8,128)} all-to-all(f32[32,72,128]{2,1,0:T(8,128)S(1)} %source_later.3), channel_id=1, replica_groups=mesh['lon'=8,'lat'=4] {'lon','lat'}, dimensions={0} | all-to-all | bytes 2359296 | tf_op jit(solution)/shard_map/all_to_all | solution.py:407
  43.6 6.1 %all-to-all-start.1 = ((f32[32,88,128]{2,1,0:T(8,128)}), f32[32,88,128]{2,1,0:T(8,128)S(1)}, u32[]{:S(2)}, u32[]{:S(2)}) async-start(f32[32,88,128]{2,1,0:T(8,128)} %copy-done.4), calls=%async_computation.1 | async-start | bytes 2883584 | tf_op jit(solution)/shard_map/all_to_all | solution.py:407
  54.7 27.3 %all-to-all-done.1.refs_0_ = f32[32,88,128]{2,1,0:T(8,128)S(1)} async-done(((f32[32,88,128]{2,1,0:T(8,128)}), f32[32,88,128]{2,1,0:T(8,128)S(1)}, u32[]{:S(2)}, u32[]{:S(2)}) %all-to-all-start.1) | async-done | bytes 1441824 | tf_op jit(solution)/shard_map/all_to_all | solution.py:407
  82.0 6.2 %all-to-all-start = ((f32[32,72,128]{2,1,0:T(8,128)}), f32[32,72,128]{2,1,0:T(8,128)S(1)}, u32[]{:S(2)}, u32[]{:S(2)}) async-start(f32[32,72,128]{2,1,0:T(8,128)} %copy-done.3), calls=%async_computation | async-start | bytes 2359296 | tf_op jit(solution)/shard_map/all_to_all | solution.py:407
  88.2 4.2 %place.3 = (f32[2592,128]{1,0:T(8,128)S(1)}, f32[9,9,8,128]{3,2,1,0:T(8,128)}, f32[9,9,8,128]{3,2,1,0:T(8,128)}, f32[9,8,128]{2,1,0:T(8,128)}, f32[9,8,128]{2,1,0:T(8,128)S(1)}, /*index=5*/s32[1,1024]{1,0:T(1,128)S(1)}) custom-call(f32[32,88,128]{2,1,0:T(8,128)S(1)} %all-to-all-done.1.refs_0_, f32[25]{0:T(128)S(1)} %copy-done.13, f32[2,512]{1,0:T(2,128)S(1)} %copy-done.9), custom_call_target="tpu_custom_call" | custom-call | tf_op jit(solution)/shard_map/place/pallas_call | solution.py:413
  93.5 3.9 %place.5 = (f32[2304,128]{1,0:T(8,128)S(1)}, f32[8,9,8,128]{3,2,1,0:T(8,128)}, f32[8,9,8,128]{3,2,1,0:T(8,128)}, f32[8,8,128]{2,1,0:T(8,128)S(1)}, f32[8,8,128]{2,1,0:T(8,128)S(1)}) custom-call(f32[32,72,128]{2,1,0:T(8,128)S(1)} %copy-done.2, f32[25]{0:T(128)S(1)} %copy-done.13, f32[2,512]{1,0:T(2,128)S(1)} %copy-done.9, s32[1,1024]{1,0:T(1,128)S(1)} %get-tuple-element.42.refs_3_), custom_call_target="tpu_custom_call" | custom-call | tf_op jit(solution)/shard_map/place/pallas_call | solution.py:413
  99.9 3.9 %collective-permute-start.10 = (f32[8,8,128]{2,1,0:T(8,128)S(1)}, f32[8,8,128]{2,1,0:T(8,128)S(1)}, u32[]{:S(2)}, u32[]{:S(2)}) collective-permute-start(f32[8,8,128]{2,1,0:T(8,128)S(1)} %get-tuple-element.56), channel_id=1, source_target_pairs={{0,1},{1,2},{2,3},{4,5},{5,6},{6,7},{8,9},{9,10},{10,11},{12,13},{... | collective-permute-start | bytes 98312 | tf_op jit(solution)/shard_map/ppermute | solution.py:347
  103.8 2.9 %collective-permute-start.16 = (f32[9,9,8,128]{3,2,1,0:T(8,128)}, f32[9,9,8,128]{3,2,1,0:T(8,128)S(1)}, u32[]{:S(2)}, u32[]{:S(2)}) collective-permute-start(f32[9,9,8,128]{3,2,1,0:T(8,128)} %get-tuple-element.64), channel_id=1, source_target_pairs={{0,4},{4,8},{8,12},{12,16},{16,20},{20,24},{24,28},{28,0},{1,5},{5... | collective-permute-start | bytes 995336 | tf_op jit(solution)/shard_map/ppermute | solution.py:345
  108.7 3.9 %collective-permute-done.11.refs_4_ = f32[8,8,128]{2,1,0:T(8,128)S(1)} collective-permute-done((f32[8,8,128]{2,1,0:T(8,128)S(1)}, f32[8,8,128]{2,1,0:T(8,128)S(1)}, u32[]{:S(2)}, u32[]{:S(2)}) %collective-permute-start.11) | collective-permute-done | bytes 32800 | tf_op jit(solution)/shard_map/ppermute | solution.py:348
  115.3 12.1 %all-to-all-done.refs_0_ = f32[32,72,128]{2,1,0:T(8,128)S(1)} async-done(((f32[32,72,128]{2,1,0:T(8,128)}), f32[32,72,128]{2,1,0:T(8,128)S(1)}, u32[]{:S(2)}, u32[]{:S(2)}) %all-to-all-start) | async-done | bytes 1179680 | tf_op jit(solution)/shard_map/all_to_all | solution.py:407
  128.0 3.1 %place.4 = (f32[2304,128]{1,0:T(8,128)S(1)}, f32[8,9,8,128]{3,2,1,0:T(8,128)S(1)}, f32[8,9,8,128]{3,2,1,0:T(8,128)S(1)}, f32[8,8,128]{2,1,0:T(8,128)S(1)}, f32[8,8,128]{2,1,0:T(8,128)S(1)}) custom-call(f32[32,72,128]{2,1,0:T(8,128)S(1)} %all-to-all-done.refs_0_, f32[25]{0:T(128)S(1)} %copy-done.13, f32[2,512]{1,0:T(2,128)S(1)} %copy-done.9, ...), custom_call_target="tpu_custom_call" | custom-call | tf_op jit(solution)/shard_map/place/pallas_call | solution.py:413
  137.5 2.8 %step.4 = (f32[8,36,8,128]{3,2,1,0:T(8,128)S(1)}, f32[8,9,8,128]{3,2,1,0:T(8,128)S(1)}, f32[8,9,8,128]{3,2,1,0:T(8,128)S(1)}, f32[8,8,128]{2,1,0:T(8,128)S(1)}, f32[8,8,128]{2,1,0:T(8,128)S(1)}) custom-call(f32[8,36,8,128]{3,2,1,0:T(8,128)S(1)} %bitcast.13, f32[8,9,8,128]{3,2,1,0:T(8,128)S(1)} %collective-permute-done.8.refs_1_, ...), custom_call_target="tpu_custom_call" | custom-call | tf_op jit(solution)/shard_map/step/pallas_call | solution.py:436
  140.3 4.5 %collective-permute-start.12 = (f32[8,9,8,128]{3,2,1,0:T(8,128)S(1)}, f32[8,9,8,128]{3,2,1,0:T(8,128)S(1)}, u32[]{:S(2)}, u32[]{:S(2)}) collective-permute-start(f32[8,9,8,128]{3,2,1,0:T(8,128)S(1)} %get-tuple-element.59), channel_id=1, source_target_pairs={{0,4},{4,8},{8,12},{12,16},{16,20},{20,24},{24,28},{28,0},{1,5},{5... | collective-permute-start | bytes 884744 | tf_op jit(solution)/shard_map/ppermute | solution.py:345
  144.8 3.3 %collective-permute-start.2 = (f32[8,8,128]{2,1,0:T(8,128)S(1)}, f32[8,8,128]{2,1,0:T(8,128)S(1)}, u32[]{:S(2)}, u32[]{:S(2)}) collective-permute-start(f32[8,8,128]{2,1,0:T(8,128)S(1)} %get-tuple-element.46), channel_id=1, source_target_pairs={{0,1},{1,2},{2,3},{4,5},{5,6},{6,7},{8,9},{9,10},{10,11},{12,13},{... | collective-permute-start | bytes 98312 | tf_op jit(solution)/shard_map/ppermute | solution.py:347
  150.1 2.6 %step.5 = (f32[9,36,8,128]{3,2,1,0:T(8,128)S(1)}, f32[9,9,8,128]{3,2,1,0:T(8,128)S(1)}, f32[9,9,8,128]{3,2,1,0:T(8,128)S(1)}, f32[9,8,128]{2,1,0:T(8,128)S(1)}, f32[9,8,128]{2,1,0:T(8,128)S(1)}) custom-call(f32[9,36,8,128]{3,2,1,0:T(8,128)S(1)} %bitcast.11, f32[9,9,8,128]{3,2,1,0:T(8,128)S(1)} %collective-permute-done.16.refs_1_, ...), custom_call_target="tpu_custom_call" | custom-call | tf_op jit(solution)/shard_map/step/pallas_call | solution.py:436
  152.7 3.6 %collective-permute-start.14 = (f32[8,8,128]{2,1,0:T(8,128)S(1)}, f32[8,8,128]{2,1,0:T(8,128)S(1)}, u32[]{:S(2)}, u32[]{:S(2)}) collective-permute-start(f32[8,8,128]{2,1,0:T(8,128)S(1)} %get-tuple-element.61), channel_id=1, source_target_pairs={{0,1},{1,2},{2,3},{4,5},{5,6},{6,7},{8,9},{9,10},{10,11},{12,13},{... | collective-permute-start | bytes 98312 | tf_op jit(solution)/shard_map/ppermute | solution.py:347
  159.8 4.2 %collective-permute-start.22 = (f32[9,8,128]{2,1,0:T(8,128)S(1)}, f32[9,8,128]{2,1,0:T(8,128)S(1)}, u32[]{:S(2)}, u32[]{:S(2)}) collective-permute-start(f32[9,8,128]{2,1,0:T(8,128)S(1)} %get-tuple-element.71), channel_id=1, source_target_pairs={{0,1},{1,2},{2,3},{4,5},{5,6},{6,7},{8,9},{9,10},{10,11},{12,13},{... | collective-permute-start | bytes 110600 | tf_op jit(solution)/shard_map/ppermute | solution.py:347
  169.6 3.0 %collective-permute-start.4 = (f32[8,9,8,128]{3,2,1,0:T(8,128)S(1)}, f32[8,9,8,128]{3,2,1,0:T(8,128)S(1)}, u32[]{:S(2)}, u32[]{:S(2)}) collective-permute-start(f32[8,9,8,128]{3,2,1,0:T(8,128)S(1)} %get-tuple-element.49), channel_id=1, source_target_pairs={{0,4},{4,8},{8,12},{12,16},{16,20},{20,24},{24,28},{28,0},{1,5},{5... | collective-permute-start | bytes 884744 | tf_op jit(solution)/shard_map/ppermute | solution.py:345
  172.6 15.4 %collective-permute-done.20.refs_1_ = f32[9,9,8,128]{3,2,1,0:T(8,128)S(1)} collective-permute-done((f32[9,9,8,128]{3,2,1,0:T(8,128)S(1)}, f32[9,9,8,128]{3,2,1,0:T(8,128)S(1)}, u32[]{:S(2)}, u32[]{:S(2)}) %collective-permute-start.20) | collective-permute-done | bytes 331808 | tf_op jit(solution)/shard_map/ppermute | solution.py:345
  188.0 4.5 %collective-permute-start.6 = (f32[8,8,128]{2,1,0:T(8,128)S(1)}, f32[8,8,128]{2,1,0:T(8,128)S(1)}, u32[]{:S(2)}, u32[]{:S(2)}) collective-permute-start(f32[8,8,128]{2,1,0:T(8,128)S(1)} %get-tuple-element.51), channel_id=1, source_target_pairs={{0,1},{1,2},{2,3},{4,5},{5,6},{6,7},{8,9},{9,10},{10,11},{12,13},{... | collective-permute-start | bytes 98312 | tf_op jit(solution)/shard_map/ppermute | solution.py:347
  194.4 3.1 %last_step.3.refs_10_ = f32[25,36,8,128]{3,2,1,0:T(8,128)} custom-call(f32[9,36,8,128]{3,2,1,0:T(8,128)S(1)} %get-tuple-element.68.refs_0_, f32[9,9,8,128]{3,2,1,0:T(8,128)S(1)} %collective-permute-done.20.refs_1_, f32[9,9,8,128]{3,2,1,0:T(8,128)S(1)} %collective-permute-done.21.refs_2_, f32[9,8,128]{2,1,0:T(8,128)S(1)} %collective-permute-done.22.refs_3_, ...), custom_call_target="tpu_custom_call" | custom-call | tf_op jit(solution)/shard_map/last_step/pallas_call | solution.py:436
  197.5 2.9 %last_step.4.refs_10_ = f32[25,36,8,128]{3,2,1,0:T(8,128)} custom-call(f32[8,36,8,128]{3,2,1,0:T(8,128)S(1)} %get-tuple-element.58.refs_0_, f32[8,9,8,128]{3,2,1,0:T(8,128)S(1)} %collective-permute-done.12.refs_1_, f32[8,9,8,128]{3,2,1,0:T(8,128)S(1)} %collective-permute-done.13.refs_2_, ...), custom_call_target="tpu_custom_call", output_to_operand_aliasing={{}: (10, {})} | custom-call | tf_op jit(solution)/shard_map/last_step/pallas_call | solution.py:436
  200.4 2.9 %last_step.5 = f32[25,36,8,128]{3,2,1,0:T(8,128)} custom-call(f32[8,36,8,128]{3,2,1,0:T(8,128)S(1)} %get-tuple-element.48.refs_0_, f32[8,9,8,128]{3,2,1,0:T(8,128)S(1)} %collective-permute-done.4.refs_1_, f32[8,9,8,128]{3,2,1,0:T(8,128)S(1)} %collective-permute-done.5.refs_2_, ...), custom_call_target="tpu_custom_call", output_to_operand_aliasing={{}: (10, {})} | custom-call | tf_op jit(solution)/shard_map/last_step/pallas_call | solution.py:436
  (85 shorter events, 40.0 us)
Async XLA Ops:
  43.6 38.4 %all-to-all-start.1 = ((f32[32,88,128]{2,1,0:T(8,128)}), f32[32,88,128]{2,1,0:T(8,128)S(1)}, u32[]{:S(2)}, u32[]{:S(2)}) async-start(f32[32,88,128]{2,1,0:T(8,128)} %copy-done.4), calls=%async_computation.1 | async-start | bytes 2883584 | tf_op jit(solution)/shard_map/all_to_all | solution.py:407
  82.0 45.3 %all-to-all-start = ((f32[32,72,128]{2,1,0:T(8,128)}), f32[32,72,128]{2,1,0:T(8,128)S(1)}, u32[]{:S(2)}, u32[]{:S(2)}) async-start(f32[32,72,128]{2,1,0:T(8,128)} %copy-done.3), calls=%async_computation | async-start | bytes 2359296 | tf_op jit(solution)/shard_map/all_to_all | solution.py:407
  98.5 34.7 %collective-permute-start.8 = (f32[8,9,8,128]{3,2,1,0:T(8,128)}, f32[8,9,8,128]{3,2,1,0:T(8,128)S(1)}, u32[]{:S(2)}, u32[]{:S(2)}) collective-permute-start(f32[8,9,8,128]{3,2,1,0:T(8,128)} %get-tuple-element.54), channel_id=1, source_target_pairs={{0,4},{4,8},{8,12},{12,16},{16,20},{20,24},{24,28},{28,0},{1,5},{5... | collective-permute-start | bytes 884744 | tf_op jit(solution)/shard_map/ppermute | solution.py:345
  98.5 34.7 %collective-permute-start.9 = (f32[8,9,8,128]{3,2,1,0:T(8,128)}, f32[8,9,8,128]{3,2,1,0:T(8,128)}, u32[]{:S(2)}, u32[]{:S(2)}) collective-permute-start(f32[8,9,8,128]{3,2,1,0:T(8,128)} %get-tuple-element.55), channel_id=1, source_target_pairs={{4,0},{8,4},{12,8},{16,12},{20,16},{24,20},{28,24},{0,28},{5,1},{9... | collective-permute-start | bytes 884744 | tf_op jit(solution)/shard_map/ppermute | solution.py:346
  99.9 6.8 %collective-permute-start.10 = (f32[8,8,128]{2,1,0:T(8,128)S(1)}, f32[8,8,128]{2,1,0:T(8,128)S(1)}, u32[]{:S(2)}, u32[]{:S(2)}) collective-permute-start(f32[8,8,128]{2,1,0:T(8,128)S(1)} %get-tuple-element.56), channel_id=1, source_target_pairs={{0,1},{1,2},{2,3},{4,5},{5,6},{6,7},{8,9},{9,10},{10,11},{12,13},{... | collective-permute-start | bytes 98312 | tf_op jit(solution)/shard_map/ppermute | solution.py:347
  103.8 41.0 %collective-permute-start.16 = (f32[9,9,8,128]{3,2,1,0:T(8,128)}, f32[9,9,8,128]{3,2,1,0:T(8,128)S(1)}, u32[]{:S(2)}, u32[]{:S(2)}) collective-permute-start(f32[9,9,8,128]{3,2,1,0:T(8,128)} %get-tuple-element.64), channel_id=1, source_target_pairs={{0,4},{4,8},{8,12},{12,16},{16,20},{20,24},{24,28},{28,0},{1,5},{5... | collective-permute-start | bytes 995336 | tf_op jit(solution)/shard_map/ppermute | solution.py:345
  106.7 41.4 %collective-permute-start.17 = (f32[9,9,8,128]{3,2,1,0:T(8,128)}, f32[9,9,8,128]{3,2,1,0:T(8,128)S(1)}, u32[]{:S(2)}, u32[]{:S(2)}) collective-permute-start(f32[9,9,8,128]{3,2,1,0:T(8,128)} %get-tuple-element.65), channel_id=1, source_target_pairs={{4,0},{8,4},{12,8},{16,12},{20,16},{24,20},{28,24},{0,28},{5,1},{9... | collective-permute-start | bytes 995336 | tf_op jit(solution)/shard_map/ppermute | solution.py:346
  113.2 17.9 %collective-permute-start.18 = (f32[9,8,128]{2,1,0:T(8,128)}, f32[9,8,128]{2,1,0:T(8,128)S(1)}, u32[]{:S(2)}, u32[]{:S(2)}) collective-permute-start(f32[9,8,128]{2,1,0:T(8,128)} %get-tuple-element.66), channel_id=1, source_target_pairs={{0,1},{1,2},{2,3},{4,5},{5,6},{6,7},{8,9},{9,10},{10,11},{12,13},{... | collective-permute-start | bytes 110600 | tf_op jit(solution)/shard_map/ppermute | solution.py:347
  131.1 27.2 %collective-permute-start = (f32[8,9,8,128]{3,2,1,0:T(8,128)S(1)}, f32[8,9,8,128]{3,2,1,0:T(8,128)S(1)}, u32[]{:S(2)}, u32[]{:S(2)}) collective-permute-start(f32[8,9,8,128]{3,2,1,0:T(8,128)S(1)} %get-tuple-element.44), channel_id=1, source_target_pairs={{0,4},{4,8},{8,12},{12,16},{16,20},{20,24},{24,28},{28,0},{1,5},{5... | collective-permute-start | bytes 884744 | tf_op jit(solution)/shard_map/ppermute | solution.py:345
  133.2 25.2 %collective-permute-start.1 = (f32[8,9,8,128]{3,2,1,0:T(8,128)S(1)}, f32[8,9,8,128]{3,2,1,0:T(8,128)S(1)}, u32[]{:S(2)}, u32[]{:S(2)}) collective-permute-start(f32[8,9,8,128]{3,2,1,0:T(8,128)S(1)} %get-tuple-element.45), channel_id=1, source_target_pairs={{4,0},{8,4},{12,8},{16,12},{20,16},{24,20},{28,24},{0,28},{5,1},{9... | collective-permute-start | bytes 884744 | tf_op jit(solution)/shard_map/ppermute | solution.py:346
  133.2 7.2 %collective-permute-start.19 = (f32[9,8,128]{2,1,0:T(8,128)}, f32[9,8,128]{2,1,0:T(8,128)S(1)}, u32[]{:S(2)}, u32[]{:S(2)}) collective-permute-start(f32[9,8,128]{2,1,0:T(8,128)} %copy-done.21), channel_id=1, source_target_pairs={{1,0},{2,1},{3,2},{5,4},{6,5},{7,6},{9,8},{10,9},{11,10},{13,12},{... | collective-permute-start | bytes 110600 | tf_op jit(solution)/shard_map/ppermute | solution.py:348
  140.3 32.3 %collective-permute-start.12 = (f32[8,9,8,128]{3,2,1,0:T(8,128)S(1)}, f32[8,9,8,128]{3,2,1,0:T(8,128)S(1)}, u32[]{:S(2)}, u32[]{:S(2)}) collective-permute-start(f32[8,9,8,128]{3,2,1,0:T(8,128)S(1)} %get-tuple-element.59), channel_id=1, source_target_pairs={{0,4},{4,8},{8,12},{12,16},{16,20},{20,24},{24,28},{28,0},{1,5},{5... | collective-permute-start | bytes 884744 | tf_op jit(solution)/shard_map/ppermute | solution.py:345
  144.8 7.9 %collective-permute-start.2 = (f32[8,8,128]{2,1,0:T(8,128)S(1)}, f32[8,8,128]{2,1,0:T(8,128)S(1)}, u32[]{:S(2)}, u32[]{:S(2)}) collective-permute-start(f32[8,8,128]{2,1,0:T(8,128)S(1)} %get-tuple-element.46), channel_id=1, source_target_pairs={{0,1},{1,2},{2,3},{4,5},{5,6},{6,7},{8,9},{9,10},{10,11},{12,13},{... | collective-permute-start | bytes 98312 | tf_op jit(solution)/shard_map/ppermute | solution.py:347
  148.1 8.2 %collective-permute-start.3 = (f32[8,8,128]{2,1,0:T(8,128)S(1)}, f32[8,8,128]{2,1,0:T(8,128)S(1)}, u32[]{:S(2)}, u32[]{:S(2)}) collective-permute-start(f32[8,8,128]{2,1,0:T(8,128)S(1)} %get-tuple-element.47), channel_id=1, source_target_pairs={{1,0},{2,1},{3,2},{5,4},{6,5},{7,6},{9,8},{10,9},{11,10},{13,12},{... | collective-permute-start | bytes 98312 | tf_op jit(solution)/shard_map/ppermute | solution.py:348
  152.7 7.1 %collective-permute-start.14 = (f32[8,8,128]{2,1,0:T(8,128)S(1)}, f32[8,8,128]{2,1,0:T(8,128)S(1)}, u32[]{:S(2)}, u32[]{:S(2)}) collective-permute-start(f32[8,8,128]{2,1,0:T(8,128)S(1)} %get-tuple-element.61), channel_id=1, source_target_pairs={{0,1},{1,2},{2,3},{4,5},{5,6},{6,7},{8,9},{9,10},{10,11},{12,13},{... | collective-permute-start | bytes 98312 | tf_op jit(solution)/shard_map/ppermute | solution.py:347
  156.4 7.7 %collective-permute-start.15 = (f32[8,8,128]{2,1,0:T(8,128)S(1)}, f32[8,8,128]{2,1,0:T(8,128)S(1)}, u32[]{:S(2)}, u32[]{:S(2)}) collective-permute-start(f32[8,8,128]{2,1,0:T(8,128)S(1)} %get-tuple-element.62), channel_id=1, source_target_pairs={{1,0},{2,1},{3,2},{5,4},{6,5},{7,6},{9,8},{10,9},{11,10},{13,12},{... | collective-permute-start | bytes 98312 | tf_op jit(solution)/shard_map/ppermute | solution.py:348
  158.3 29.7 %collective-permute-start.20 = (f32[9,9,8,128]{3,2,1,0:T(8,128)S(1)}, f32[9,9,8,128]{3,2,1,0:T(8,128)S(1)}, u32[]{:S(2)}, u32[]{:S(2)}) collective-permute-start(f32[9,9,8,128]{3,2,1,0:T(8,128)S(1)} %get-tuple-element.69), channel_id=1, source_target_pairs={{0,4},{4,8},{8,12},{12,16},{16,20},{20,24},{24,28},{28,0},{1,5},{5... | collective-permute-start | bytes 995336 | tf_op jit(solution)/shard_map/ppermute | solution.py:345
  158.4 34.1 %collective-permute-start.21 = (f32[9,9,8,128]{3,2,1,0:T(8,128)S(1)}, f32[9,9,8,128]{3,2,1,0:T(8,128)S(1)}, u32[]{:S(2)}, u32[]{:S(2)}) collective-permute-start(f32[9,9,8,128]{3,2,1,0:T(8,128)S(1)} %get-tuple-element.70), channel_id=1, source_target_pairs={{4,0},{8,4},{12,8},{16,12},{20,16},{24,20},{28,24},{0,28},{5,1},{9... | collective-permute-start | bytes 995336 | tf_op jit(solution)/shard_map/ppermute | solution.py:346
  159.8 8.5 %collective-permute-start.22 = (f32[9,8,128]{2,1,0:T(8,128)S(1)}, f32[9,8,128]{2,1,0:T(8,128)S(1)}, u32[]{:S(2)}, u32[]{:S(2)}) collective-permute-start(f32[9,8,128]{2,1,0:T(8,128)S(1)} %get-tuple-element.71), channel_id=1, source_target_pairs={{0,1},{1,2},{2,3},{4,5},{5,6},{6,7},{8,9},{9,10},{10,11},{12,13},{... | collective-permute-start | bytes 110600 | tf_op jit(solution)/shard_map/ppermute | solution.py:347
  168.4 29.1 %collective-permute-start.13 = (f32[8,9,8,128]{3,2,1,0:T(8,128)S(1)}, f32[8,9,8,128]{3,2,1,0:T(8,128)S(1)}, u32[]{:S(2)}, u32[]{:S(2)}) collective-permute-start(f32[8,9,8,128]{3,2,1,0:T(8,128)S(1)} %get-tuple-element.60), channel_id=1, source_target_pairs={{4,0},{8,4},{12,8},{16,12},{20,16},{24,20},{28,24},{0,28},{5,1},{9... | collective-permute-start | bytes 884744 | tf_op jit(solution)/shard_map/ppermute | solution.py:346
  169.6 30.8 %collective-permute-start.4 = (f32[8,9,8,128]{3,2,1,0:T(8,128)S(1)}, f32[8,9,8,128]{3,2,1,0:T(8,128)S(1)}, u32[]{:S(2)}, u32[]{:S(2)}) collective-permute-start(f32[8,9,8,128]{3,2,1,0:T(8,128)S(1)} %get-tuple-element.49), channel_id=1, source_target_pairs={{0,4},{4,8},{8,12},{12,16},{16,20},{20,24},{24,28},{28,0},{1,5},{5... | collective-permute-start | bytes 884744 | tf_op jit(solution)/shard_map/ppermute | solution.py:345
  172.6 27.8 %collective-permute-start.5 = (f32[8,9,8,128]{3,2,1,0:T(8,128)S(1)}, f32[8,9,8,128]{3,2,1,0:T(8,128)S(1)}, u32[]{:S(2)}, u32[]{:S(2)}) collective-permute-start(f32[8,9,8,128]{3,2,1,0:T(8,128)S(1)} %get-tuple-element.50), channel_id=1, source_target_pairs={{4,0},{8,4},{12,8},{16,12},{20,16},{24,20},{28,24},{0,28},{5,1},{9... | collective-permute-start | bytes 884744 | tf_op jit(solution)/shard_map/ppermute | solution.py:346
  188.0 12.4 %collective-permute-start.6 = (f32[8,8,128]{2,1,0:T(8,128)S(1)}, f32[8,8,128]{2,1,0:T(8,128)S(1)}, u32[]{:S(2)}, u32[]{:S(2)}) collective-permute-start(f32[8,8,128]{2,1,0:T(8,128)S(1)} %get-tuple-element.51), channel_id=1, source_target_pairs={{0,1},{1,2},{2,3},{4,5},{5,6},{6,7},{8,9},{9,10},{10,11},{12,13},{... | collective-permute-start | bytes 98312 | tf_op jit(solution)/shard_map/ppermute | solution.py:347
  192.5 7.9 %collective-permute-start.7 = (f32[8,8,128]{2,1,0:T(8,128)S(1)}, f32[8,8,128]{2,1,0:T(8,128)S(1)}, u32[]{:S(2)}, u32[]{:S(2)}) collective-permute-start(f32[8,8,128]{2,1,0:T(8,128)S(1)} %get-tuple-element.52), channel_id=1, source_target_pairs={{1,0},{2,1},{3,2},{5,4},{6,5},{7,6},{9,8},{10,9},{11,10},{13,12},{... | collective-permute-start | bytes 98312 | tf_op jit(solution)/shard_map/ppermute | solution.py:348
  (24 other events, 270.8 us)

commit v2 on v1

--- a/solution.py
+++ b/solution.py
@@ -11,7 +11,6 @@
 
 F32 = jnp.float32
 BF16 = jnp.bfloat16
-NSUB = 2
 LANES = 128
 SUB = 8
 CHUNKS = (9, 8, 8)
@@ -85,7 +84,7 @@
     return both[:total] + both[total:]
 
 
-def send_rows(plan, pair_ref, target, out_ref):
+def send_rows(plan, pair_ref, target, out_ref, done=None):
     slots = pair_ref.shape[1]
     groups = NBLOCK // LANES
     for block in range(slots // NBLOCK):
@@ -97,6 +96,8 @@
             ]
             for i, message in enumerate(swap_blocks(blocks, plan.cap)):
                 out_ref[(block * groups + g) * plan.parts + i] = message
+        if done is not None:
+            done(block)
 
 
 def source_rows(plan, spectra_ref, first, count, nfreq, gain, x_ref):
@@ -108,25 +109,32 @@
             x_ref[row : row + length, :] = rows[offset : offset + length]
 
 
+PIECES = 5
+
+
 def first_source_kernel(
-    plan, count, shape, spectra_ref, growth_ref, dir_ref, cell_ref,
-    out_ref, gain_ref, target_ref, x_ref, pair_ref,
+    plan, count, shape, spectra_hbm, growth_hbm, dir_hbm, cell_hbm,
+    out_hbm, gain_ref, target_ref,
+    spectra_ref, growth_ref, dir_ref, cell_ref, x_ref, pair_ref, message_ref, sems, out_sems,
 ):
     rows_x, rows_y, lat_count, devices = shape
     nfreq, ndir, slots = spectra_ref.shape
-    dtheta = 2.0 * math.pi / ndir
-    total = None
-    for f in range(nfreq):
-        width = float(np.float32(0.1) * np.float32(1.1) ** np.float32(f)) * dtheta
-        term = spectra_ref[f] * width
-        total = term if total is None else total + term
-    energy = jnp.sum(total, axis=0, keepdims=True)
-    load = energy / (energy + 10.0)
-    theta = (lax.broadcasted_iota(jnp.int32, (ndir, slots), 0).astype(F32) + 0.5) * dtheta
-    lobe = jnp.maximum(jnp.cos(theta - dir_ref[...]), 0.0)
-    gain = growth_ref[...] * (lobe * lobe) - 0.4 * load
-    gain_ref[...] = gain
-
+    bounds = [nfreq * k // PIECES for k in range(PIECES + 1)]
+    small = [
+        pltpu.make_async_copy(src, dst, sems.at[PIECES + k])
+        for k, (src, dst) in enumerate(
+            ((cell_hbm, cell_ref), (growth_hbm, growth_ref), (dir_hbm, dir_ref))
+        )
+    ]
+    pieces = [
+        pltpu.make_async_copy(
+            spectra_hbm.at[pl.ds(lo, hi - lo)], spectra_ref.at[pl.ds(lo, hi - lo)], sems.at[k]
+        )
+        for k, (lo, hi) in enumerate(zip(bounds, bounds[1:]))
+    ]
+    for copy in small + pieces:
+        copy.start()
+    small[0].wait()
     point = cell_ref[...]
     valid = point >= 0
     col_x, col_y = divide(jnp.maximum(point, 0), rows_y * lat_count)
@@ -152,10 +160,39 @@
     target = jnp.where(valid, owner * plan.cap + place, slots)
     target_ref[...] = target
 
+    small[1].wait()
+    small[2].wait()
+    dtheta = 2.0 * math.pi / ndir
+    total = None
+    for k, copy in enumerate(pieces):
+        copy.wait()
+        for f in range(bounds[k], bounds[k + 1]):
+            width = float(np.float32(0.1) * np.float32(1.1) ** np.float32(f)) * dtheta
+            term = spectra_ref[f] * width
+            total = term if total is None else total + term
+    energy = jnp.sum(total, axis=0, keepdims=True)
+    load = energy / (energy + 10.0)
+    theta = (lax.broadcasted_iota(jnp.int32, (ndir, slots), 0).astype(F32) + 0.5) * dtheta
+    lobe = jnp.maximum(jnp.cos(theta - dir_ref[...]), 0.0)
+    gain = growth_ref[...] * (lobe * lobe) - 0.4 * load
+    gain_ref[...] = gain
+
     source_rows(plan, spectra_ref, 0, count, nfreq, gain, x_ref)
     x_ref[plan.label_row : plan.label_row + 1, :] = label
     split_rows(x_ref, pair_ref)
-    send_rows(plan, pair_ref, target, out_ref)
+    copies = []
+
+    def sent(block):
+        per = devices * NBLOCK // slots
+        part = pl.ds(block * per, per)
+        copies.append(
+            pltpu.make_async_copy(message_ref.at[part], out_hbm.at[part], out_sems.at[block])
+        )
+        copies[-1].start()
+
+    send_rows(plan, pair_ref, target, message_ref, sent)
+    for copy in copies:
+        copy.wait()
 
 
 def later_source_kernel(
@@ -179,7 +216,7 @@
     )
 
 
-def edge_messages(read, weight, f, ndir, right_ref, left_ref, up_ref, down_ref):
+def edge_messages(read, weight, odd_lon, f, ndir, pair_ref, cross_ref, side_ref):
     row, lane = tile_ids()
     odd = (row & 1) == 1
     quarter = ndir // 4
@@ -188,24 +225,26 @@
     moved = [read(d) * weight for d in range(ndir)]
     for e in range(quarter):
         a, b = moved[3 * quarter + e], moved[e]
-        right_ref[f, e] = jnp.where(odd, b, pltpu.roll(a, SUB - 1, 0))
+        right = jnp.where(odd, b, pltpu.roll(a, SUB - 1, 0))
         a, b = moved[quarter + e], moved[2 * quarter + e]
-        left_ref[f, e] = jnp.where(odd, pltpu.roll(b, 1, 0), a)
+        left = jnp.where(odd, pltpu.roll(b, 1, 0), a)
+        pair_ref[f, e] = jnp.where(odd_lon, left, right)
+        cross_ref[f, e] = jnp.where(odd_lon, right, left)
     for k in range(2 * quarter):
         up = jnp.where(lane == k, pltpu.roll(moved[k], k + 1, 1), up)
         low = moved[2 * quarter + k]
         down = jnp.where(lane == k, pltpu.roll(low, k, 1) if k else low, down)
-    up_ref[f] = up
-    down_ref[f] = down
+    side_ref[f] = jnp.where(row >= SUB // 2, up, down)
 
 
 def place_kernel(plan, first, count, ndir, with_labels, *refs):
     if with_labels:
-        in_ref, speed_ref, shoal_ref, *refs = refs
-        own_ref, right_ref, left_ref, up_ref, down_ref, label_ref, x_ref, pair_ref = refs
+        in_ref, speed_ref, ids_ref, shoal_ref, *refs = refs
+        own_ref, right_ref, left_ref, side_ref, label_ref, x_ref, pair_ref = refs
     else:
-        in_ref, speed_ref, shoal_ref, label_ref, *refs = refs
-        own_ref, right_ref, left_ref, up_ref, down_ref, x_ref, pair_ref = refs
+        in_ref, speed_ref, ids_ref, shoal_ref, label_ref, *refs = refs
+        refs = refs[-6:]
+        own_ref, right_ref, left_ref, side_ref, x_ref, pair_ref = refs
     slots = x_ref.shape[1]
     for g in range(slots // LANES):
         blocks = [in_ref[g * plan.parts + i] for i in range(plan.parts)]
@@ -233,18 +272,17 @@
             return own_ref[pl.ds(pl.multiple_of((f * ndir + d) * SUB, SUB), SUB), :]
 
         edge_messages(
-            read, shoal * speed_ref[first + f], f, ndir, right_ref, left_ref, up_ref, down_ref
+            read, shoal * speed_ref[first + f], ids_ref[4] == 1, f, ndir, right_ref, left_ref, side_ref
         )
 
 
-def step_kernel(first, last, *refs):
-    (own_ref, right_in, left_in, up_in, down_in, speed_ref,
+def step_kernel(first, side_first, last, *refs):
+    (own_ref, pair_in, cross_in, side_in, speed_ref, lat_ref,
      shoal_ref, slope_x_ref, slope_y_ref, mask_ref, *refs) = refs
     if last:
-        *refs, new_ref, turn_ref, done_sem = refs
-        out_ref = refs[-1]
+        out_ref, new_ref, turn_ref, done_sem = refs[-4:]
     else:
-        new_ref, right_ref, left_ref, up_ref, down_ref, turn_ref = refs
+        new_ref, right_ref, left_ref, side_ref, turn_ref = refs
     count, ndir = own_ref.shape[:2]
     quarter = ndir // 4
     row, lane = tile_ids()
@@ -259,23 +297,27 @@
     for d in range(ndir):
         turn_ref[d] = sin[d] * slope_x - cos[d] * slope_y
 
+    odd_lon = lat_ref[4] == 1
+    keep_up = lat_ref[2].astype(F32)
+    keep_down = lat_ref[3].astype(F32)
+
     @pl.loop(0, count)
     def advance(f):
         speed = speed_ref[first + f]
         weight = shoal * speed
-        up_all = up_in[f]
-        down_all = down_in[f]
+        up_all = side_in[lat_ref[0], side_first + f] * keep_up
+        down_all = side_in[lat_ref[1], side_first + f] * keep_down
 
         def halved(d):
             field = own_ref[f, d]
             moved = weight * field
             if d >= 3 * quarter or d < quarter:
-                edge = right_in[f, d % quarter]
+                edge = jnp.where(odd_lon, pair_in[f, d % quarter], cross_in[f, d % quarter])
                 if d < quarter:
                     edge = pltpu.roll(edge, SUB - 1, 0)
                 from_x = jnp.where(odd, pltpu.roll(moved, 1, 0), edge)
             else:
-                edge = left_in[f, d % quarter]
+                edge = jnp.where(odd_lon, cross_in[f, d % quarter], pair_in[f, d % quarter])
                 if d < 2 * quarter:
                     edge = pltpu.roll(edge, 1, 0)
                 from_x = jnp.where(odd, edge, pltpu.roll(moved, SUB - 1, 0))
@@ -310,7 +352,7 @@
             half, qt, below = half_next, qt_next, above
         if not last:
             edge_messages(
-                lambda d: new_ref[f, d], weight, f, ndir, right_ref, left_ref, up_ref, down_ref
+                lambda d: new_ref[f, d], weight, odd_lon, f, ndir, right_ref, left_ref, side_ref
             )
 
     if last:
@@ -329,23 +371,20 @@
 
 SMEM_SPEC = pl.BlockSpec(memory_space=pltpu.SMEM)
 ANY_SPEC = pl.BlockSpec(memory_space=pl.ANY)
+HBM_SPEC = pl.BlockSpec(memory_space=pltpu.HBM)
 
 
 def edge_shapes(count, ndir):
     tile = jax.ShapeDtypeStruct((count, ndir // 4, SUB, LANES), F32)
     line = jax.ShapeDtypeStruct((count, SUB, LANES), F32)
-    return [tile, tile, line, line]
-
-
-def send_edges(edges):
-    right, left, up, down = edges
+    return [tile, tile, line]
+
+
+def send_edges(pair, cross):
     lon = lax.axis_size("lon")
-    lat = lax.axis_size("lat")
     return (
-        lax.ppermute(right, "lon", [(i, (i + 1) % lon) for i in range(lon)]),
-        lax.ppermute(left, "lon", [((i + 1) % lon, i) for i in range(lon)]),
-        lax.ppermute(up, "lat", [(i, i + 1) for i in range(lat - 1)]),
-        lax.ppermute(down, "lat", [(i + 1, i) for i in range(lat - 1)]),
+        lax.ppermute(pair, "lon", [(i, i ^ 1) for i in range(lon)]),
+        lax.ppermute(cross, "lon", [(i, (i + 2 * (i & 1) - 1) % lon) for i in range(lon)]),
     )
 
 
@@ -376,10 +415,19 @@
                     jax.ShapeDtypeStruct((ndir, slots), F32),
                     jax.ShapeDtypeStruct((1, slots), jnp.int32),
                 ],
-                in_specs=vmem(4),
-                out_specs=vmem(3),
-                scratch_shapes=scratch,
-                compiler_params=params(),
+                in_specs=[HBM_SPEC] * 4,
+                out_specs=[HBM_SPEC] + vmem(2),
+                scratch_shapes=[
+                    pltpu.VMEM(spectra.shape, F32),
+                    pltpu.VMEM((1, slots), F32),
+                    pltpu.VMEM((1, slots), F32),
+                    pltpu.VMEM((1, slots), jnp.int32),
+                    *scratch,
+                    pltpu.VMEM(shape.shape, F32),
+                    pltpu.SemaphoreType.DMA((PIECES + 3,)),
+                    pltpu.SemaphoreType.DMA((slots // NBLOCK,)),
+                ],
+                compiler_params=pltpu.CompilerParams(vmem_limit_bytes=60 * 2**20),
                 name="source_first",
             )(
                 spectra,
@@ -401,59 +449,104 @@
             )(spectra, gain, target)
         messages.append(message)
 
+    whole = jax.ShapeDtypeStruct((nfreq, ndir, SUB, LANES), F32)
+    grids = (shoaling, slope_x, slope_y, land_mask)
+    lat = lax.axis_index("lat")
+    lat_ids = jnp.stack(
+        [
+            jnp.maximum(lat - 1, 0),
+            jnp.minimum(lat + 1, lat_count - 1),
+            (lat > 0).astype(jnp.int32),
+            (lat < lat_count - 1).astype(jnp.int32),
+            lax.axis_index("lon") & 1,
+        ]
+    )
+    label = None
     out = None
-    label = None
-    for i, (first, count, plan) in enumerate(zip(starts, CHUNKS, plans)):
-        arrived = lax.all_to_all(
-            messages[i], ("lon", "lat"), split_axis=0, concat_axis=0, tiled=True
-        )
-        edges = edge_shapes(count, ndir)
-        own_shape = jax.ShapeDtypeStruct((count * ndir * SUB, LANES), F32)
-        label_shape = jax.ShapeDtypeStruct((1, slots), jnp.int32)
-        placed = pl.pallas_call(
+
+    def place(i, arrived, after=()):
+        first, count, plan = starts[i], CHUNKS[i], plans[i]
+        outs = [jax.ShapeDtypeStruct((count * ndir * SUB, LANES), F32)] + edge_shapes(count, ndir)
+        if i == 0:
+            outs.append(jax.ShapeDtypeStruct((1, slots), jnp.int32))
+        field, *sent = pl.pallas_call(
             functools.partial(place_kernel, plan, first, count, ndir, i == 0),
-            out_shape=[own_shape] + edges + ([label_shape] if i == 0 else []),
-            in_specs=vmem(1) + [SMEM_SPEC] + vmem(1 if i == 0 else 2),
-            out_specs=vmem(6 if i == 0 else 5),
+            out_shape=outs,
+            in_specs=vmem(1) + [SMEM_SPEC, SMEM_SPEC] + vmem(1 if i == 0 else 2) + [ANY_SPEC] * len(after),
+            out_specs=vmem(len(outs)),
             scratch_shapes=[
                 pltpu.VMEM((plan.total, slots), F32),
                 pltpu.VMEM((2 * plan.total, slots), BF16),
             ],
             compiler_params=params(),
             name="place",
-        )(arrived, speed, shoaling, *([] if i == 0 else [label]))
+        )(arrived, speed, lat_ids, shoaling, *([] if i == 0 else [label]), *after)
+        return field.reshape(count, ndir, SUB, LANES), sent
+
+    def step(i, field, received, side_first):
+        same = jax.ShapeDtypeStruct(field.shape, F32)
+        field, *sent = pl.pallas_call(
+            functools.partial(step_kernel, starts[i], side_first, False),
+            out_shape=[same] + edge_shapes(CHUNKS[i], ndir),
+            in_specs=vmem(4) + [SMEM_SPEC, SMEM_SPEC] + vmem(4),
+            out_specs=vmem(4),
+            scratch_shapes=[pltpu.VMEM((ndir, SUB, LANES), F32)],
+            compiler_params=params(),
+            name="step",
+        )(field, *received, speed, lat_ids, *grids)
+        return field, sent
+
+    def last_step(i, field, received, side_first, out, after=()):
+        chained = out is not None
+        return pl.pallas_call(
+            functools.partial(step_kernel, starts[i], side_first, True),
+            out_shape=whole,
+            in_specs=vmem(4) + [SMEM_SPEC, SMEM_SPEC] + vmem(4) + [ANY_SPEC] * (len(after) + chained),
+            out_specs=ANY_SPEC,
+            scratch_shapes=[
+                pltpu.VMEM(field.shape, F32),
+                pltpu.VMEM((ndir, SUB, LANES), F32),
+                pltpu.SemaphoreType.DMA(()),
+            ],
+            input_output_aliases={10: 0} if chained else {},
+            compiler_params=params(),
+            name="last_step",
+        )(field, *received, speed, lat_ids, *grids, *([out] if chained else []), *after)
+
+    n = len(CHUNKS)
+    tie = lax.optimization_barrier
+    waiting = None
+    for i in range(n):
+        arrived = lax.all_to_all(
+            messages[i], ("lon", "lat"), split_axis=0, concat_axis=0, tiled=True
+        )
+        if i + 1 < n:
+            arrived, messages[i + 1] = tie((arrived, messages[i + 1]))
+        if i >= 2:
+            arrived, out = tie((arrived, out))
+        after = (waiting[2],) if i >= 2 else ()
+        field, sent = place(i, arrived, after)
         if i == 0:
-            *placed, label = placed
-        field, *sent = placed
-        field = field.reshape(count, ndir, SUB, LANES)
-        for step in range(NSUB):
-            last = step == NSUB - 1
-            received = send_edges(sent)
-            whole = jax.ShapeDtypeStruct((nfreq, ndir, SUB, LANES), F32)
-            same = jax.ShapeDtypeStruct(field.shape, F32)
-            tables = [pltpu.VMEM((ndir, SUB, LANES), F32)]
-            chained = last and out is not None
-            result = pl.pallas_call(
-                functools.partial(step_kernel, first, last),
-                out_shape=whole if last else [same] + edges,
-                in_specs=vmem(5) + [SMEM_SPEC] + vmem(4) + ([ANY_SPEC] if chained else []),
-                out_specs=ANY_SPEC if last else vmem(5),
-                scratch_shapes=(
-                    [pltpu.VMEM(field.shape, F32)] + tables + [pltpu.SemaphoreType.DMA(())]
-                    if last
-                    else tables
-                ),
-                input_output_aliases={10: 0} if chained else {},
-                compiler_params=params(),
-                name="last_step" if last else "step",
-            )(
-                field, *received, speed, shoaling, slope_x, slope_y, land_mask,
-                *([out] if chained else []),
-            )
-            if last:
-                out = result
+            *sent, label = sent
+        received = send_edges(*sent[:2])
+        if waiting is None:
+            sides = lax.all_gather(sent[2], "lat")
+            side_first = 0
+        else:
+            sides = lax.all_gather(jnp.concatenate([waiting[2], sent[2]], axis=0), "lat")
+            side_first = CHUNKS[i - 1]
+            if i < n - 1:
+                out = last_step(i - 1, waiting[0], (*waiting[1], sides), 0, out)
             else:
-                field, *sent = result
+                pending = (i - 1, waiting[0], (*waiting[1], sides), 0, out)
+        field, sent = step(i, field, (*received, sides), side_first)
+        if i + 2 < n:
+            *sent, messages[i + 2] = tie((*sent, messages[i + 2]))
+        waiting = (field, send_edges(*sent[:2]), sent[2])
+    field, received, side = waiting
+    sides = lax.all_gather(side, "lat")
+    out = last_step(*pending, (sides,))
+    out = last_step(n - 1, field, (*received, sides), 0, out)
     bands = rows_y // LANES
     out = out.reshape(nfreq, ndir, bands, rows_x, LANES)
     return out.transpose(0, 1, 3, 2, 4).reshape(nfreq, ndir, rows_x, rows_y)

time: 204 us -> 187 us (0.917)
  the two profiles are of different devices: /device:TPU:29 before, /device:TPU:0 now
where the time goes in v2:
time: 187 us; the launch traced here: 186 us
  waiting for transfers between devices  76.5 us (41%)
  starting transfers between devices  42.1 us (23%)
  Pallas kernels  36.8 us (20%)
  blocking collectives  23.9 us (13%)
  local copies, waits for them, and re-layouts  6.51 us (3%)
    ppermute x6, waiting for transfers between devices, send_edges(): lax.ppermute(pair, 'lon', [(i, i ^ 1) for i in range(lon)])  37.7 us
    all_to_all x3, waiting for transfers between devices, on_device(): lax.all_to_all(messages[i], ('lon', 'lat'), split_axis=0, concat_axis=0,...  30.1 us
    ppermute x6, starting transfers between devices, send_edges(): lax.ppermute(cross, 'lon', [(i, (i + 2 * (i & 1) - 1) % lon) for i in ran...  19.4 us
    all_to_all x3, starting transfers between devices, on_device(): lax.all_to_all(messages[i], ('lon', 'lat'), split_axis=0, concat_axis=0,...  18.1 us
    all_gather x2, blocking collectives, on_device(): lax.all_gather(jnp.concatenate([waiting[2], sent[2]], axis=0), 'lat')  13.1 us
    pallas_call x3, Pallas kernels, place(): pl.pallas_call(functools.partial(place_kernel, plan, first, count, ndir,...  9.66 us
    pallas_call x3, Pallas kernels, last_step(): pl.pallas_call(functools.partial(step_kernel, starts[i], side_first, True...  8.81 us
    ppermute x6, waiting for transfers between devices, send_edges(): lax.ppermute(cross, 'lon', [(i, (i + 2 * (i & 1) - 1) % lon) for i in ran...  8.73 us
  transfers between devices with their start and end apart: 15, of which 8 were waited for; matrix products, arithmetic and copies ran while one was open for 0% of the time, Pallas kernels for 13%

profile of v2, /device:TPU:0, one launch (start us, length us, event | category | flops | bytes accessed | tf_op | source)
XLA Modules:
  0.0 186.3 jit_solution(3452127241614384015)
XLA Ops:
  0.0 6.4 %source_first.1 = (f32[32,88,128]{2,1,0:T(8,128)}, f32[36,1024]{1,0:T(8,128)}, s32[1,1024]{1,0:T(1,128)}) custom-call(f32[25,36,1024]{2,1,0:T(8,128)} %spectra_ref.3, f32[1,1024]{1,0:T(1,128)} %bitcast.30, f32[1,1024]{1,0:T(1,128)} %bitcast.31, s32[1,1024]{1,0:T(1,128)} %bitcast.32), custom_call_target="tpu_custom_call" | custom-call | tf_op jit(solution)/shard_map/source_first/pallas_call | solution.py:409
  6.4 7.3 %all-to-all-start = ((f32[32,88,128]{2,1,0:T(8,128)}), f32[32,88,128]{2,1,0:T(8,128)S(1)}, u32[]{:S(2)}, u32[]{:S(2)}) async-start(f32[32,88,128]{2,1,0:T(8,128)} %get-tuple-element.43), calls=%async_computation | async-start | bytes 2883584 | tf_op jit(solution)/shard_map/all_to_all | solution.py:520
  18.6 30.1 %all-to-all-done.refs_0_ = f32[32,88,128]{2,1,0:T(8,128)S(1)} async-done(((f32[32,88,128]{2,1,0:T(8,128)}), f32[32,88,128]{2,1,0:T(8,128)S(1)}, u32[]{:S(2)}, u32[]{:S(2)}) %all-to-all-start) | async-done | bytes 1441824 | tf_op jit(solution)/shard_map/all_to_all | solution.py:520
  48.7 3.6 %all-to-all-start.1 = ((f32[32,72,128]{2,1,0:T(8,128)}), f32[32,72,128]{2,1,0:T(8,128)S(1)}, u32[]{:S(2)}, u32[]{:S(2)}) async-start(f32[32,72,128]{2,1,0:T(8,128)} %copy-done.2), calls=%async_computation.1 | async-start | bytes 2359296 | tf_op jit(solution)/shard_map/all_to_all | solution.py:520
  52.4 3.4 %place.3 = (f32[2592,128]{1,0:T(8,128)S(1)}, f32[9,9,8,128]{3,2,1,0:T(8,128)S(1)}, f32[9,9,8,128]{3,2,1,0:T(8,128)S(1)}, f32[9,8,128]{2,1,0:T(8,128)S(1)}, s32[1,1024]{1,0:T(1,128)S(1)}) custom-call(f32[32,88,128]{2,1,0:T(8,128)S(1)} %all-to-all-done.refs_0_, f32[25]{0:T(128)S(1)} %copy-done.10, s32[5]{0:T(128)S(1)} %stack.31.refs_2_.refs_5_, ...), custom_call_target="tpu_custom_call" | custom-call | tf_op jit(solution)/shard_map/place/pallas_call | solution.py:472
  57.7 3.3 %collective-permute-start.1 = (f32[9,9,8,128]{3,2,1,0:T(8,128)S(1)}, f32[9,9,8,128]{3,2,1,0:T(8,128)S(1)}, u32[]{:S(2)}, u32[]{:S(2)}) collective-permute-start(f32[9,9,8,128]{3,2,1,0:T(8,128)S(1)} %get-tuple-element.50), channel_id=1, source_target_pairs={{0,28},{4,8},{8,4},{12,16},{16,12},{20,24},{24,20},{28,0},{1,29},{... | collective-permute-start | bytes 995336 | tf_op jit(solution)/shard_map/ppermute | solution.py:387
  66.0 5.5 %all-gather = f32[36,8,128]{2,1,0:T(8,128)S(1)} all-gather(f32[9,8,128]{2,1,0:T(8,128)S(1)} %get-tuple-element.51), channel_id=2, replica_groups=mesh['lon'=8,'lat'=4] {'lat'}, dimensions={0}, use_global_device_ids=true | all-gather | bytes 184320 | tf_op jit(solution)/shard_map/all_gather | solution.py:533
  71.4 8.6 %collective-permute-done.refs_1_ = f32[9,9,8,128]{3,2,1,0:T(8,128)S(1)} collective-permute-done((f32[9,9,8,128]{3,2,1,0:T(8,128)S(1)}, f32[9,9,8,128]{3,2,1,0:T(8,128)S(1)}, u32[]{:S(2)}, u32[]{:S(2)}) %collective-permute-start) | collective-permute-done | bytes 331808 | tf_op jit(solution)/shard_map/ppermute | solution.py:386
  80.0 4.2 %collective-permute-done.1.refs_2_ = f32[9,9,8,128]{3,2,1,0:T(8,128)S(1)} collective-permute-done((f32[9,9,8,128]{3,2,1,0:T(8,128)S(1)}, f32[9,9,8,128]{3,2,1,0:T(8,128)S(1)}, u32[]{:S(2)}, u32[]{:S(2)}) %collective-permute-start.1) | collective-permute-done | bytes 331808 | tf_op jit(solution)/shard_map/ppermute | solution.py:387
  87.9 7.2 %all-to-all-start.2 = ((f32[32,72,128]{2,1,0:T(8,128)}), f32[32,72,128]{2,1,0:T(8,128)S(1)}, u32[]{:S(2)}, u32[]{:S(2)}) async-start(f32[32,72,128]{2,1,0:T(8,128)} %source_later.3), calls=%async_computation.2 | async-start | bytes 2359296 | tf_op jit(solution)/shard_map/all_to_all | solution.py:520
  96.9 3.3 %collective-permute-start.3 = (f32[9,9,8,128]{3,2,1,0:T(8,128)S(1)}, f32[9,9,8,128]{3,2,1,0:T(8,128)S(1)}, u32[]{:S(2)}, u32[]{:S(2)}) collective-permute-start(f32[9,9,8,128]{3,2,1,0:T(8,128)S(1)} %get-tuple-element.59), channel_id=1, source_target_pairs={{0,28},{4,8},{8,4},{12,16},{16,12},{20,24},{24,20},{28,0},{1,29},{... | collective-permute-start | bytes 995336 | tf_op jit(solution)/shard_map/ppermute | solution.py:387
  100.3 3.1 %place.4 = (f32[2304,128]{1,0:T(8,128)S(1)}, f32[8,9,8,128]{3,2,1,0:T(8,128)S(1)}, f32[8,9,8,128]{3,2,1,0:T(8,128)S(1)}, f32[8,8,128]{2,1,0:T(8,128)S(1)}) custom-call(f32[32,72,128]{2,1,0:T(8,128)S(1)} %all-to-all-done.1.refs_0_, f32[25]{0:T(128)S(1)} %copy-done.10, s32[5]{0:T(128)S(1)} %stack.31.refs_2_.refs_5_, f32[2,512]{1,0:T(2,128)S(1)} %copy-done.6, ...), custom_call_target="tpu_custom_call" | custom-call | tf_op jit(solution)/shard_map/place/pallas_call | solution.py:472
  105.4 7.3 %all-gather.1 = f32[68,8,128]{2,1,0:T(8,128)S(1)} all-gather(f32[17,8,128]{2,1,0:T(8,128)S(1)} %pad_maximum_fusion), channel_id=3, replica_groups=mesh['lon'=8,'lat'=4] {'lat'}, dimensions={0}, use_global_device_ids=true | all-gather | bytes 348160 | tf_op jit(solution)/shard_map/all_gather | solution.py:536
  112.7 10.2 %collective-permute-done.2.refs_1_ = f32[9,9,8,128]{3,2,1,0:T(8,128)S(1)} collective-permute-done((f32[9,9,8,128]{3,2,1,0:T(8,128)S(1)}, f32[9,9,8,128]{3,2,1,0:T(8,128)S(1)}, u32[]{:S(2)}, u32[]{:S(2)}) %collective-permute-start.2) | collective-permute-done | bytes 331808 | tf_op jit(solution)/shard_map/ppermute | solution.py:386
  122.9 4.6 %collective-permute-done.3.refs_2_ = f32[9,9,8,128]{3,2,1,0:T(8,128)S(1)} collective-permute-done((f32[9,9,8,128]{3,2,1,0:T(8,128)S(1)}, f32[9,9,8,128]{3,2,1,0:T(8,128)S(1)}, u32[]{:S(2)}, u32[]{:S(2)}) %collective-permute-start.3) | collective-permute-done | bytes 331808 | tf_op jit(solution)/shard_map/ppermute | solution.py:387
  127.5 3.1 %last_step.3.refs_10_ = f32[25,36,8,128]{3,2,1,0:T(8,128)} custom-call(f32[9,36,8,128]{3,2,1,0:T(8,128)S(1)} %copy-done.4, f32[9,9,8,128]{3,2,1,0:T(8,128)S(1)} %collective-permute-done.2.refs_1_, f32[9,9,8,128]{3,2,1,0:T(8,128)S(1)} %collective-permute-done.3.refs_2_, f32[4,17,8,128]{3,2,1,0:T(8,128)S(1)} %bitcast.20, f32[25]{0:T(128)S(1)} %copy-done.10, ...), custom_call_target="tpu_custom_call" | custom-call | tf_op jit(solution)/shard_map/last_step/pallas_call | solution.py:501
  130.6 6.9 %collective-permute-done.4.refs_1_ = f32[8,9,8,128]{3,2,1,0:T(8,128)S(1)} collective-permute-done((f32[8,9,8,128]{3,2,1,0:T(8,128)S(1)}, f32[8,9,8,128]{3,2,1,0:T(8,128)S(1)}, u32[]{:S(2)}, u32[]{:S(2)}) %collective-permute-start.4) | collective-permute-done | bytes 294944 | tf_op jit(solution)/shard_map/ppermute | solution.py:386
  139.9 3.1 %place.5 = (f32[2304,128]{1,0:T(8,128)S(1)}, f32[8,9,8,128]{3,2,1,0:T(8,128)S(1)}, f32[8,9,8,128]{3,2,1,0:T(8,128)S(1)}, f32[8,8,128]{2,1,0:T(8,128)S(1)}) custom-call(f32[32,72,128]{2,1,0:T(8,128)S(1)} %all-to-all-done.2.refs_0_, f32[25]{0:T(128)S(1)} %copy-done.10, s32[5]{0:T(128)S(1)} %stack.31.refs_2_.refs_5_, f32[2,512]{1,0:T(2,128)S(1)} %copy-done.6, ...), custom_call_target="tpu_custom_call" | custom-call | tf_op jit(solution)/shard_map/place/pallas_call | solution.py:472
  143.5 4.4 %collective-permute-start.7 = (f32[8,9,8,128]{3,2,1,0:T(8,128)S(1)}, f32[8,9,8,128]{3,2,1,0:T(8,128)S(1)}, u32[]{:S(2)}, u32[]{:S(2)}) collective-permute-start(f32[8,9,8,128]{3,2,1,0:T(8,128)S(1)} %get-tuple-element.71), channel_id=1, source_target_pairs={{0,28},{4,8},{8,4},{12,16},{16,12},{20,24},{24,20},{28,0},{1,29},{... | collective-permute-start | bytes 884744 | tf_op jit(solution)/shard_map/ppermute | solution.py:387
  149.9 5.8 %all-gather.2 = f32[64,8,128]{2,1,0:T(8,128)S(1)} all-gather(f32[16,8,128]{2,1,0:T(8,128)S(1)} %pad_maximum_fusion.1), channel_id=4, replica_groups=mesh['lon'=8,'lat'=4] {'lat'}, dimensions={0}, use_global_device_ids=true | all-gather | bytes 327680 | tf_op jit(solution)/shard_map/all_gather | solution.py:536
  155.6 10.0 %collective-permute-done.6.refs_1_ = f32[8,9,8,128]{3,2,1,0:T(8,128)S(1)} collective-permute-done((f32[8,9,8,128]{3,2,1,0:T(8,128)S(1)}, f32[8,9,8,128]{3,2,1,0:T(8,128)S(1)}, u32[]{:S(2)}, u32[]{:S(2)}) %collective-permute-start.6) | collective-permute-done | bytes 294944 | tf_op jit(solution)/shard_map/ppermute | solution.py:386
  168.5 4.5 %collective-permute-start.9 = (f32[8,9,8,128]{3,2,1,0:T(8,128)S(1)}, f32[8,9,8,128]{3,2,1,0:T(8,128)S(1)}, u32[]{:S(2)}, u32[]{:S(2)}) collective-permute-start(f32[8,9,8,128]{3,2,1,0:T(8,128)S(1)} %get-tuple-element.75), channel_id=1, source_target_pairs={{0,28},{4,8},{8,4},{12,16},{16,12},{20,24},{24,20},{28,0},{1,29},{... | collective-permute-start | bytes 884744 | tf_op jit(solution)/shard_map/ppermute | solution.py:387
  173.0 5.4 %all-gather.3 = f32[32,8,128]{2,1,0:T(8,128)S(1)} all-gather(f32[8,8,128]{2,1,0:T(8,128)S(1)} %get-tuple-element.76), channel_id=5, replica_groups=mesh['lon'=8,'lat'=4] {'lat'}, dimensions={0}, use_global_device_ids=true | all-gather | bytes 163840 | tf_op jit(solution)/shard_map/all_gather | solution.py:547
  178.4 2.9 %last_step.4.refs_10_ = f32[25,36,8,128]{3,2,1,0:T(8,128)} custom-call(f32[8,36,8,128]{3,2,1,0:T(8,128)S(1)} %get-tuple-element.77.refs_0_, f32[8,9,8,128]{3,2,1,0:T(8,128)S(1)} %collective-permute-done.10.refs_1_, f32[8,9,8,128]{3,2,1,0:T(8,128)S(1)} %collective-permute-done.11.refs_2_, ...), custom_call_target="tpu_custom_call", output_to_operand_aliasing={{}: (10, {})} | custom-call | tf_op jit(solution)/shard_map/last_step/pallas_call | solution.py:501
  (49 shorter events, 31.9 us)
Async XLA Ops:
  6.4 7.3 %copy-start.5 = (f32[36,1024]{1,0:T(8,128)S(1)}, f32[36,1024]{1,0:T(8,128)}, u32[]{:S(2)}) copy-start(f32[36,1024]{1,0:T(8,128)} %get-tuple-element.44.gain_ref) | copy-start | bytes 442372
  6.4 7.3 %copy-start.11 = (s32[1,1024]{1,0:T(1,128)S(1)}, s32[1,1024]{1,0:T(1,128)}, u32[]{:S(2)}) copy-start(s32[1,1024]{1,0:T(1,128)} %get-tuple-element.45.target_ref) | copy-start | bytes 12292
  6.4 42.3 %all-to-all-start = ((f32[32,88,128]{2,1,0:T(8,128)}), f32[32,88,128]{2,1,0:T(8,128)S(1)}, u32[]{:S(2)}, u32[]{:S(2)}) async-start(f32[32,88,128]{2,1,0:T(8,128)} %get-tuple-element.43), calls=%async_computation | async-start | bytes 2883584 | tf_op jit(solution)/shard_map/all_to_all | solution.py:520
  13.7 2.2 %copy-start = (f32[25,36,1024]{2,1,0:T(8,128)S(1)}, f32[25,36,1024]{2,1,0:T(8,128)}, u32[]{:S(2)}) copy-start(f32[25,36,1024]{2,1,0:T(8,128)} %spectra_ref.3) | copy-start | bytes 11059204
  18.6 33.8 %copy-start.6 = (f32[2,512]{1,0:T(2,128)S(1)}, f32[2,512]{1,0:T(2,128)}, u32[]{:S(2)}) copy-start(f32[2,512]{1,0:T(2,128)} %refs_6_.11) | copy-start | bytes 12292
  18.6 33.8 %copy-start.10 = (f32[25]{0:T(128)S(1)}, f32[25]{0:T(128)}, u32[]{:S(2)}) copy-start(f32[25]{0:T(128)} %constant.19.clone.refs_1_.refs_4_) | copy-start | bytes 304
  48.7 39.2 %all-to-all-start.1 = ((f32[32,72,128]{2,1,0:T(8,128)}), f32[32,72,128]{2,1,0:T(8,128)S(1)}, u32[]{:S(2)}, u32[]{:S(2)}) async-start(f32[32,72,128]{2,1,0:T(8,128)} %copy-done.2), calls=%async_computation.1 | async-start | bytes 2359296 | tf_op jit(solution)/shard_map/all_to_all | solution.py:520
  55.9 24.1 %collective-permute-start = (f32[9,9,8,128]{3,2,1,0:T(8,128)S(1)}, f32[9,9,8,128]{3,2,1,0:T(8,128)S(1)}, u32[]{:S(2)}, u32[]{:S(2)}) collective-permute-start(f32[9,9,8,128]{3,2,1,0:T(8,128)S(1)} %get-tuple-element.49), channel_id=1, source_target_pairs={{0,4},{4,0},{8,12},{12,8},{16,20},{20,16},{24,28},{28,24},{1,5},{5... | collective-permute-start | bytes 995336 | tf_op jit(solution)/shard_map/ppermute | solution.py:386
  57.7 26.4 %collective-permute-start.1 = (f32[9,9,8,128]{3,2,1,0:T(8,128)S(1)}, f32[9,9,8,128]{3,2,1,0:T(8,128)S(1)}, u32[]{:S(2)}, u32[]{:S(2)}) collective-permute-start(f32[9,9,8,128]{3,2,1,0:T(8,128)S(1)} %get-tuple-element.50), channel_id=1, source_target_pairs={{0,28},{4,8},{8,4},{12,16},{16,12},{20,24},{24,20},{28,0},{1,29},{... | collective-permute-start | bytes 995336 | tf_op jit(solution)/shard_map/ppermute | solution.py:387
  63.2 20.9 %copy-start.7 = (f32[2,512]{1,0:T(2,128)S(1)}, f32[2,512]{1,0:T(2,128)}, u32[]{:S(2)}) copy-start(f32[2,512]{1,0:T(2,128)} %refs_7_.11) | copy-start | bytes 12292
  63.2 20.9 %copy-start.8 = (f32[2,512]{1,0:T(2,128)S(1)}, f32[2,512]{1,0:T(2,128)}, u32[]{:S(2)}) copy-start(f32[2,512]{1,0:T(2,128)} %refs_8_.11) | copy-start | bytes 12292
  63.2 20.9 %copy-start.9 = (s32[2,512]{1,0:T(2,128)S(1)}, s32[2,512]{1,0:T(2,128)}, u32[]{:S(2)}) copy-start(s32[2,512]{1,0:T(2,128)} %refs_9_.11) | copy-start | bytes 12292
  87.9 52.0 %all-to-all-start.2 = ((f32[32,72,128]{2,1,0:T(8,128)}), f32[32,72,128]{2,1,0:T(8,128)S(1)}, u32[]{:S(2)}, u32[]{:S(2)}) async-start(f32[32,72,128]{2,1,0:T(8,128)} %source_later.3), calls=%async_computation.2 | async-start | bytes 2359296 | tf_op jit(solution)/shard_map/all_to_all | solution.py:520
  95.1 32.4 %copy-start.4 = (f32[9,36,8,128]{3,2,1,0:T(8,128)S(1)}, f32[9,36,8,128]{3,2,1,0:T(8,128)}, u32[]{:S(2)}) copy-start(f32[9,36,8,128]{3,2,1,0:T(8,128)} %copy-done.3) | copy-start | bytes 3981316
  95.1 27.8 %collective-permute-start.2 = (f32[9,9,8,128]{3,2,1,0:T(8,128)S(1)}, f32[9,9,8,128]{3,2,1,0:T(8,128)S(1)}, u32[]{:S(2)}, u32[]{:S(2)}) collective-permute-start(f32[9,9,8,128]{3,2,1,0:T(8,128)S(1)} %get-tuple-element.58), channel_id=1, source_target_pairs={{0,4},{4,0},{8,12},{12,8},{16,20},{20,16},{24,28},{28,24},{1,5},{5... | collective-permute-start | bytes 995336 | tf_op jit(solution)/shard_map/ppermute | solution.py:386
  96.9 30.5 %collective-permute-start.3 = (f32[9,9,8,128]{3,2,1,0:T(8,128)S(1)}, f32[9,9,8,128]{3,2,1,0:T(8,128)S(1)}, u32[]{:S(2)}, u32[]{:S(2)}) collective-permute-start(f32[9,9,8,128]{3,2,1,0:T(8,128)S(1)} %get-tuple-element.59), channel_id=1, source_target_pairs={{0,28},{4,8},{8,4},{12,16},{16,12},{20,24},{24,20},{28,0},{1,29},{... | collective-permute-start | bytes 995336 | tf_op jit(solution)/shard_map/ppermute | solution.py:387
  103.4 34.1 %collective-permute-start.4 = (f32[8,9,8,128]{3,2,1,0:T(8,128)S(1)}, f32[8,9,8,128]{3,2,1,0:T(8,128)S(1)}, u32[]{:S(2)}, u32[]{:S(2)}) collective-permute-start(f32[8,9,8,128]{3,2,1,0:T(8,128)S(1)} %get-tuple-element.66), channel_id=1, source_target_pairs={{0,4},{4,0},{8,12},{12,8},{16,20},{20,16},{24,28},{28,24},{1,5},{5... | collective-permute-start | bytes 884744 | tf_op jit(solution)/shard_map/ppermute | solution.py:386
  103.5 34.0 %collective-permute-start.5 = (f32[8,9,8,128]{3,2,1,0:T(8,128)S(1)}, f32[8,9,8,128]{3,2,1,0:T(8,128)S(1)}, u32[]{:S(2)}, u32[]{:S(2)}) collective-permute-start(f32[8,9,8,128]{3,2,1,0:T(8,128)S(1)} %get-tuple-element.67), channel_id=1, source_target_pairs={{0,28},{4,8},{8,4},{12,16},{16,12},{20,24},{24,20},{28,0},{1,29},{... | collective-permute-start | bytes 884744 | tf_op jit(solution)/shard_map/ppermute | solution.py:387
  143.0 22.6 %collective-permute-start.6 = (f32[8,9,8,128]{3,2,1,0:T(8,128)S(1)}, f32[8,9,8,128]{3,2,1,0:T(8,128)S(1)}, u32[]{:S(2)}, u32[]{:S(2)}) collective-permute-start(f32[8,9,8,128]{3,2,1,0:T(8,128)S(1)} %get-tuple-element.70), channel_id=1, source_target_pairs={{0,4},{4,0},{8,12},{12,8},{16,20},{20,16},{24,28},{28,24},{1,5},{5... | collective-permute-start | bytes 884744 | tf_op jit(solution)/shard_map/ppermute | solution.py:386
  143.5 22.2 %collective-permute-start.7 = (f32[8,9,8,128]{3,2,1,0:T(8,128)S(1)}, f32[8,9,8,128]{3,2,1,0:T(8,128)S(1)}, u32[]{:S(2)}, u32[]{:S(2)}) collective-permute-start(f32[8,9,8,128]{3,2,1,0:T(8,128)S(1)} %get-tuple-element.71), channel_id=1, source_target_pairs={{0,28},{4,8},{8,4},{12,16},{16,12},{20,24},{24,20},{28,0},{1,29},{... | collective-permute-start | bytes 884744 | tf_op jit(solution)/shard_map/ppermute | solution.py:387
  147.9 30.5 %collective-permute-start.10 = (f32[8,9,8,128]{3,2,1,0:T(8,128)S(1)}, f32[8,9,8,128]{3,2,1,0:T(8,128)S(1)}, u32[]{:S(2)}, u32[]{:S(2)}) collective-permute-start(f32[8,9,8,128]{3,2,1,0:T(8,128)S(1)} %get-tuple-element.78), channel_id=1, source_target_pairs={{0,4},{4,0},{8,12},{12,8},{16,20},{20,16},{24,28},{28,24},{1,5},{5... | collective-permute-start | bytes 884744 | tf_op jit(solution)/shard_map/ppermute | solution.py:386
  147.9 30.5 %collective-permute-start.11 = (f32[8,9,8,128]{3,2,1,0:T(8,128)S(1)}, f32[8,9,8,128]{3,2,1,0:T(8,128)S(1)}, u32[]{:S(2)}, u32[]{:S(2)}) collective-permute-start(f32[8,9,8,128]{3,2,1,0:T(8,128)S(1)} %get-tuple-element.79), channel_id=1, source_target_pairs={{0,28},{4,8},{8,4},{12,16},{16,12},{20,24},{24,20},{28,0},{1,29},{... | collective-permute-start | bytes 884744 | tf_op jit(solution)/shard_map/ppermute | solution.py:387
  168.1 15.2 %collective-permute-start.8 = (f32[8,9,8,128]{3,2,1,0:T(8,128)S(1)}, f32[8,9,8,128]{3,2,1,0:T(8,128)S(1)}, u32[]{:S(2)}, u32[]{:S(2)}) collective-permute-start(f32[8,9,8,128]{3,2,1,0:T(8,128)S(1)} %get-tuple-element.74), channel_id=1, source_target_pairs={{0,4},{4,0},{8,12},{12,8},{16,20},{20,16},{24,28},{28,24},{1,5},{5... | collective-permute-start | bytes 884744 | tf_op jit(solution)/shard_map/ppermute | solution.py:386
  168.5 14.8 %collective-permute-start.9 = (f32[8,9,8,128]{3,2,1,0:T(8,128)S(1)}, f32[8,9,8,128]{3,2,1,0:T(8,128)S(1)}, u32[]{:S(2)}, u32[]{:S(2)}) collective-permute-start(f32[8,9,8,128]{3,2,1,0:T(8,128)S(1)} %get-tuple-element.75), channel_id=1, source_target_pairs={{0,28},{4,8},{8,4},{12,16},{16,12},{20,24},{24,20},{28,0},{1,29},{... | collective-permute-start | bytes 884744 | tf_op jit(solution)/shard_map/ppermute | solution.py:387
  (3 other events, 4.3 us)

commit v3 on v2

--- a/solution.py
+++ b/solution.py
@@ -216,7 +216,7 @@
     )
 
 
-def edge_messages(read, weight, odd_lon, f, ndir, pair_ref, cross_ref, side_ref):
+def edge_messages(read, weight, odd_lon, f, ndir, near_ref, cross_ref, side_ref):
     row, lane = tile_ids()
     odd = (row & 1) == 1
     quarter = ndir // 4
@@ -228,7 +228,7 @@
         right = jnp.where(odd, b, pltpu.roll(a, SUB - 1, 0))
         a, b = moved[quarter + e], moved[2 * quarter + e]
         left = jnp.where(odd, pltpu.roll(b, 1, 0), a)
-        pair_ref[f, e] = jnp.where(odd_lon, left, right)
+        near_ref[f, e] = jnp.where(odd_lon, left, right)
         cross_ref[f, e] = jnp.where(odd_lon, right, left)
     for k in range(2 * quarter):
         up = jnp.where(lane == k, pltpu.roll(moved[k], k + 1, 1), up)
@@ -240,11 +240,11 @@
 def place_kernel(plan, first, count, ndir, with_labels, *refs):
     if with_labels:
         in_ref, speed_ref, ids_ref, shoal_ref, *refs = refs
-        own_ref, right_ref, left_ref, side_ref, label_ref, x_ref, pair_ref = refs
+        own_ref, near_ref, cross_ref, side_ref, label_ref, x_ref, pair_ref = refs
     else:
         in_ref, speed_ref, ids_ref, shoal_ref, label_ref, *refs = refs
         refs = refs[-6:]
-        own_ref, right_ref, left_ref, side_ref, x_ref, pair_ref = refs
+        own_ref, near_ref, cross_ref, side_ref, x_ref, pair_ref = refs
     slots = x_ref.shape[1]
     for g in range(slots // LANES):
         blocks = [in_ref[g * plan.parts + i] for i in range(plan.parts)]
@@ -272,7 +272,7 @@
             return own_ref[pl.ds(pl.multiple_of((f * ndir + d) * SUB, SUB), SUB), :]
 
         edge_messages(
-            read, shoal * speed_ref[first + f], ids_ref[4] == 1, f, ndir, right_ref, left_ref, side_ref
+            read, shoal * speed_ref[first + f], ids_ref[4] == 1, f, ndir, near_ref, cross_ref, side_ref
         )
 
 
@@ -282,7 +282,7 @@
     if last:
         out_ref, new_ref, turn_ref, done_sem = refs[-4:]
     else:
-        new_ref, right_ref, left_ref, side_ref, turn_ref = refs
+        new_ref, near_ref, cross_ref, side_ref, turn_ref = refs
     count, ndir = own_ref.shape[:2]
     quarter = ndir // 4
     row, lane = tile_ids()
@@ -300,6 +300,9 @@
     odd_lon = lat_ref[4] == 1
     keep_up = lat_ref[2].astype(F32)
     keep_down = lat_ref[3].astype(F32)
+
+    def write(f):
+        return pltpu.make_async_copy(new_ref.at[f], out_ref.at[first + f], done_sem.at[f])
 
     @pl.loop(0, count)
     def advance(f):
@@ -352,13 +355,16 @@
             half, qt, below = half_next, qt_next, above
         if not last:
             edge_messages(
-                lambda d: new_ref[f, d], weight, odd_lon, f, ndir, right_ref, left_ref, side_ref
+                lambda d: new_ref[f, d], weight, odd_lon, f, ndir, near_ref, cross_ref, side_ref
             )
+        if last:
+            write(f).start()
 
     if last:
-        copy = pltpu.make_async_copy(new_ref, out_ref.at[pl.ds(first, count)], done_sem)
-        copy.start()
-        copy.wait()
+
+        @pl.loop(0, count)
+        def finish(f):
+            write(f).wait()
 
 
 def params():
@@ -506,7 +512,7 @@
             scratch_shapes=[
                 pltpu.VMEM(field.shape, F32),
                 pltpu.VMEM((ndir, SUB, LANES), F32),
-                pltpu.SemaphoreType.DMA(()),
+                pltpu.SemaphoreType.DMA((CHUNKS[i],)),
             ],
             input_output_aliases={10: 0} if chained else {},
             compiler_params=params(),

time: 187 us -> 186 us (level)
  no operation moved by 1% of the time
where the time goes in v3:
time: 186 us
  waiting for transfers between devices  77.1 us (41%)
  starting transfers between devices  42.1 us (23%)
  Pallas kernels  35.9 us (19%)
  blocking collectives  23.9 us (13%)
  local copies, waits for them, and re-layouts  6.51 us (4%)
    ppermute x6, waiting for transfers between devices, send_edges(): lax.ppermute(pair, 'lon', [(i, i ^ 1) for i in range(lon)])  38.3 us
    all_to_all x3, waiting for transfers between devices, on_device(): lax.all_to_all(messages[i], ('lon', 'lat'), split_axis=0, concat_axis=0,...  30.1 us
    ppermute x6, starting transfers between devices, send_edges(): lax.ppermute(cross, 'lon', [(i, (i + 2 * (i & 1) - 1) % lon) for i in ran...  19.4 us
    all_to_all x3, starting transfers between devices, on_device(): lax.all_to_all(messages[i], ('lon', 'lat'), split_axis=0, concat_axis=0,...  18.1 us
    all_gather x2, blocking collectives, on_device(): lax.all_gather(jnp.concatenate([waiting[2], sent[2]], axis=0), 'lat')  13.1 us
    pallas_call x3, Pallas kernels, place(): pl.pallas_call(functools.partial(place_kernel, plan, first, count, ndir,...  9.66 us
    ppermute x6, waiting for transfers between devices, send_edges(): lax.ppermute(cross, 'lon', [(i, (i + 2 * (i & 1) - 1) % lon) for i in ran...  8.73 us
    pallas_call x3, Pallas kernels, last_step(): pl.pallas_call(functools.partial(step_kernel, starts[i], side_first, True...  7.93 us
  transfers between devices with their start and end apart: 15, of which 8 were waited for; matrix products, arithmetic and copies ran while one was open for 0% of the time, Pallas kernels for 13%

profile of v3, /device:TPU:0, one launch (start us, length us, event | category | flops | bytes accessed | tf_op | source)
XLA Modules:
  0.0 186.0 jit_solution(1483322308082401405)
XLA Ops:
  0.0 6.4 %source_first.1 = (f32[32,88,128]{2,1,0:T(8,128)}, f32[36,1024]{1,0:T(8,128)}, s32[1,1024]{1,0:T(1,128)}) custom-call(f32[25,36,1024]{2,1,0:T(8,128)} %spectra_ref.3, f32[1,1024]{1,0:T(1,128)} %bitcast.30, f32[1,1024]{1,0:T(1,128)} %bitcast.31, s32[1,1024]{1,0:T(1,128)} %bitcast.32), custom_call_target="tpu_custom_call" | custom-call | tf_op jit(solution)/shard_map/source_first/pallas_call | solution.py:415
  6.4 7.3 %all-to-all-start = ((f32[32,88,128]{2,1,0:T(8,128)}), f32[32,88,128]{2,1,0:T(8,128)S(1)}, u32[]{:S(2)}, u32[]{:S(2)}) async-start(f32[32,88,128]{2,1,0:T(8,128)} %get-tuple-element.43), calls=%async_computation | async-start | bytes 2883584 | tf_op jit(solution)/shard_map/all_to_all | solution.py:526
  18.6 30.1 %all-to-all-done.refs_0_ = f32[32,88,128]{2,1,0:T(8,128)S(1)} async-done(((f32[32,88,128]{2,1,0:T(8,128)}), f32[32,88,128]{2,1,0:T(8,128)S(1)}, u32[]{:S(2)}, u32[]{:S(2)}) %all-to-all-start) | async-done | bytes 1441824 | tf_op jit(solution)/shard_map/all_to_all | solution.py:526
  48.7 3.6 %all-to-all-start.1 = ((f32[32,72,128]{2,1,0:T(8,128)}), f32[32,72,128]{2,1,0:T(8,128)S(1)}, u32[]{:S(2)}, u32[]{:S(2)}) async-start(f32[32,72,128]{2,1,0:T(8,128)} %copy-done.2), calls=%async_computation.1 | async-start | bytes 2359296 | tf_op jit(solution)/shard_map/all_to_all | solution.py:526
  52.4 3.4 %place.3 = (f32[2592,128]{1,0:T(8,128)S(1)}, f32[9,9,8,128]{3,2,1,0:T(8,128)S(1)}, f32[9,9,8,128]{3,2,1,0:T(8,128)S(1)}, f32[9,8,128]{2,1,0:T(8,128)S(1)}, s32[1,1024]{1,0:T(1,128)S(1)}) custom-call(f32[32,88,128]{2,1,0:T(8,128)S(1)} %all-to-all-done.refs_0_, f32[25]{0:T(128)S(1)} %copy-done.10, s32[5]{0:T(128)S(1)} %stack.31.refs_2_.refs_5_, ...), custom_call_target="tpu_custom_call" | custom-call | tf_op jit(solution)/shard_map/place/pallas_call | solution.py:478
  57.7 3.3 %collective-permute-start.1 = (f32[9,9,8,128]{3,2,1,0:T(8,128)S(1)}, f32[9,9,8,128]{3,2,1,0:T(8,128)S(1)}, u32[]{:S(2)}, u32[]{:S(2)}) collective-permute-start(f32[9,9,8,128]{3,2,1,0:T(8,128)S(1)} %get-tuple-element.50), channel_id=1, source_target_pairs={{0,28},{4,8},{8,4},{12,16},{16,12},{20,24},{24,20},{28,0},{1,29},{... | collective-permute-start | bytes 995336 | tf_op jit(solution)/shard_map/ppermute | solution.py:393
  63.2 2.7 %source_later.3 = f32[32,72,128]{2,1,0:T(8,128)} custom-call(f32[25,36,1024]{2,1,0:T(8,128)S(1)} %copy-done.1, f32[36,1024]{1,0:T(8,128)S(1)} %copy-done.5, s32[1,1024]{1,0:T(1,128)S(1)} %copy-done.11), custom_call_target="tpu_custom_call" | custom-call | tf_op jit(solution)/shard_map/source_later/pallas_call | solution.py:445
  66.0 5.5 %all-gather = f32[36,8,128]{2,1,0:T(8,128)S(1)} all-gather(f32[9,8,128]{2,1,0:T(8,128)S(1)} %get-tuple-element.51), channel_id=2, replica_groups=mesh['lon'=8,'lat'=4] {'lat'}, dimensions={0}, use_global_device_ids=true | all-gather | bytes 184320 | tf_op jit(solution)/shard_map/all_gather | solution.py:539
  71.4 8.6 %collective-permute-done.refs_1_ = f32[9,9,8,128]{3,2,1,0:T(8,128)S(1)} collective-permute-done((f32[9,9,8,128]{3,2,1,0:T(8,128)S(1)}, f32[9,9,8,128]{3,2,1,0:T(8,128)S(1)}, u32[]{:S(2)}, u32[]{:S(2)}) %collective-permute-start) | collective-permute-done | bytes 331808 | tf_op jit(solution)/shard_map/ppermute | solution.py:392
  80.0 4.2 %collective-permute-done.1.refs_2_ = f32[9,9,8,128]{3,2,1,0:T(8,128)S(1)} collective-permute-done((f32[9,9,8,128]{3,2,1,0:T(8,128)S(1)}, f32[9,9,8,128]{3,2,1,0:T(8,128)S(1)}, u32[]{:S(2)}, u32[]{:S(2)}) %collective-permute-start.1) | collective-permute-done | bytes 331808 | tf_op jit(solution)/shard_map/ppermute | solution.py:393
  87.9 7.2 %all-to-all-start.2 = ((f32[32,72,128]{2,1,0:T(8,128)}), f32[32,72,128]{2,1,0:T(8,128)S(1)}, u32[]{:S(2)}, u32[]{:S(2)}) async-start(f32[32,72,128]{2,1,0:T(8,128)} %source_later.3), calls=%async_computation.2 | async-start | bytes 2359296 | tf_op jit(solution)/shard_map/all_to_all | solution.py:526
  96.9 3.3 %collective-permute-start.3 = (f32[9,9,8,128]{3,2,1,0:T(8,128)S(1)}, f32[9,9,8,128]{3,2,1,0:T(8,128)S(1)}, u32[]{:S(2)}, u32[]{:S(2)}) collective-permute-start(f32[9,9,8,128]{3,2,1,0:T(8,128)S(1)} %get-tuple-element.59), channel_id=1, source_target_pairs={{0,28},{4,8},{8,4},{12,16},{16,12},{20,24},{24,20},{28,0},{1,29},{... | collective-permute-start | bytes 995336 | tf_op jit(solution)/shard_map/ppermute | solution.py:393
  100.3 3.1 %place.4 = (f32[2304,128]{1,0:T(8,128)S(1)}, f32[8,9,8,128]{3,2,1,0:T(8,128)S(1)}, f32[8,9,8,128]{3,2,1,0:T(8,128)S(1)}, f32[8,8,128]{2,1,0:T(8,128)S(1)}) custom-call(f32[32,72,128]{2,1,0:T(8,128)S(1)} %all-to-all-done.1.refs_0_, f32[25]{0:T(128)S(1)} %copy-done.10, s32[5]{0:T(128)S(1)} %stack.31.refs_2_.refs_5_, f32[2,512]{1,0:T(2,128)S(1)} %copy-done.6, ...), custom_call_target="tpu_custom_call" | custom-call | tf_op jit(solution)/shard_map/place/pallas_call | solution.py:478
  105.4 7.3 %all-gather.1 = f32[68,8,128]{2,1,0:T(8,128)S(1)} all-gather(f32[17,8,128]{2,1,0:T(8,128)S(1)} %pad_maximum_fusion), channel_id=3, replica_groups=mesh['lon'=8,'lat'=4] {'lat'}, dimensions={0}, use_global_device_ids=true | all-gather | bytes 348160 | tf_op jit(solution)/shard_map/all_gather | solution.py:542
  112.7 10.2 %collective-permute-done.2.refs_1_ = f32[9,9,8,128]{3,2,1,0:T(8,128)S(1)} collective-permute-done((f32[9,9,8,128]{3,2,1,0:T(8,128)S(1)}, f32[9,9,8,128]{3,2,1,0:T(8,128)S(1)}, u32[]{:S(2)}, u32[]{:S(2)}) %collective-permute-start.2) | collective-permute-done | bytes 331808 | tf_op jit(solution)/shard_map/ppermute | solution.py:392
  122.9 4.6 %collective-permute-done.3.refs_2_ = f32[9,9,8,128]{3,2,1,0:T(8,128)S(1)} collective-permute-done((f32[9,9,8,128]{3,2,1,0:T(8,128)S(1)}, f32[9,9,8,128]{3,2,1,0:T(8,128)S(1)}, u32[]{:S(2)}, u32[]{:S(2)}) %collective-permute-start.3) | collective-permute-done | bytes 331808 | tf_op jit(solution)/shard_map/ppermute | solution.py:393
  127.5 2.8 %last_step.3.refs_10_ = f32[25,36,8,128]{3,2,1,0:T(8,128)} custom-call(f32[9,36,8,128]{3,2,1,0:T(8,128)S(1)} %copy-done.4, f32[9,9,8,128]{3,2,1,0:T(8,128)S(1)} %collective-permute-done.2.refs_1_, f32[9,9,8,128]{3,2,1,0:T(8,128)S(1)} %collective-permute-done.3.refs_2_, f32[4,17,8,128]{3,2,1,0:T(8,128)S(1)} %bitcast.20, f32[25]{0:T(128)S(1)} %copy-done.10, ...), custom_call_target="tpu_custom_call" | custom-call | tf_op jit(solution)/shard_map/last_step/pallas_call | solution.py:507
  130.2 7.2 %collective-permute-done.4.refs_1_ = f32[8,9,8,128]{3,2,1,0:T(8,128)S(1)} collective-permute-done((f32[8,9,8,128]{3,2,1,0:T(8,128)S(1)}, f32[8,9,8,128]{3,2,1,0:T(8,128)S(1)}, u32[]{:S(2)}, u32[]{:S(2)}) %collective-permute-start.4) | collective-permute-done | bytes 294944 | tf_op jit(solution)/shard_map/ppermute | solution.py:392
  139.9 3.1 %place.5 = (f32[2304,128]{1,0:T(8,128)S(1)}, f32[8,9,8,128]{3,2,1,0:T(8,128)S(1)}, f32[8,9,8,128]{3,2,1,0:T(8,128)S(1)}, f32[8,8,128]{2,1,0:T(8,128)S(1)}) custom-call(f32[32,72,128]{2,1,0:T(8,128)S(1)} %all-to-all-done.2.refs_0_, f32[25]{0:T(128)S(1)} %copy-done.10, s32[5]{0:T(128)S(1)} %stack.31.refs_2_.refs_5_, f32[2,512]{1,0:T(2,128)S(1)} %copy-done.6, ...), custom_call_target="tpu_custom_call" | custom-call | tf_op jit(solution)/shard_map/place/pallas_call | solution.py:478
  143.5 4.4 %collective-permute-start.7 = (f32[8,9,8,128]{3,2,1,0:T(8,128)S(1)}, f32[8,9,8,128]{3,2,1,0:T(8,128)S(1)}, u32[]{:S(2)}, u32[]{:S(2)}) collective-permute-start(f32[8,9,8,128]{3,2,1,0:T(8,128)S(1)} %get-tuple-element.71), channel_id=1, source_target_pairs={{0,28},{4,8},{8,4},{12,16},{16,12},{20,24},{24,20},{28,0},{1,29},{... | collective-permute-start | bytes 884744 | tf_op jit(solution)/shard_map/ppermute | solution.py:393
  149.9 5.8 %all-gather.2 = f32[64,8,128]{2,1,0:T(8,128)S(1)} all-gather(f32[16,8,128]{2,1,0:T(8,128)S(1)} %pad_maximum_fusion.1), channel_id=4, replica_groups=mesh['lon'=8,'lat'=4] {'lat'}, dimensions={0}, use_global_device_ids=true | all-gather | bytes 327680 | tf_op jit(solution)/shard_map/all_gather | solution.py:542
  155.6 10.0 %collective-permute-done.6.refs_1_ = f32[8,9,8,128]{3,2,1,0:T(8,128)S(1)} collective-permute-done((f32[8,9,8,128]{3,2,1,0:T(8,128)S(1)}, f32[8,9,8,128]{3,2,1,0:T(8,128)S(1)}, u32[]{:S(2)}, u32[]{:S(2)}) %collective-permute-start.6) | collective-permute-done | bytes 294944 | tf_op jit(solution)/shard_map/ppermute | solution.py:392
  168.5 4.5 %collective-permute-start.9 = (f32[8,9,8,128]{3,2,1,0:T(8,128)S(1)}, f32[8,9,8,128]{3,2,1,0:T(8,128)S(1)}, u32[]{:S(2)}, u32[]{:S(2)}) collective-permute-start(f32[8,9,8,128]{3,2,1,0:T(8,128)S(1)} %get-tuple-element.75), channel_id=1, source_target_pairs={{0,28},{4,8},{8,4},{12,16},{16,12},{20,24},{24,20},{28,0},{1,29},{... | collective-permute-start | bytes 884744 | tf_op jit(solution)/shard_map/ppermute | solution.py:393
  173.0 5.4 %all-gather.3 = f32[32,8,128]{2,1,0:T(8,128)S(1)} all-gather(f32[8,8,128]{2,1,0:T(8,128)S(1)} %get-tuple-element.76), channel_id=5, replica_groups=mesh['lon'=8,'lat'=4] {'lat'}, dimensions={0}, use_global_device_ids=true | all-gather | bytes 163840 | tf_op jit(solution)/shard_map/all_gather | solution.py:553
  (49 shorter events, 31.7 us)
Async XLA Ops:
  6.4 7.3 %copy-start.5 = (f32[36,1024]{1,0:T(8,128)S(1)}, f32[36,1024]{1,0:T(8,128)}, u32[]{:S(2)}) copy-start(f32[36,1024]{1,0:T(8,128)} %get-tuple-element.44.gain_ref) | copy-start | bytes 442372
  6.4 7.3 %copy-start.11 = (s32[1,1024]{1,0:T(1,128)S(1)}, s32[1,1024]{1,0:T(1,128)}, u32[]{:S(2)}) copy-start(s32[1,1024]{1,0:T(1,128)} %get-tuple-element.45.target_ref) | copy-start | bytes 12292
  6.4 42.3 %all-to-all-start = ((f32[32,88,128]{2,1,0:T(8,128)}), f32[32,88,128]{2,1,0:T(8,128)S(1)}, u32[]{:S(2)}, u32[]{:S(2)}) async-start(f32[32,88,128]{2,1,0:T(8,128)} %get-tuple-element.43), calls=%async_computation | async-start | bytes 2883584 | tf_op jit(solution)/shard_map/all_to_all | solution.py:526
  13.7 2.2 %copy-start = (f32[25,36,1024]{2,1,0:T(8,128)S(1)}, f32[25,36,1024]{2,1,0:T(8,128)}, u32[]{:S(2)}) copy-start(f32[25,36,1024]{2,1,0:T(8,128)} %spectra_ref.3) | copy-start | bytes 11059204
  18.6 33.8 %copy-start.6 = (f32[2,512]{1,0:T(2,128)S(1)}, f32[2,512]{1,0:T(2,128)}, u32[]{:S(2)}) copy-start(f32[2,512]{1,0:T(2,128)} %refs_6_.11) | copy-start | bytes 12292
  18.6 33.8 %copy-start.10 = (f32[25]{0:T(128)S(1)}, f32[25]{0:T(128)}, u32[]{:S(2)}) copy-start(f32[25]{0:T(128)} %constant.19.clone.refs_1_.refs_4_) | copy-start | bytes 304
  48.7 39.2 %all-to-all-start.1 = ((f32[32,72,128]{2,1,0:T(8,128)}), f32[32,72,128]{2,1,0:T(8,128)S(1)}, u32[]{:S(2)}, u32[]{:S(2)}) async-start(f32[32,72,128]{2,1,0:T(8,128)} %copy-done.2), calls=%async_computation.1 | async-start | bytes 2359296 | tf_op jit(solution)/shard_map/all_to_all | solution.py:526
  55.9 24.1 %collective-permute-start = (f32[9,9,8,128]{3,2,1,0:T(8,128)S(1)}, f32[9,9,8,128]{3,2,1,0:T(8,128)S(1)}, u32[]{:S(2)}, u32[]{:S(2)}) collective-permute-start(f32[9,9,8,128]{3,2,1,0:T(8,128)S(1)} %get-tuple-element.49), channel_id=1, source_target_pairs={{0,4},{4,0},{8,12},{12,8},{16,20},{20,16},{24,28},{28,24},{1,5},{5... | collective-permute-start | bytes 995336 | tf_op jit(solution)/shard_map/ppermute | solution.py:392
  57.7 26.4 %collective-permute-start.1 = (f32[9,9,8,128]{3,2,1,0:T(8,128)S(1)}, f32[9,9,8,128]{3,2,1,0:T(8,128)S(1)}, u32[]{:S(2)}, u32[]{:S(2)}) collective-permute-start(f32[9,9,8,128]{3,2,1,0:T(8,128)S(1)} %get-tuple-element.50), channel_id=1, source_target_pairs={{0,28},{4,8},{8,4},{12,16},{16,12},{20,24},{24,20},{28,0},{1,29},{... | collective-permute-start | bytes 995336 | tf_op jit(solution)/shard_map/ppermute | solution.py:393
  63.2 20.9 %copy-start.7 = (f32[2,512]{1,0:T(2,128)S(1)}, f32[2,512]{1,0:T(2,128)}, u32[]{:S(2)}) copy-start(f32[2,512]{1,0:T(2,128)} %refs_7_.11) | copy-start | bytes 12292
  63.2 20.9 %copy-start.8 = (f32[2,512]{1,0:T(2,128)S(1)}, f32[2,512]{1,0:T(2,128)}, u32[]{:S(2)}) copy-start(f32[2,512]{1,0:T(2,128)} %refs_8_.11) | copy-start | bytes 12292
  63.2 20.9 %copy-start.9 = (s32[2,512]{1,0:T(2,128)S(1)}, s32[2,512]{1,0:T(2,128)}, u32[]{:S(2)}) copy-start(s32[2,512]{1,0:T(2,128)} %refs_9_.11) | copy-start | bytes 12292
  87.9 52.0 %all-to-all-start.2 = ((f32[32,72,128]{2,1,0:T(8,128)}), f32[32,72,128]{2,1,0:T(8,128)S(1)}, u32[]{:S(2)}, u32[]{:S(2)}) async-start(f32[32,72,128]{2,1,0:T(8,128)} %source_later.3), calls=%async_computation.2 | async-start | bytes 2359296 | tf_op jit(solution)/shard_map/all_to_all | solution.py:526
  95.1 32.4 %copy-start.4 = (f32[9,36,8,128]{3,2,1,0:T(8,128)S(1)}, f32[9,36,8,128]{3,2,1,0:T(8,128)}, u32[]{:S(2)}) copy-start(f32[9,36,8,128]{3,2,1,0:T(8,128)} %copy-done.3) | copy-start | bytes 3981316
  95.1 27.8 %collective-permute-start.2 = (f32[9,9,8,128]{3,2,1,0:T(8,128)S(1)}, f32[9,9,8,128]{3,2,1,0:T(8,128)S(1)}, u32[]{:S(2)}, u32[]{:S(2)}) collective-permute-start(f32[9,9,8,128]{3,2,1,0:T(8,128)S(1)} %get-tuple-element.58), channel_id=1, source_target_pairs={{0,4},{4,0},{8,12},{12,8},{16,20},{20,16},{24,28},{28,24},{1,5},{5... | collective-permute-start | bytes 995336 | tf_op jit(solution)/shard_map/ppermute | solution.py:392
  96.9 30.5 %collective-permute-start.3 = (f32[9,9,8,128]{3,2,1,0:T(8,128)S(1)}, f32[9,9,8,128]{3,2,1,0:T(8,128)S(1)}, u32[]{:S(2)}, u32[]{:S(2)}) collective-permute-start(f32[9,9,8,128]{3,2,1,0:T(8,128)S(1)} %get-tuple-element.59), channel_id=1, source_target_pairs={{0,28},{4,8},{8,4},{12,16},{16,12},{20,24},{24,20},{28,0},{1,29},{... | collective-permute-start | bytes 995336 | tf_op jit(solution)/shard_map/ppermute | solution.py:393
  103.4 34.1 %collective-permute-start.4 = (f32[8,9,8,128]{3,2,1,0:T(8,128)S(1)}, f32[8,9,8,128]{3,2,1,0:T(8,128)S(1)}, u32[]{:S(2)}, u32[]{:S(2)}) collective-permute-start(f32[8,9,8,128]{3,2,1,0:T(8,128)S(1)} %get-tuple-element.66), channel_id=1, source_target_pairs={{0,4},{4,0},{8,12},{12,8},{16,20},{20,16},{24,28},{28,24},{1,5},{5... | collective-permute-start | bytes 884744 | tf_op jit(solution)/shard_map/ppermute | solution.py:392
  103.5 34.0 %collective-permute-start.5 = (f32[8,9,8,128]{3,2,1,0:T(8,128)S(1)}, f32[8,9,8,128]{3,2,1,0:T(8,128)S(1)}, u32[]{:S(2)}, u32[]{:S(2)}) collective-permute-start(f32[8,9,8,128]{3,2,1,0:T(8,128)S(1)} %get-tuple-element.67), channel_id=1, source_target_pairs={{0,28},{4,8},{8,4},{12,16},{16,12},{20,24},{24,20},{28,0},{1,29},{... | collective-permute-start | bytes 884744 | tf_op jit(solution)/shard_map/ppermute | solution.py:393
  143.0 22.6 %collective-permute-start.6 = (f32[8,9,8,128]{3,2,1,0:T(8,128)S(1)}, f32[8,9,8,128]{3,2,1,0:T(8,128)S(1)}, u32[]{:S(2)}, u32[]{:S(2)}) collective-permute-start(f32[8,9,8,128]{3,2,1,0:T(8,128)S(1)} %get-tuple-element.70), channel_id=1, source_target_pairs={{0,4},{4,0},{8,12},{12,8},{16,20},{20,16},{24,28},{28,24},{1,5},{5... | collective-permute-start | bytes 884744 | tf_op jit(solution)/shard_map/ppermute | solution.py:392
  143.5 22.2 %collective-permute-start.7 = (f32[8,9,8,128]{3,2,1,0:T(8,128)S(1)}, f32[8,9,8,128]{3,2,1,0:T(8,128)S(1)}, u32[]{:S(2)}, u32[]{:S(2)}) collective-permute-start(f32[8,9,8,128]{3,2,1,0:T(8,128)S(1)} %get-tuple-element.71), channel_id=1, source_target_pairs={{0,28},{4,8},{8,4},{12,16},{16,12},{20,24},{24,20},{28,0},{1,29},{... | collective-permute-start | bytes 884744 | tf_op jit(solution)/shard_map/ppermute | solution.py:393
  147.9 30.5 %collective-permute-start.10 = (f32[8,9,8,128]{3,2,1,0:T(8,128)S(1)}, f32[8,9,8,128]{3,2,1,0:T(8,128)S(1)}, u32[]{:S(2)}, u32[]{:S(2)}) collective-permute-start(f32[8,9,8,128]{3,2,1,0:T(8,128)S(1)} %get-tuple-element.78), channel_id=1, source_target_pairs={{0,4},{4,0},{8,12},{12,8},{16,20},{20,16},{24,28},{28,24},{1,5},{5... | collective-permute-start | bytes 884744 | tf_op jit(solution)/shard_map/ppermute | solution.py:392
  147.9 30.5 %collective-permute-start.11 = (f32[8,9,8,128]{3,2,1,0:T(8,128)S(1)}, f32[8,9,8,128]{3,2,1,0:T(8,128)S(1)}, u32[]{:S(2)}, u32[]{:S(2)}) collective-permute-start(f32[8,9,8,128]{3,2,1,0:T(8,128)S(1)} %get-tuple-element.79), channel_id=1, source_target_pairs={{0,28},{4,8},{8,4},{12,16},{16,12},{20,24},{24,20},{28,0},{1,29},{... | collective-permute-start | bytes 884744 | tf_op jit(solution)/shard_map/ppermute | solution.py:393
  168.1 15.2 %collective-permute-start.8 = (f32[8,9,8,128]{3,2,1,0:T(8,128)S(1)}, f32[8,9,8,128]{3,2,1,0:T(8,128)S(1)}, u32[]{:S(2)}, u32[]{:S(2)}) collective-permute-start(f32[8,9,8,128]{3,2,1,0:T(8,128)S(1)} %get-tuple-element.74), channel_id=1, source_target_pairs={{0,4},{4,0},{8,12},{12,8},{16,20},{20,16},{24,28},{28,24},{1,5},{5... | collective-permute-start | bytes 884744 | tf_op jit(solution)/shard_map/ppermute | solution.py:392
  168.5 14.8 %collective-permute-start.9 = (f32[8,9,8,128]{3,2,1,0:T(8,128)S(1)}, f32[8,9,8,128]{3,2,1,0:T(8,128)S(1)}, u32[]{:S(2)}, u32[]{:S(2)}) collective-permute-start(f32[8,9,8,128]{3,2,1,0:T(8,128)S(1)} %get-tuple-element.75), channel_id=1, source_target_pairs={{0,28},{4,8},{8,4},{12,16},{16,12},{20,24},{24,20},{28,0},{1,29},{... | collective-permute-start | bytes 884744 | tf_op jit(solution)/shard_map/ppermute | solution.py:393
  (3 other events, 4.3 us)

commit v4 on v3

--- a/solution.py
+++ b/solution.py
@@ -13,7 +13,7 @@
 BF16 = jnp.bfloat16
 LANES = 128
 SUB = 8
-CHUNKS = (9, 8, 8)
+CHUNKS = (10, 8, 7)
 NBLOCK = 256
 VMEM_LIMIT = 32 * 2**20
 
@@ -243,7 +243,6 @@
         own_ref, near_ref, cross_ref, side_ref, label_ref, x_ref, pair_ref = refs
     else:
         in_ref, speed_ref, ids_ref, shoal_ref, label_ref, *refs = refs
-        refs = refs[-6:]
         own_ref, near_ref, cross_ref, side_ref, x_ref, pair_ref = refs
     slots = x_ref.shape[1]
     for g in range(slots // LANES):
@@ -470,7 +469,7 @@
     label = None
     out = None
 
-    def place(i, arrived, after=()):
+    def place(i, arrived):
         first, count, plan = starts[i], CHUNKS[i], plans[i]
         outs = [jax.ShapeDtypeStruct((count * ndir * SUB, LANES), F32)] + edge_shapes(count, ndir)
         if i == 0:
@@ -478,7 +477,7 @@
         field, *sent = pl.pallas_call(
             functools.partial(place_kernel, plan, first, count, ndir, i == 0),
             out_shape=outs,
-            in_specs=vmem(1) + [SMEM_SPEC, SMEM_SPEC] + vmem(1 if i == 0 else 2) + [ANY_SPEC] * len(after),
+            in_specs=vmem(1) + [SMEM_SPEC, SMEM_SPEC] + vmem(1 if i == 0 else 2),
             out_specs=vmem(len(outs)),
             scratch_shapes=[
                 pltpu.VMEM((plan.total, slots), F32),
@@ -486,7 +485,7 @@
             ],
             compiler_params=params(),
             name="place",
-        )(arrived, speed, lat_ids, shoaling, *([] if i == 0 else [label]), *after)
+        )(arrived, speed, lat_ids, shoaling, *([] if i == 0 else [label]))
         return field.reshape(count, ndir, SUB, LANES), sent
 
     def step(i, field, received, side_first):
@@ -530,8 +529,7 @@
             arrived, messages[i + 1] = tie((arrived, messages[i + 1]))
         if i >= 2:
             arrived, out = tie((arrived, out))
-        after = (waiting[2],) if i >= 2 else ()
-        field, sent = place(i, arrived, after)
+        field, sent = place(i, arrived)
         if i == 0:
             *sent, label = sent
         received = send_edges(*sent[:2])

time: 186 us -> 183 us (0.984)
  waiting for transfers between devices: 77.1 us -> 72.4 us
    ppermute x6, waiting for transfers between devices: 8.73 us -> 3 us  [send_edges(): lax.ppermute(cross, 'lon', [(i, (i + 2 * (i & 1) - 1) % lon) for i in ran...]
    all_to_all x3, waiting for transfers between devices: 30.1 us -> 34.8 us  [on_device(): lax.all_to_all(messages[i], ('lon', 'lat'), split_axis=0, concat_axis=0,...]
    ppermute x6, waiting for transfers between devices: 38.3 us -> 34.6 us  [send_edges(): lax.ppermute(pair, 'lon', [(i, i ^ 1) for i in range(lon)])]
    ppermute x6, starting transfers between devices: 19.4 us -> 15.8 us  [send_edges(): lax.ppermute(cross, 'lon', [(i, (i + 2 * (i & 1) - 1) % lon) for i in ran...]
    ppermute x6, starting transfers between devices: 4.58 us -> 8.17 us  [send_edges(): lax.ppermute(pair, 'lon', [(i, i ^ 1) for i in range(lon)])]
  transfers between devices with their start and end apart: 15 -> 15, of which waited for: 8 -> 7; matrix products, arithmetic and copies ran while one was open for 0% -> 0% of each run, Pallas kernels for 13% -> 16%
where the time goes in v4:
time: 183 us; the launch traced here: 182 us
  waiting for transfers between devices  72.4 us (40%)
  starting transfers between devices  42.3 us (23%)
  Pallas kernels  37.5 us (20%)
  blocking collectives  23.4 us (13%)
  local copies, waits for them, and re-layouts  6.56 us (4%)
    all_to_all x3, waiting for transfers between devices, on_device(): lax.all_to_all(messages[i], ('lon', 'lat'), split_axis=0, concat_axis=0,...  34.8 us
    ppermute x6, waiting for transfers between devices, send_edges(): lax.ppermute(pair, 'lon', [(i, i ^ 1) for i in range(lon)])  34.6 us
    all_to_all x3, starting transfers between devices, on_device(): lax.all_to_all(messages[i], ('lon', 'lat'), split_axis=0, concat_axis=0,...  18.3 us
    ppermute x6, starting transfers between devices, send_edges(): lax.ppermute(cross, 'lon', [(i, (i + 2 * (i & 1) - 1) % lon) for i in ran...  15.8 us
    all_gather x2, blocking collectives, on_device(): lax.all_gather(jnp.concatenate([waiting[2], sent[2]], axis=0), 'lat')  12.5 us
    pallas_call x3, Pallas kernels, place(): pl.pallas_call(functools.partial(place_kernel, plan, first, count, ndir,...  10.4 us
    pallas_call x3, Pallas kernels, step(): pl.pallas_call(functools.partial(step_kernel, starts[i], side_first, Fals...  8.33 us
    ppermute x6, starting transfers between devices, send_edges(): lax.ppermute(pair, 'lon', [(i, i ^ 1) for i in range(lon)])  8.17 us
  transfers between devices with their start and end apart: 15, of which 7 were waited for; matrix products, arithmetic and copies ran while one was open for 0% of the time, Pallas kernels for 16%

profile of v4, /device:TPU:0, one launch (start us, length us, event | category | flops | bytes accessed | tf_op | source)
XLA Modules:
  0.0 182.5 jit_solution(3269500987215334441)
XLA Ops:
  0.0 6.6 %source_first.1 = (f32[32,96,128]{2,1,0:T(8,128)}, f32[36,1024]{1,0:T(8,128)}, s32[1,1024]{1,0:T(1,128)}) custom-call(f32[25,36,1024]{2,1,0:T(8,128)} %spectra_ref.3, f32[1,1024]{1,0:T(1,128)} %bitcast.30, f32[1,1024]{1,0:T(1,128)} %bitcast.31, s32[1,1024]{1,0:T(1,128)} %bitcast.32), custom_call_target="tpu_custom_call" | custom-call | tf_op jit(solution)/shard_map/source_first/pallas_call | solution.py:414
  6.6 7.3 %all-to-all-start = ((f32[32,96,128]{2,1,0:T(8,128)}), f32[32,96,128]{2,1,0:T(8,128)S(1)}, u32[]{:S(2)}, u32[]{:S(2)}) async-start(f32[32,96,128]{2,1,0:T(8,128)} %get-tuple-element.43), calls=%async_computation | async-start | bytes 3145728 | tf_op jit(solution)/shard_map/all_to_all | solution.py:525
  18.8 32.8 %all-to-all-done.refs_0_ = f32[32,96,128]{2,1,0:T(8,128)S(1)} async-done(((f32[32,96,128]{2,1,0:T(8,128)}), f32[32,96,128]{2,1,0:T(8,128)S(1)}, u32[]{:S(2)}, u32[]{:S(2)}) %all-to-all-start) | async-done | bytes 1572896 | tf_op jit(solution)/shard_map/all_to_all | solution.py:525
  51.6 3.8 %all-to-all-start.1 = ((f32[32,72,128]{2,1,0:T(8,128)}), f32[32,72,128]{2,1,0:T(8,128)S(1)}, u32[]{:S(2)}, u32[]{:S(2)}) async-start(f32[32,72,128]{2,1,0:T(8,128)} %copy-done.2), calls=%async_computation.1 | async-start | bytes 2359296 | tf_op jit(solution)/shard_map/all_to_all | solution.py:525
  55.5 3.7 %place.3 = (f32[2880,128]{1,0:T(8,128)S(1)}, f32[10,9,8,128]{3,2,1,0:T(8,128)S(1)}, f32[10,9,8,128]{3,2,1,0:T(8,128)S(1)}, f32[10,8,128]{2,1,0:T(8,128)S(1)}, s32[1,1024]{1,0:T(1,128)S(1)}) custom-call(f32[32,96,128]{2,1,0:T(8,128)S(1)} %all-to-all-done.refs_0_, f32[25]{0:T(128)S(1)} %copy-done.10, s32[5]{0:T(128)S(1)} %stack.31.refs_2_.refs_5_, ...), custom_call_target="tpu_custom_call" | custom-call | tf_op jit(solution)/shard_map/place/pallas_call | solution.py:477
  61.1 3.3 %collective-permute-start.1 = (f32[10,9,8,128]{3,2,1,0:T(8,128)S(1)}, f32[10,9,8,128]{3,2,1,0:T(8,128)S(1)}, u32[]{:S(2)}, u32[]{:S(2)}) collective-permute-start(f32[10,9,8,128]{3,2,1,0:T(8,128)S(1)} %get-tuple-element.50), channel_id=1, source_target_pairs={{0,28},{4,8},{8,4},{12,16},{16,12},{20,24},{24,20},{28,0},{1,29},{... | collective-permute-start | bytes 1105928 | tf_op jit(solution)/shard_map/ppermute | solution.py:392
  66.6 2.5 %source_later.3 = f32[32,64,128]{2,1,0:T(8,128)} custom-call(f32[25,36,1024]{2,1,0:T(8,128)S(1)} %copy-done.1, f32[36,1024]{1,0:T(8,128)S(1)} %copy-done.5, s32[1,1024]{1,0:T(1,128)S(1)} %copy-done.11), custom_call_target="tpu_custom_call" | custom-call | tf_op jit(solution)/shard_map/source_later/pallas_call | solution.py:444
  69.1 5.5 %all-gather = f32[40,8,128]{2,1,0:T(8,128)S(1)} all-gather(f32[10,8,128]{2,1,0:T(8,128)S(1)} %get-tuple-element.51), channel_id=2, replica_groups=mesh['lon'=8,'lat'=4] {'lat'}, dimensions={0}, use_global_device_ids=true | all-gather | bytes 204800 | tf_op jit(solution)/shard_map/all_gather | solution.py:537
  74.6 10.4 %collective-permute-done.refs_1_ = f32[10,9,8,128]{3,2,1,0:T(8,128)S(1)} collective-permute-done((f32[10,9,8,128]{3,2,1,0:T(8,128)S(1)}, f32[10,9,8,128]{3,2,1,0:T(8,128)S(1)}, u32[]{:S(2)}, u32[]{:S(2)}) %collective-permute-start) | collective-permute-done | bytes 368672 | tf_op jit(solution)/shard_map/ppermute | solution.py:391
  85.0 3.0 %collective-permute-done.1.refs_2_ = f32[10,9,8,128]{3,2,1,0:T(8,128)S(1)} collective-permute-done((f32[10,9,8,128]{3,2,1,0:T(8,128)S(1)}, f32[10,9,8,128]{3,2,1,0:T(8,128)S(1)}, u32[]{:S(2)}, u32[]{:S(2)}) %collective-permute-start.1) | collective-permute-done | bytes 368672 | tf_op jit(solution)/shard_map/ppermute | solution.py:392
  88.0 3.7 %step.3 = (f32[10,36,8,128]{3,2,1,0:T(8,128)S(1)}, f32[10,9,8,128]{3,2,1,0:T(8,128)}, f32[10,9,8,128]{3,2,1,0:T(8,128)}, f32[10,8,128]{2,1,0:T(8,128)S(1)}) custom-call(f32[10,36,8,128]{3,2,1,0:T(8,128)S(1)} %bitcast.24, f32[10,9,8,128]{3,2,1,0:T(8,128)S(1)} %collective-permute-done.refs_1_, f32[10,9,8,128]{3,2,1,0:T(8,128)S(1)} %collective-permute-done.1.refs_2_, ...), custom_call_target="tpu_custom_call" | custom-call | tf_op jit(solution)/shard_map/step/pallas_call | solution.py:493
  92.8 7.2 %all-to-all-start.2 = ((f32[32,64,128]{2,1,0:T(8,128)}), f32[32,64,128]{2,1,0:T(8,128)S(1)}, u32[]{:S(2)}, u32[]{:S(2)}) async-start(f32[32,64,128]{2,1,0:T(8,128)} %source_later.3), calls=%async_computation.2 | async-start | bytes 2097152 | tf_op jit(solution)/shard_map/all_to_all | solution.py:525
  101.9 3.3 %collective-permute-start.3 = (f32[10,9,8,128]{3,2,1,0:T(8,128)}, f32[10,9,8,128]{3,2,1,0:T(8,128)S(1)}, u32[]{:S(2)}, u32[]{:S(2)}) collective-permute-start(f32[10,9,8,128]{3,2,1,0:T(8,128)} %get-tuple-element.59), channel_id=1, source_target_pairs={{0,28},{4,8},{8,4},{12,16},{16,12},{20,24},{24,20},{28,0},{1,29},{... | collective-permute-start | bytes 1105928 | tf_op jit(solution)/shard_map/ppermute | solution.py:392
  105.2 3.8 %place.4 = (f32[2304,128]{1,0:T(8,128)S(1)}, f32[8,9,8,128]{3,2,1,0:T(8,128)}, f32[8,9,8,128]{3,2,1,0:T(8,128)}, f32[8,8,128]{2,1,0:T(8,128)S(1)}) custom-call(f32[32,72,128]{2,1,0:T(8,128)S(1)} %all-to-all-done.1.refs_0_, f32[25]{0:T(128)S(1)} %copy-done.10, s32[5]{0:T(128)S(1)} %stack.31.refs_2_.refs_5_, f32[2,512]{1,0:T(2,128)S(1)} %copy-done.6, ...), custom_call_target="tpu_custom_call" | custom-call | tf_op jit(solution)/shard_map/place/pallas_call | solution.py:477
  111.0 6.8 %all-gather.1 = f32[72,8,128]{2,1,0:T(8,128)S(1)} all-gather(f32[18,8,128]{2,1,0:T(8,128)S(1)} %pad_maximum_fusion), channel_id=3, replica_groups=mesh['lon'=8,'lat'=4] {'lat'}, dimensions={0}, use_global_device_ids=true | all-gather | bytes 368640 | tf_op jit(solution)/shard_map/all_gather | solution.py:540
  117.9 16.5 %collective-permute-done.2.refs_1_ = f32[10,9,8,128]{3,2,1,0:T(8,128)S(1)} collective-permute-done((f32[10,9,8,128]{3,2,1,0:T(8,128)}, f32[10,9,8,128]{3,2,1,0:T(8,128)S(1)}, u32[]{:S(2)}, u32[]{:S(2)}) %collective-permute-start.2) | collective-permute-done | bytes 368672 | tf_op jit(solution)/shard_map/ppermute | solution.py:391
  134.4 2.9 %last_step.3.refs_10_ = f32[25,36,8,128]{3,2,1,0:T(8,128)} custom-call(f32[10,36,8,128]{3,2,1,0:T(8,128)S(1)} %copy-done.4, f32[10,9,8,128]{3,2,1,0:T(8,128)S(1)} %collective-permute-done.2.refs_1_, f32[10,9,8,128]{3,2,1,0:T(8,128)S(1)} %collective-permute-done.3.refs_2_, f32[4,18,8,128]{3,2,1,0:T(8,128)S(1)} %bitcast.20, f32[25]{0:T(128)S(1)} %copy-done.10, ...), custom_call_target="tpu_custom_call" | custom-call | tf_op jit(solution)/shard_map/last_step/pallas_call | solution.py:506
  139.3 2.9 %place.5 = (f32[2016,128]{1,0:T(8,128)S(1)}, f32[7,9,8,128]{3,2,1,0:T(8,128)S(1)}, f32[7,9,8,128]{3,2,1,0:T(8,128)S(1)}, f32[7,8,128]{2,1,0:T(8,128)S(1)}) custom-call(f32[32,64,128]{2,1,0:T(8,128)S(1)} %all-to-all-done.2.refs_0_, f32[25]{0:T(128)S(1)} %copy-done.10, s32[5]{0:T(128)S(1)} %stack.31.refs_2_.refs_5_, f32[2,512]{1,0:T(2,128)S(1)} %copy-done.6, ...), custom_call_target="tpu_custom_call" | custom-call | tf_op jit(solution)/shard_map/place/pallas_call | solution.py:477
  142.2 2.7 %collective-permute-start.4 = (f32[7,9,8,128]{3,2,1,0:T(8,128)S(1)}, f32[7,9,8,128]{3,2,1,0:T(8,128)S(1)}, u32[]{:S(2)}, u32[]{:S(2)}) collective-permute-start(f32[7,9,8,128]{3,2,1,0:T(8,128)S(1)} %get-tuple-element.66), channel_id=1, source_target_pairs={{0,4},{4,0},{8,12},{12,8},{16,20},{20,16},{24,28},{28,24},{1,5},{5... | collective-permute-start | bytes 774152 | tf_op jit(solution)/shard_map/ppermute | solution.py:391
  144.9 2.5 %collective-permute-start.5 = (f32[7,9,8,128]{3,2,1,0:T(8,128)S(1)}, f32[7,9,8,128]{3,2,1,0:T(8,128)S(1)}, u32[]{:S(2)}, u32[]{:S(2)}) collective-permute-start(f32[7,9,8,128]{3,2,1,0:T(8,128)S(1)} %get-tuple-element.67), channel_id=1, source_target_pairs={{0,28},{4,8},{8,4},{12,16},{16,12},{20,24},{24,20},{28,0},{1,29},{... | collective-permute-start | bytes 774152 | tf_op jit(solution)/shard_map/ppermute | solution.py:392
  152.2 5.7 %all-gather.2 = f32[60,8,128]{2,1,0:T(8,128)S(1)} all-gather(f32[15,8,128]{2,1,0:T(8,128)S(1)} %pad_maximum_fusion.1), channel_id=4, replica_groups=mesh['lon'=8,'lat'=4] {'lat'}, dimensions={0}, use_global_device_ids=true | all-gather | bytes 307200 | tf_op jit(solution)/shard_map/all_gather | solution.py:540
  158.0 5.8 %collective-permute-done.4.refs_1_ = f32[7,9,8,128]{3,2,1,0:T(8,128)S(1)} collective-permute-done((f32[7,9,8,128]{3,2,1,0:T(8,128)S(1)}, f32[7,9,8,128]{3,2,1,0:T(8,128)S(1)}, u32[]{:S(2)}, u32[]{:S(2)}) %collective-permute-start.4) | collective-permute-done | bytes 258080 | tf_op jit(solution)/shard_map/ppermute | solution.py:391
  170.1 5.4 %all-gather.3 = f32[28,8,128]{2,1,0:T(8,128)S(1)} all-gather(f32[7,8,128]{2,1,0:T(8,128)S(1)} %get-tuple-element.76), channel_id=5, replica_groups=mesh['lon'=8,'lat'=4] {'lat'}, dimensions={0}, use_global_device_ids=true | all-gather | bytes 143360 | tf_op jit(solution)/shard_map/all_gather | solution.py:551
  175.4 2.6 %last_step.4.refs_10_ = f32[25,36,8,128]{3,2,1,0:T(8,128)} custom-call(f32[8,36,8,128]{3,2,1,0:T(8,128)S(1)} %get-tuple-element.77.refs_0_, f32[8,9,8,128]{3,2,1,0:T(8,128)S(1)} %collective-permute-done.10.refs_1_, f32[8,9,8,128]{3,2,1,0:T(8,128)S(1)} %collective-permute-done.11.refs_2_, ...), custom_call_target="tpu_custom_call", output_to_operand_aliasing={{}: (10, {})} | custom-call | tf_op jit(solution)/shard_map/last_step/pallas_call | solution.py:506
  (49 shorter events, 31.3 us)
Async XLA Ops:
  6.6 7.3 %copy-start.5 = (f32[36,1024]{1,0:T(8,128)S(1)}, f32[36,1024]{1,0:T(8,128)}, u32[]{:S(2)}) copy-start(f32[36,1024]{1,0:T(8,128)} %get-tuple-element.44.gain_ref) | copy-start | bytes 442372
  6.6 7.3 %copy-start.11 = (s32[1,1024]{1,0:T(1,128)S(1)}, s32[1,1024]{1,0:T(1,128)}, u32[]{:S(2)}) copy-start(s32[1,1024]{1,0:T(1,128)} %get-tuple-element.45.target_ref) | copy-start | bytes 12292
  6.6 45.0 %all-to-all-start = ((f32[32,96,128]{2,1,0:T(8,128)}), f32[32,96,128]{2,1,0:T(8,128)S(1)}, u32[]{:S(2)}, u32[]{:S(2)}) async-start(f32[32,96,128]{2,1,0:T(8,128)} %get-tuple-element.43), calls=%async_computation | async-start | bytes 3145728 | tf_op jit(solution)/shard_map/all_to_all | solution.py:525
  13.9 2.2 %copy-start = (f32[25,36,1024]{2,1,0:T(8,128)S(1)}, f32[25,36,1024]{2,1,0:T(8,128)}, u32[]{:S(2)}) copy-start(f32[25,36,1024]{2,1,0:T(8,128)} %spectra_ref.3) | copy-start | bytes 11059204
  18.8 36.7 %copy-start.6 = (f32[2,512]{1,0:T(2,128)S(1)}, f32[2,512]{1,0:T(2,128)}, u32[]{:S(2)}) copy-start(f32[2,512]{1,0:T(2,128)} %refs_6_.11) | copy-start | bytes 12292
  18.8 36.7 %copy-start.10 = (f32[25]{0:T(128)S(1)}, f32[25]{0:T(128)}, u32[]{:S(2)}) copy-start(f32[25]{0:T(128)} %constant.19.clone.refs_1_.refs_4_) | copy-start | bytes 304
  51.6 41.2 %all-to-all-start.1 = ((f32[32,72,128]{2,1,0:T(8,128)}), f32[32,72,128]{2,1,0:T(8,128)S(1)}, u32[]{:S(2)}, u32[]{:S(2)}) async-start(f32[32,72,128]{2,1,0:T(8,128)} %copy-done.2), calls=%async_computation.1 | async-start | bytes 2359296 | tf_op jit(solution)/shard_map/all_to_all | solution.py:525
  59.3 25.8 %collective-permute-start = (f32[10,9,8,128]{3,2,1,0:T(8,128)S(1)}, f32[10,9,8,128]{3,2,1,0:T(8,128)S(1)}, u32[]{:S(2)}, u32[]{:S(2)}) collective-permute-start(f32[10,9,8,128]{3,2,1,0:T(8,128)S(1)} %get-tuple-element.49), channel_id=1, source_target_pairs={{0,4},{4,0},{8,12},{12,8},{16,20},{20,16},{24,28},{28,24},{1,5},{5... | collective-permute-start | bytes 1105928 | tf_op jit(solution)/shard_map/ppermute | solution.py:391
  61.1 26.9 %collective-permute-start.1 = (f32[10,9,8,128]{3,2,1,0:T(8,128)S(1)}, f32[10,9,8,128]{3,2,1,0:T(8,128)S(1)}, u32[]{:S(2)}, u32[]{:S(2)}) collective-permute-start(f32[10,9,8,128]{3,2,1,0:T(8,128)S(1)} %get-tuple-element.50), channel_id=1, source_target_pairs={{0,28},{4,8},{8,4},{12,16},{16,12},{20,24},{24,20},{28,0},{1,29},{... | collective-permute-start | bytes 1105928 | tf_op jit(solution)/shard_map/ppermute | solution.py:392
  66.6 21.4 %copy-start.7 = (f32[2,512]{1,0:T(2,128)S(1)}, f32[2,512]{1,0:T(2,128)}, u32[]{:S(2)}) copy-start(f32[2,512]{1,0:T(2,128)} %refs_7_.11) | copy-start | bytes 12292
  66.6 21.4 %copy-start.8 = (f32[2,512]{1,0:T(2,128)S(1)}, f32[2,512]{1,0:T(2,128)}, u32[]{:S(2)}) copy-start(f32[2,512]{1,0:T(2,128)} %refs_8_.11) | copy-start | bytes 12292
  66.6 21.4 %copy-start.9 = (s32[2,512]{1,0:T(2,128)S(1)}, s32[2,512]{1,0:T(2,128)}, u32[]{:S(2)}) copy-start(s32[2,512]{1,0:T(2,128)} %refs_9_.11) | copy-start | bytes 12292
  92.8 46.5 %all-to-all-start.2 = ((f32[32,64,128]{2,1,0:T(8,128)}), f32[32,64,128]{2,1,0:T(8,128)S(1)}, u32[]{:S(2)}, u32[]{:S(2)}) async-start(f32[32,64,128]{2,1,0:T(8,128)} %source_later.3), calls=%async_computation.2 | async-start | bytes 2097152 | tf_op jit(solution)/shard_map/all_to_all | solution.py:525
  100.1 34.3 %copy-start.4 = (f32[10,36,8,128]{3,2,1,0:T(8,128)S(1)}, f32[10,36,8,128]{3,2,1,0:T(8,128)}, u32[]{:S(2)}) copy-start(f32[10,36,8,128]{3,2,1,0:T(8,128)} %copy-done.3) | copy-start | bytes 4423684
  100.1 34.3 %collective-permute-start.2 = (f32[10,9,8,128]{3,2,1,0:T(8,128)}, f32[10,9,8,128]{3,2,1,0:T(8,128)S(1)}, u32[]{:S(2)}, u32[]{:S(2)}) collective-permute-start(f32[10,9,8,128]{3,2,1,0:T(8,128)} %get-tuple-element.58), channel_id=1, source_target_pairs={{0,4},{4,0},{8,12},{12,8},{16,20},{20,16},{24,28},{28,24},{1,5},{5... | collective-permute-start | bytes 1105928 | tf_op jit(solution)/shard_map/ppermute | solution.py:391
  101.9 32.5 %collective-permute-start.3 = (f32[10,9,8,128]{3,2,1,0:T(8,128)}, f32[10,9,8,128]{3,2,1,0:T(8,128)S(1)}, u32[]{:S(2)}, u32[]{:S(2)}) collective-permute-start(f32[10,9,8,128]{3,2,1,0:T(8,128)} %get-tuple-element.59), channel_id=1, source_target_pairs={{0,28},{4,8},{8,4},{12,16},{16,12},{20,24},{24,20},{28,0},{1,29},{... | collective-permute-start | bytes 1105928 | tf_op jit(solution)/shard_map/ppermute | solution.py:392
  109.0 38.4 %collective-permute-start.6 = (f32[8,9,8,128]{3,2,1,0:T(8,128)}, f32[8,9,8,128]{3,2,1,0:T(8,128)S(1)}, u32[]{:S(2)}, u32[]{:S(2)}) collective-permute-start(f32[8,9,8,128]{3,2,1,0:T(8,128)} %get-tuple-element.69), channel_id=1, source_target_pairs={{0,4},{4,0},{8,12},{12,8},{16,20},{20,16},{24,28},{28,24},{1,5},{5... | collective-permute-start | bytes 884744 | tf_op jit(solution)/shard_map/ppermute | solution.py:391
  109.0 38.4 %collective-permute-start.7 = (f32[8,9,8,128]{3,2,1,0:T(8,128)}, f32[8,9,8,128]{3,2,1,0:T(8,128)S(1)}, u32[]{:S(2)}, u32[]{:S(2)}) collective-permute-start(f32[8,9,8,128]{3,2,1,0:T(8,128)} %get-tuple-element.70), channel_id=1, source_target_pairs={{0,28},{4,8},{8,4},{12,16},{16,12},{20,24},{24,20},{28,0},{1,29},{... | collective-permute-start | bytes 884744 | tf_op jit(solution)/shard_map/ppermute | solution.py:392
  142.2 21.5 %collective-permute-start.4 = (f32[7,9,8,128]{3,2,1,0:T(8,128)S(1)}, f32[7,9,8,128]{3,2,1,0:T(8,128)S(1)}, u32[]{:S(2)}, u32[]{:S(2)}) collective-permute-start(f32[7,9,8,128]{3,2,1,0:T(8,128)S(1)} %get-tuple-element.66), channel_id=1, source_target_pairs={{0,4},{4,0},{8,12},{12,8},{16,20},{20,16},{24,28},{28,24},{1,5},{5... | collective-permute-start | bytes 774152 | tf_op jit(solution)/shard_map/ppermute | solution.py:391
  144.9 18.8 %collective-permute-start.5 = (f32[7,9,8,128]{3,2,1,0:T(8,128)S(1)}, f32[7,9,8,128]{3,2,1,0:T(8,128)S(1)}, u32[]{:S(2)}, u32[]{:S(2)}) collective-permute-start(f32[7,9,8,128]{3,2,1,0:T(8,128)S(1)} %get-tuple-element.67), channel_id=1, source_target_pairs={{0,28},{4,8},{8,4},{12,16},{16,12},{20,24},{24,20},{28,0},{1,29},{... | collective-permute-start | bytes 774152 | tf_op jit(solution)/shard_map/ppermute | solution.py:392
  149.8 25.6 %collective-permute-start.10 = (f32[8,9,8,128]{3,2,1,0:T(8,128)S(1)}, f32[8,9,8,128]{3,2,1,0:T(8,128)S(1)}, u32[]{:S(2)}, u32[]{:S(2)}) collective-permute-start(f32[8,9,8,128]{3,2,1,0:T(8,128)S(1)} %get-tuple-element.78), channel_id=1, source_target_pairs={{0,4},{4,0},{8,12},{12,8},{16,20},{20,16},{24,28},{28,24},{1,5},{5... | collective-permute-start | bytes 884744 | tf_op jit(solution)/shard_map/ppermute | solution.py:391
  149.9 25.5 %collective-permute-start.11 = (f32[8,9,8,128]{3,2,1,0:T(8,128)S(1)}, f32[8,9,8,128]{3,2,1,0:T(8,128)S(1)}, u32[]{:S(2)}, u32[]{:S(2)}) collective-permute-start(f32[8,9,8,128]{3,2,1,0:T(8,128)S(1)} %get-tuple-element.79), channel_id=1, source_target_pairs={{0,28},{4,8},{8,4},{12,16},{16,12},{20,24},{24,20},{28,0},{1,29},{... | collective-permute-start | bytes 884744 | tf_op jit(solution)/shard_map/ppermute | solution.py:392
  165.9 14.0 %collective-permute-start.8 = (f32[7,9,8,128]{3,2,1,0:T(8,128)S(1)}, f32[7,9,8,128]{3,2,1,0:T(8,128)S(1)}, u32[]{:S(2)}, u32[]{:S(2)}) collective-permute-start(f32[7,9,8,128]{3,2,1,0:T(8,128)S(1)} %get-tuple-element.74), channel_id=1, source_target_pairs={{0,4},{4,0},{8,12},{12,8},{16,20},{20,16},{24,28},{28,24},{1,5},{5... | collective-permute-start | bytes 774152 | tf_op jit(solution)/shard_map/ppermute | solution.py:391
  167.6 12.3 %collective-permute-start.9 = (f32[7,9,8,128]{3,2,1,0:T(8,128)S(1)}, f32[7,9,8,128]{3,2,1,0:T(8,128)S(1)}, u32[]{:S(2)}, u32[]{:S(2)}) collective-permute-start(f32[7,9,8,128]{3,2,1,0:T(8,128)S(1)} %get-tuple-element.75), channel_id=1, source_target_pairs={{0,28},{4,8},{8,4},{12,16},{16,12},{20,24},{24,20},{28,0},{1,29},{... | collective-permute-start | bytes 774152 | tf_op jit(solution)/shard_map/ppermute | solution.py:392
  (3 other events, 4.3 us)

commit v5 on v4

--- a/solution.py
+++ b/solution.py
@@ -449,7 +449,7 @@
                 out_specs=pl.BlockSpec(shape.shape, lambda i: (0, 0, 0)),
                 grid=(1,),
                 scratch_shapes=scratch,
-                compiler_params=params(),
+                compiler_params=pltpu.CompilerParams(vmem_limit_bytes=60 * 2**20),
                 name="source_later",
             )(spectra, gain, target)
         messages.append(message)

time: 183 us -> 183 us (level)
  Pallas kernels: 37.5 us -> 42 us
  local copies, waits for them, and re-layouts: 6.56 us -> 3.36 us
  waiting for transfers between devices: 72.4 us -> 70.2 us
    pallas_call x2, Pallas kernels: 4.23 us -> 8.05 us  [on_device(): pl.pallas_call(functools.partial(later_source_kernel, plan, first, count,...]
    unnamed x24 -> x22, local copies, waits for them, and re-layouts: 6.48 us -> 3.28 us
    ppermute x6, waiting for transfers between devices: 34.6 us -> 32.5 us  [send_edges(): lax.ppermute(pair, 'lon', [(i, i ^ 1) for i in range(lon)])]
  transfers between devices with their start and end apart: 15 -> 15, of which waited for: 7 -> 7; matrix products, arithmetic and copies ran while one was open for 0% -> 0% of each run, Pallas kernels for 16% -> 18%
where the time goes in v5:
time: 183 us; the launch traced here: 182 us
  waiting for transfers between devices  70.2 us (38%)
  starting transfers between devices  42.3 us (23%)
  Pallas kernels  42 us (23%)
  blocking collectives  24.3 us (13%)
  local copies, waits for them, and re-layouts  3.36 us (2%)
    all_to_all x3, waiting for transfers between devices, on_device(): lax.all_to_all(messages[i], ('lon', 'lat'), split_axis=0, concat_axis=0,...  35.6 us
    ppermute x6, waiting for transfers between devices, send_edges(): lax.ppermute(pair, 'lon', [(i, i ^ 1) for i in range(lon)])  32.5 us
    all_to_all x3, starting transfers between devices, on_device(): lax.all_to_all(messages[i], ('lon', 'lat'), split_axis=0, concat_axis=0,...  18.3 us
    ppermute x6, starting transfers between devices, send_edges(): lax.ppermute(cross, 'lon', [(i, (i + 2 * (i & 1) - 1) % lon) for i in ran...  15.9 us
    all_gather x2, blocking collectives, on_device(): lax.all_gather(jnp.concatenate([waiting[2], sent[2]], axis=0), 'lat')  12.8 us
    pallas_call x3, Pallas kernels, place(): pl.pallas_call(functools.partial(place_kernel, plan, first, count, ndir,...  11.1 us
    pallas_call x3, Pallas kernels, step(): pl.pallas_call(functools.partial(step_kernel, starts[i], side_first, Fals...  8.35 us
    ppermute x6, starting transfers between devices, send_edges(): lax.ppermute(pair, 'lon', [(i, i ^ 1) for i in range(lon)])  8.14 us
  transfers between devices with their start and end apart: 15, of which 7 were waited for; matrix products, arithmetic and copies ran while one was open for 0% of the time, Pallas kernels for 18%

profile of v5, /device:TPU:0, one launch (start us, length us, event | category | flops | bytes accessed | tf_op | source)
XLA Modules:
  0.0 182.5 jit_solution(2428565840070067198)
XLA Ops:
  0.0 6.6 %source_first.1 = (f32[32,96,128]{2,1,0:T(8,128)}, f32[36,1024]{1,0:T(8,128)}, s32[1,1024]{1,0:T(1,128)}) custom-call(f32[25,36,1024]{2,1,0:T(8,128)} %spectra_ref.3, f32[1,1024]{1,0:T(1,128)} %bitcast.30, f32[1,1024]{1,0:T(1,128)} %bitcast.31, s32[1,1024]{1,0:T(1,128)} %bitcast.32), custom_call_target="tpu_custom_call" | custom-call | tf_op jit(solution)/shard_map/source_first/pallas_call | solution.py:414
  6.6 7.3 %all-to-all-start = ((f32[32,96,128]{2,1,0:T(8,128)}), f32[32,96,128]{2,1,0:T(8,128)S(1)}, u32[]{:S(2)}, u32[]{:S(2)}) async-start(f32[32,96,128]{2,1,0:T(8,128)} %get-tuple-element.43), calls=%async_computation | async-start | bytes 3145728 | tf_op jit(solution)/shard_map/all_to_all | solution.py:525
  13.9 4.2 %source_later.2 = f32[32,72,128]{2,1,0:T(8,128)} custom-call(f32[25,36,1024]{2,1,0:T(8,128)} %spectra_ref.3, f32[36,1024]{1,0:T(8,128)} %get-tuple-element.44.gain_ref, s32[1,1024]{1,0:T(1,128)} %get-tuple-element.45.target_ref), custom_call_target="tpu_custom_call" | custom-call | tf_op jit(solution)/shard_map/source_later/pallas_call | solution.py:444
  18.0 33.6 %all-to-all-done.refs_0_ = f32[32,96,128]{2,1,0:T(8,128)S(1)} async-done(((f32[32,96,128]{2,1,0:T(8,128)}), f32[32,96,128]{2,1,0:T(8,128)S(1)}, u32[]{:S(2)}, u32[]{:S(2)}) %all-to-all-start) | async-done | bytes 1572896 | tf_op jit(solution)/shard_map/all_to_all | solution.py:525
  51.6 3.8 %all-to-all-start.1 = ((f32[32,72,128]{2,1,0:T(8,128)}), f32[32,72,128]{2,1,0:T(8,128)S(1)}, u32[]{:S(2)}, u32[]{:S(2)}) async-start(f32[32,72,128]{2,1,0:T(8,128)} %source_later.2), calls=%async_computation.1 | async-start | bytes 2359296 | tf_op jit(solution)/shard_map/all_to_all | solution.py:525
  55.5 4.5 %place.3 = (f32[2880,128]{1,0:T(8,128)S(1)}, f32[10,9,8,128]{3,2,1,0:T(8,128)}, f32[10,9,8,128]{3,2,1,0:T(8,128)}, f32[10,8,128]{2,1,0:T(8,128)S(1)}, s32[1,1024]{1,0:T(1,128)S(1)}) custom-call(f32[32,96,128]{2,1,0:T(8,128)S(1)} %all-to-all-done.refs_0_, f32[25]{0:T(128)S(1)} %copy-done.10, s32[5]{0:T(128)S(1)} %stack.31.refs_2_.refs_5_, f32[2,512]{1,0:T(2,128)S(1)} %copy-done.6), custom_call_target="tpu_custom_call" | custom-call | tf_op jit(solution)/shard_map/place/pallas_call | solution.py:477
  62.9 3.4 %collective-permute-start.1 = (f32[10,9,8,128]{3,2,1,0:T(8,128)}, f32[10,9,8,128]{3,2,1,0:T(8,128)S(1)}, u32[]{:S(2)}, u32[]{:S(2)}) collective-permute-start(f32[10,9,8,128]{3,2,1,0:T(8,128)} %get-tuple-element.50), channel_id=1, source_target_pairs={{0,28},{4,8},{8,4},{12,16},{16,12},{20,24},{24,20},{28,0},{1,29},{... | collective-permute-start | bytes 1105928 | tf_op jit(solution)/shard_map/ppermute | solution.py:392
  66.3 3.9 %source_later.3 = f32[32,64,128]{2,1,0:T(8,128)} custom-call(f32[25,36,1024]{2,1,0:T(8,128)} %spectra_ref.3, f32[36,1024]{1,0:T(8,128)} %get-tuple-element.44.gain_ref, s32[1,1024]{1,0:T(1,128)} %get-tuple-element.45.target_ref), custom_call_target="tpu_custom_call" | custom-call | tf_op jit(solution)/shard_map/source_later/pallas_call | solution.py:444
  70.2 6.1 %all-gather = f32[40,8,128]{2,1,0:T(8,128)S(1)} all-gather(f32[10,8,128]{2,1,0:T(8,128)S(1)} %get-tuple-element.51), channel_id=2, replica_groups=mesh['lon'=8,'lat'=4] {'lat'}, dimensions={0}, use_global_device_ids=true | all-gather | bytes 204800 | tf_op jit(solution)/shard_map/all_gather | solution.py:537
  76.3 9.5 %collective-permute-done.refs_1_ = f32[10,9,8,128]{3,2,1,0:T(8,128)S(1)} collective-permute-done((f32[10,9,8,128]{3,2,1,0:T(8,128)}, f32[10,9,8,128]{3,2,1,0:T(8,128)S(1)}, u32[]{:S(2)}, u32[]{:S(2)}) %collective-permute-start) | collective-permute-done | bytes 368672 | tf_op jit(solution)/shard_map/ppermute | solution.py:391
  88.0 3.7 %step.3 = (f32[10,36,8,128]{3,2,1,0:T(8,128)S(1)}, f32[10,9,8,128]{3,2,1,0:T(8,128)}, f32[10,9,8,128]{3,2,1,0:T(8,128)}, f32[10,8,128]{2,1,0:T(8,128)S(1)}) custom-call(f32[10,36,8,128]{3,2,1,0:T(8,128)S(1)} %bitcast.24, f32[10,9,8,128]{3,2,1,0:T(8,128)S(1)} %collective-permute-done.refs_1_, f32[10,9,8,128]{3,2,1,0:T(8,128)S(1)} %collective-permute-done.1.refs_2_, ...), custom_call_target="tpu_custom_call" | custom-call | tf_op jit(solution)/shard_map/step/pallas_call | solution.py:493
  92.8 7.2 %all-to-all-start.2 = ((f32[32,64,128]{2,1,0:T(8,128)}), f32[32,64,128]{2,1,0:T(8,128)S(1)}, u32[]{:S(2)}, u32[]{:S(2)}) async-start(f32[32,64,128]{2,1,0:T(8,128)} %source_later.3), calls=%async_computation.2 | async-start | bytes 2097152 | tf_op jit(solution)/shard_map/all_to_all | solution.py:525
  101.9 3.3 %collective-permute-start.3 = (f32[10,9,8,128]{3,2,1,0:T(8,128)}, f32[10,9,8,128]{3,2,1,0:T(8,128)S(1)}, u32[]{:S(2)}, u32[]{:S(2)}) collective-permute-start(f32[10,9,8,128]{3,2,1,0:T(8,128)} %get-tuple-element.59), channel_id=1, source_target_pairs={{0,28},{4,8},{8,4},{12,16},{16,12},{20,24},{24,20},{28,0},{1,29},{... | collective-permute-start | bytes 1105928 | tf_op jit(solution)/shard_map/ppermute | solution.py:392
  105.2 3.7 %place.4 = (f32[2304,128]{1,0:T(8,128)S(1)}, f32[8,9,8,128]{3,2,1,0:T(8,128)}, f32[8,9,8,128]{3,2,1,0:T(8,128)S(1)}, f32[8,8,128]{2,1,0:T(8,128)S(1)}) custom-call(f32[32,72,128]{2,1,0:T(8,128)S(1)} %all-to-all-done.1.refs_0_, f32[25]{0:T(128)S(1)} %copy-done.10, s32[5]{0:T(128)S(1)} %stack.31.refs_2_.refs_5_, f32[2,512]{1,0:T(2,128)S(1)} %copy-done.6, ...), custom_call_target="tpu_custom_call" | custom-call | tf_op jit(solution)/shard_map/place/pallas_call | solution.py:477
  112.0 7.1 %all-gather.1 = f32[72,8,128]{2,1,0:T(8,128)S(1)} all-gather(f32[18,8,128]{2,1,0:T(8,128)S(1)} %pad_maximum_fusion), channel_id=3, replica_groups=mesh['lon'=8,'lat'=4] {'lat'}, dimensions={0}, use_global_device_ids=true | all-gather | bytes 368640 | tf_op jit(solution)/shard_map/all_gather | solution.py:540
  119.1 15.3 %collective-permute-done.2.refs_1_ = f32[10,9,8,128]{3,2,1,0:T(8,128)S(1)} collective-permute-done((f32[10,9,8,128]{3,2,1,0:T(8,128)}, f32[10,9,8,128]{3,2,1,0:T(8,128)S(1)}, u32[]{:S(2)}, u32[]{:S(2)}) %collective-permute-start.2) | collective-permute-done | bytes 368672 | tf_op jit(solution)/shard_map/ppermute | solution.py:391
  134.4 2.9 %last_step.3.refs_10_ = f32[25,36,8,128]{3,2,1,0:T(8,128)} custom-call(f32[10,36,8,128]{3,2,1,0:T(8,128)S(1)} %copy-done.1, f32[10,9,8,128]{3,2,1,0:T(8,128)S(1)} %collective-permute-done.2.refs_1_, f32[10,9,8,128]{3,2,1,0:T(8,128)S(1)} %collective-permute-done.3.refs_2_, f32[4,18,8,128]{3,2,1,0:T(8,128)S(1)} %bitcast.20, f32[25]{0:T(128)S(1)} %copy-done.10, ...), custom_call_target="tpu_custom_call" | custom-call | tf_op jit(solution)/shard_map/last_step/pallas_call | solution.py:506
  139.3 2.9 %place.5 = (f32[2016,128]{1,0:T(8,128)S(1)}, f32[7,9,8,128]{3,2,1,0:T(8,128)S(1)}, f32[7,9,8,128]{3,2,1,0:T(8,128)S(1)}, f32[7,8,128]{2,1,0:T(8,128)S(1)}) custom-call(f32[32,64,128]{2,1,0:T(8,128)S(1)} %all-to-all-done.2.refs_0_, f32[25]{0:T(128)S(1)} %copy-done.10, s32[5]{0:T(128)S(1)} %stack.31.refs_2_.refs_5_, f32[2,512]{1,0:T(2,128)S(1)} %copy-done.6, ...), custom_call_target="tpu_custom_call" | custom-call | tf_op jit(solution)/shard_map/place/pallas_call | solution.py:477
  142.2 2.7 %collective-permute-start.4 = (f32[7,9,8,128]{3,2,1,0:T(8,128)S(1)}, f32[7,9,8,128]{3,2,1,0:T(8,128)S(1)}, u32[]{:S(2)}, u32[]{:S(2)}) collective-permute-start(f32[7,9,8,128]{3,2,1,0:T(8,128)S(1)} %get-tuple-element.66), channel_id=1, source_target_pairs={{0,4},{4,0},{8,12},{12,8},{16,20},{20,16},{24,28},{28,24},{1,5},{5... | collective-permute-start | bytes 774152 | tf_op jit(solution)/shard_map/ppermute | solution.py:391
  144.9 2.5 %collective-permute-start.5 = (f32[7,9,8,128]{3,2,1,0:T(8,128)S(1)}, f32[7,9,8,128]{3,2,1,0:T(8,128)S(1)}, u32[]{:S(2)}, u32[]{:S(2)}) collective-permute-start(f32[7,9,8,128]{3,2,1,0:T(8,128)S(1)} %get-tuple-element.67), channel_id=1, source_target_pairs={{0,28},{4,8},{8,4},{12,16},{16,12},{20,24},{24,20},{28,0},{1,29},{... | collective-permute-start | bytes 774152 | tf_op jit(solution)/shard_map/ppermute | solution.py:392
  152.2 5.7 %all-gather.2 = f32[60,8,128]{2,1,0:T(8,128)S(1)} all-gather(f32[15,8,128]{2,1,0:T(8,128)S(1)} %pad_maximum_fusion.1), channel_id=4, replica_groups=mesh['lon'=8,'lat'=4] {'lat'}, dimensions={0}, use_global_device_ids=true | all-gather | bytes 307200 | tf_op jit(solution)/shard_map/all_gather | solution.py:540
  158.0 5.8 %collective-permute-done.4.refs_1_ = f32[7,9,8,128]{3,2,1,0:T(8,128)S(1)} collective-permute-done((f32[7,9,8,128]{3,2,1,0:T(8,128)S(1)}, f32[7,9,8,128]{3,2,1,0:T(8,128)S(1)}, u32[]{:S(2)}, u32[]{:S(2)}) %collective-permute-start.4) | collective-permute-done | bytes 258080 | tf_op jit(solution)/shard_map/ppermute | solution.py:391
  170.0 5.4 %all-gather.3 = f32[28,8,128]{2,1,0:T(8,128)S(1)} all-gather(f32[7,8,128]{2,1,0:T(8,128)S(1)} %get-tuple-element.76), channel_id=5, replica_groups=mesh['lon'=8,'lat'=4] {'lat'}, dimensions={0}, use_global_device_ids=true | all-gather | bytes 143360 | tf_op jit(solution)/shard_map/all_gather | solution.py:551
  175.4 2.6 %last_step.4.refs_10_ = f32[25,36,8,128]{3,2,1,0:T(8,128)} custom-call(f32[8,36,8,128]{3,2,1,0:T(8,128)S(1)} %get-tuple-element.77.refs_0_, f32[8,9,8,128]{3,2,1,0:T(8,128)S(1)} %collective-permute-done.10.refs_1_, f32[8,9,8,128]{3,2,1,0:T(8,128)S(1)} %collective-permute-done.11.refs_2_, ...), custom_call_target="tpu_custom_call", output_to_operand_aliasing={{}: (10, {})} | custom-call | tf_op jit(solution)/shard_map/last_step/pallas_call | solution.py:506
  (47 shorter events, 28.5 us)
Async XLA Ops:
  6.6 45.0 %all-to-all-start = ((f32[32,96,128]{2,1,0:T(8,128)}), f32[32,96,128]{2,1,0:T(8,128)S(1)}, u32[]{:S(2)}, u32[]{:S(2)}) async-start(f32[32,96,128]{2,1,0:T(8,128)} %get-tuple-element.43), calls=%async_computation | async-start | bytes 3145728 | tf_op jit(solution)/shard_map/all_to_all | solution.py:525
  18.0 37.5 %copy-start.6 = (f32[2,512]{1,0:T(2,128)S(1)}, f32[2,512]{1,0:T(2,128)}, u32[]{:S(2)}) copy-start(f32[2,512]{1,0:T(2,128)} %refs_6_.11) | copy-start | bytes 12292
  18.0 37.5 %copy-start.10 = (f32[25]{0:T(128)S(1)}, f32[25]{0:T(128)}, u32[]{:S(2)}) copy-start(f32[25]{0:T(128)} %constant.19.clone.refs_1_.refs_4_) | copy-start | bytes 304
  51.6 41.2 %all-to-all-start.1 = ((f32[32,72,128]{2,1,0:T(8,128)}), f32[32,72,128]{2,1,0:T(8,128)S(1)}, u32[]{:S(2)}, u32[]{:S(2)}) async-start(f32[32,72,128]{2,1,0:T(8,128)} %source_later.2), calls=%async_computation.1 | async-start | bytes 2359296 | tf_op jit(solution)/shard_map/all_to_all | solution.py:525
  60.0 1.1 copy-start.2
  61.1 24.7 %collective-permute-start = (f32[10,9,8,128]{3,2,1,0:T(8,128)}, f32[10,9,8,128]{3,2,1,0:T(8,128)S(1)}, u32[]{:S(2)}, u32[]{:S(2)}) collective-permute-start(f32[10,9,8,128]{3,2,1,0:T(8,128)} %get-tuple-element.49), channel_id=1, source_target_pairs={{0,4},{4,0},{8,12},{12,8},{16,20},{20,16},{24,28},{28,24},{1,5},{5... | collective-permute-start | bytes 1105928 | tf_op jit(solution)/shard_map/ppermute | solution.py:391
  62.9 25.1 %copy-start.3 = (f32[2880,128]{1,0:T(8,128)S(1)}, f32[2880,128]{1,0:T(8,128)}, u32[]{:S(2)}) copy-start(f32[2880,128]{1,0:T(8,128)} %copy-done.2) | copy-start | bytes 4423684
  62.9 25.1 %copy-start.7 = (f32[2,512]{1,0:T(2,128)S(1)}, f32[2,512]{1,0:T(2,128)}, u32[]{:S(2)}) copy-start(f32[2,512]{1,0:T(2,128)} %refs_7_.11) | copy-start | bytes 12292
  62.9 25.1 %copy-start.8 = (f32[2,512]{1,0:T(2,128)S(1)}, f32[2,512]{1,0:T(2,128)}, u32[]{:S(2)}) copy-start(f32[2,512]{1,0:T(2,128)} %refs_8_.11) | copy-start | bytes 12292
  62.9 25.1 %copy-start.9 = (s32[2,512]{1,0:T(2,128)S(1)}, s32[2,512]{1,0:T(2,128)}, u32[]{:S(2)}) copy-start(s32[2,512]{1,0:T(2,128)} %refs_9_.11) | copy-start | bytes 12292
  62.9 25.1 %collective-permute-start.1 = (f32[10,9,8,128]{3,2,1,0:T(8,128)}, f32[10,9,8,128]{3,2,1,0:T(8,128)S(1)}, u32[]{:S(2)}, u32[]{:S(2)}) collective-permute-start(f32[10,9,8,128]{3,2,1,0:T(8,128)} %get-tuple-element.50), channel_id=1, source_target_pairs={{0,28},{4,8},{8,4},{12,16},{16,12},{20,24},{24,20},{28,0},{1,29},{... | collective-permute-start | bytes 1105928 | tf_op jit(solution)/shard_map/ppermute | solution.py:392
  92.8 46.5 %all-to-all-start.2 = ((f32[32,64,128]{2,1,0:T(8,128)}), f32[32,64,128]{2,1,0:T(8,128)S(1)}, u32[]{:S(2)}, u32[]{:S(2)}) async-start(f32[32,64,128]{2,1,0:T(8,128)} %source_later.3), calls=%async_computation.2 | async-start | bytes 2097152 | tf_op jit(solution)/shard_map/all_to_all | solution.py:525
  100.1 34.3 %copy-start.1 = (f32[10,36,8,128]{3,2,1,0:T(8,128)S(1)}, f32[10,36,8,128]{3,2,1,0:T(8,128)}, u32[]{:S(2)}) copy-start(f32[10,36,8,128]{3,2,1,0:T(8,128)} %copy-done) | copy-start | bytes 4423684
  100.1 34.3 %collective-permute-start.2 = (f32[10,9,8,128]{3,2,1,0:T(8,128)}, f32[10,9,8,128]{3,2,1,0:T(8,128)S(1)}, u32[]{:S(2)}, u32[]{:S(2)}) collective-permute-start(f32[10,9,8,128]{3,2,1,0:T(8,128)} %get-tuple-element.58), channel_id=1, source_target_pairs={{0,4},{4,0},{8,12},{12,8},{16,20},{20,16},{24,28},{28,24},{1,5},{5... | collective-permute-start | bytes 1105928 | tf_op jit(solution)/shard_map/ppermute | solution.py:391
  101.9 32.5 %collective-permute-start.3 = (f32[10,9,8,128]{3,2,1,0:T(8,128)}, f32[10,9,8,128]{3,2,1,0:T(8,128)S(1)}, u32[]{:S(2)}, u32[]{:S(2)}) collective-permute-start(f32[10,9,8,128]{3,2,1,0:T(8,128)} %get-tuple-element.59), channel_id=1, source_target_pairs={{0,28},{4,8},{8,4},{12,16},{16,12},{20,24},{24,20},{28,0},{1,29},{... | collective-permute-start | bytes 1105928 | tf_op jit(solution)/shard_map/ppermute | solution.py:392
  110.0 37.4 %collective-permute-start.6 = (f32[8,9,8,128]{3,2,1,0:T(8,128)}, f32[8,9,8,128]{3,2,1,0:T(8,128)S(1)}, u32[]{:S(2)}, u32[]{:S(2)}) collective-permute-start(f32[8,9,8,128]{3,2,1,0:T(8,128)} %get-tuple-element.69), channel_id=1, source_target_pairs={{0,4},{4,0},{8,12},{12,8},{16,20},{20,16},{24,28},{28,24},{1,5},{5... | collective-permute-start | bytes 884744 | tf_op jit(solution)/shard_map/ppermute | solution.py:391
  110.0 37.4 %collective-permute-start.7 = (f32[8,9,8,128]{3,2,1,0:T(8,128)S(1)}, f32[8,9,8,128]{3,2,1,0:T(8,128)S(1)}, u32[]{:S(2)}, u32[]{:S(2)}) collective-permute-start(f32[8,9,8,128]{3,2,1,0:T(8,128)S(1)} %get-tuple-element.70), channel_id=1, source_target_pairs={{0,28},{4,8},{8,4},{12,16},{16,12},{20,24},{24,20},{28,0},{1,29},{... | collective-permute-start | bytes 884744 | tf_op jit(solution)/shard_map/ppermute | solution.py:392
  134.4 13.0 %copy-start.5 = (f32[2304,128]{1,0:T(8,128)S(1)}, f32[2304,128]{1,0:T(8,128)}, u32[]{:S(2)}) copy-start(f32[2304,128]{1,0:T(8,128)} %copy-done.4) | copy-start | bytes 3538948
  142.2 21.5 %collective-permute-start.4 = (f32[7,9,8,128]{3,2,1,0:T(8,128)S(1)}, f32[7,9,8,128]{3,2,1,0:T(8,128)S(1)}, u32[]{:S(2)}, u32[]{:S(2)}) collective-permute-start(f32[7,9,8,128]{3,2,1,0:T(8,128)S(1)} %get-tuple-element.66), channel_id=1, source_target_pairs={{0,4},{4,0},{8,12},{12,8},{16,20},{20,16},{24,28},{28,24},{1,5},{5... | collective-permute-start | bytes 774152 | tf_op jit(solution)/shard_map/ppermute | solution.py:391
  144.9 18.8 %collective-permute-start.5 = (f32[7,9,8,128]{3,2,1,0:T(8,128)S(1)}, f32[7,9,8,128]{3,2,1,0:T(8,128)S(1)}, u32[]{:S(2)}, u32[]{:S(2)}) collective-permute-start(f32[7,9,8,128]{3,2,1,0:T(8,128)S(1)} %get-tuple-element.67), channel_id=1, source_target_pairs={{0,28},{4,8},{8,4},{12,16},{16,12},{20,24},{24,20},{28,0},{1,29},{... | collective-permute-start | bytes 774152 | tf_op jit(solution)/shard_map/ppermute | solution.py:392
  149.8 25.6 %collective-permute-start.10 = (f32[8,9,8,128]{3,2,1,0:T(8,128)S(1)}, f32[8,9,8,128]{3,2,1,0:T(8,128)S(1)}, u32[]{:S(2)}, u32[]{:S(2)}) collective-permute-start(f32[8,9,8,128]{3,2,1,0:T(8,128)S(1)} %get-tuple-element.78), channel_id=1, source_target_pairs={{0,4},{4,0},{8,12},{12,8},{16,20},{20,16},{24,28},{28,24},{1,5},{5... | collective-permute-start | bytes 884744 | tf_op jit(solution)/shard_map/ppermute | solution.py:391
  149.9 25.5 %collective-permute-start.11 = (f32[8,9,8,128]{3,2,1,0:T(8,128)S(1)}, f32[8,9,8,128]{3,2,1,0:T(8,128)S(1)}, u32[]{:S(2)}, u32[]{:S(2)}) collective-permute-start(f32[8,9,8,128]{3,2,1,0:T(8,128)S(1)} %get-tuple-element.79), channel_id=1, source_target_pairs={{0,28},{4,8},{8,4},{12,16},{16,12},{20,24},{24,20},{28,0},{1,29},{... | collective-permute-start | bytes 884744 | tf_op jit(solution)/shard_map/ppermute | solution.py:392
  165.9 14.0 %collective-permute-start.8 = (f32[7,9,8,128]{3,2,1,0:T(8,128)S(1)}, f32[7,9,8,128]{3,2,1,0:T(8,128)S(1)}, u32[]{:S(2)}, u32[]{:S(2)}) collective-permute-start(f32[7,9,8,128]{3,2,1,0:T(8,128)S(1)} %get-tuple-element.74), channel_id=1, source_target_pairs={{0,4},{4,0},{8,12},{12,8},{16,20},{20,16},{24,28},{28,24},{1,5},{5... | collective-permute-start | bytes 774152 | tf_op jit(solution)/shard_map/ppermute | solution.py:391
  167.7 12.2 %collective-permute-start.9 = (f32[7,9,8,128]{3,2,1,0:T(8,128)S(1)}, f32[7,9,8,128]{3,2,1,0:T(8,128)S(1)}, u32[]{:S(2)}, u32[]{:S(2)}) collective-permute-start(f32[7,9,8,128]{3,2,1,0:T(8,128)S(1)} %get-tuple-element.75), channel_id=1, source_target_pairs={{0,28},{4,8},{8,4},{12,16},{16,12},{20,24},{24,20},{28,0},{1,29},{... | collective-permute-start | bytes 774152 | tf_op jit(solution)/shard_map/ppermute | solution.py:392
  (2 other events, 2.1 us)
